TPU v7x, 256 devices: a whole 4x4x8 slice. The times are simulated.
256 devices in a mesh: freq: 4 (over x_hi, core), strip: 64 (over x_lo, z, y).
Axes of the slice: x: 4 (x_hi: 2, x_lo: 2; x = x_hi * 2 + x_lo), y: 4, z: 8, core: 2. Of those that a mesh axis runs over, the one named last changes fastest.
Arguments:
- source: float32 [2, 4, 512, 8192], P(None, 'freq', None, 'strip'), may hold values from -6 to 6
- receiver: float32 [2, 4, 512, 8192], P(None, 'freq', None, 'strip'), may hold values from -6 to 6
- velocity: float32 [2, 512, 8192], P(None, 'strip'), may hold values from 1.5 to 4.5
- omega: float32 [4], P('freq'), may hold values from 1 to 3
Outputs:
- image: float32 [2, 512, 8192], P(None, 'freq', 'strip')
All inputs are finite; a program needn't handle non-finite values.
Results may differ from a plain program's by a relative error of at most 0.00002.
Values sent between devices are 32-bit elements; how exact they have to be, the bound alone decides.
No kernel may reach another device: no remote copies, remote signals or barrier semaphores. Data moves between devices by JAX's collectives and lax.ppermute only.
A program may use at most 64 MiB of HBM per device.

v0:
```python
import jax
import jax.numpy as jnp
from jax import lax
from jax.sharding import PartitionSpec as P

SUBS = 2


phase_depth = 2.0
fd_coef = 0.03


def with_halo(block, sides, width):
    for axis, dim in sides:
        count = lax.axis_size(axis)
        forward = [(i, i + 1) for i in range(count - 1)]
        backward = [(target, source) for source, target in forward]
        low = lax.ppermute(
            lax.slice_in_dim(block, block.shape[dim] - width, None, axis=dim), axis, forward
        )
        high = lax.ppermute(lax.slice_in_dim(block, 0, width, axis=dim), axis, backward)
        block = jnp.concatenate([low, block, high], axis=dim)
    return block


def laplace_rimmed(padded):
    center = padded[..., 1:-1]
    across = padded[..., 2:] + padded[..., :-2]
    xpad = jnp.pad(center, ((0, 0), (0, 0), (1, 1), (0, 0)))
    along = xpad[:, :, 2:] + xpad[:, :, :-2]
    return across + along - 4.0 * center


def turn_lap(lap):
    return jnp.stack([-lap[1], lap[0], lap[3], -lap[2]])


def slice_speed(velocity, depth):
    layer = velocity[depth]
    return lax.all_to_all(layer, "strip", split_axis=1, concat_axis=0, tiled=True)


def shards(source, receiver, velocity, omega):
    waves = jnp.concatenate([source, receiver], 0)
    freq = omega[:, None, None]
    layers = []
    for depth in range(velocity.shape[0]):
        speed = slice_speed(velocity, depth)[None]
        theta = freq * phase_depth / speed
        cosine = jnp.cos(theta)
        sine = jnp.sin(theta)
        src_re, src_im, rec_re, rec_im = (waves[0], waves[1], waves[2], waves[3])
        waves = jnp.stack(
            [
                src_re * cosine - src_im * sine,
                src_re * sine + src_im * cosine,
                rec_re * cosine + rec_im * sine,
                rec_im * cosine - rec_re * sine,
            ]
        )
        coef = fd_coef * speed / freq
        for sub in range(SUBS):
            padded = with_halo(waves, (("strip", 3),), 1)
            lap = laplace_rimmed(padded)
            waves = waves + coef[None] * turn_lap(lap)
        product = jnp.sum(waves[0] * waves[2] + waves[1] * waves[3], axis=0)
        layers.append(lax.psum_scatter(product, "freq", scatter_dimension=0, tiled=True))
    return jnp.stack(layers)


def solution(mesh):
    return jax.shard_map(
        shards,
        mesh=mesh,
        in_specs=(
            P(None, "freq", None, "strip"),
            P(None, "freq", None, "strip"),
            P(None, "strip", None),
            P("freq"),
        ),
        out_specs=P(None, "freq", "strip"),
        check_vma=False,
    )
```

profile of v0, /device:TPU:1, one launch (start us, length us, event | category | flops | bytes accessed | tf_op | source)
XLA Modules:
  0.0 190.5 jit_solution(3066003575423778573)
XLA Ops:
  6.5 1.9 %slice_bitcast_fusion = (f32[8,64,128]{2,0,1:T(8,128)}, f32[8,64,128]{2,0,1:T(8,128)}) fusion(f32[2,8,8192]{2,1,0:T(8,128)} %param.6), kind=kLoop, calls=%fused_computation.79 | loop fusion | bytes 1048576 | tf_op jit(solution)/shard_map/all_to_all | solution.py:40
  8.5 13.6 %all-to-all-start = ((f32[8,64,128]{2,0,1:T(8,128)}), f32[8,64,128]{2,0,1:T(8,128)S(1)}, u32[]{:S(2)}, u32[]{:S(2)}) async-start(f32[8,64,128]{2,0,1:T(8,128)} %get-tuple-element.39), calls=%async_computation | async-start | bytes 524288 | tf_op jit(solution)/shard_map/all_to_all | solution.py:40
  22.7 10.1 %all-to-all-done = f32[8,64,128]{2,0,1:T(8,128)S(1)} async-done(((f32[8,64,128]{2,0,1:T(8,128)}), f32[8,64,128]{2,0,1:T(8,128)S(1)}, u32[]{:S(2)}, u32[]{:S(2)}) %all-to-all-start) | async-done | bytes 262176 | tf_op jit(solution)/shard_map/all_to_all | solution.py:40
  32.9 1.1 fusion.22
  34.0 1.3 fusion.33
  35.4 1.5 copy.22
  36.9 1.3 collective-permute-start
  38.2 0.3 copy.24
  38.5 4.0 %collective-permute-start.1 = (f32[4,1,512,1]{2,0,3,1:T(4,128)S(1)}, f32[4,1,512,1]{2,0,3,1:T(4,128)S(1)}, u32[]{:S(2)}, u32[]{:S(2)}) collective-permute-start(f32[4,1,512,1]{2,0,3,1:T(4,128)S(1)} %copy.24), channel_id=1, source_target_pairs={{0,1},{1,2},{2,3},{3,4},{4,5},{5,6},{6,7},{7,8},{8,9},{9,10},{10,1... | collective-permute-start | bytes 24584 | tf_op jit(solution)/shard_map/ppermute | solution.py:18
  42.5 0.7 divide_bitcast_fusion.1
  43.3 0.4 copy.23
  43.7 1.4 copy.25
  45.0 2.1 %fusion.11 = f32[4,1,512,128]{3,2,1,0:T(8,128)S(1)} fusion(f32[4,1,512,1]{3,2,1,0:T(8,128)} %copy.25, f32[1,1,512,128]{3,2,1,0:T(8,128)S(1)} %get-tuple-element.40, f32[1,1,512,128]{3,2,1,0:T(8,128)S(1)} %get-tuple-element.41, f32[1,1,512,128]{3,2,1,0:T(8,128)S(1)} %get-tuple-element.35, f32[1,1,512,128]{3,2,1,0:T(8,128)S(1)} %get-tuple-element.34, ...), kind=kLoop, calls=%fused_computation.24 | loop fusion | flops 3407872 | bytes 3162112 | tf_op jit(solution)/shard_map/sub | solution.py:31
  47.3 0.7 copy-done.9
  47.9 0.1 copy-done.11
  48.1 0.1 copy-done.13
  48.2 0.1 fusion.12
  48.3 1.3 fusion.32
  49.7 1.5 copy.26
  51.2 1.3 collective-permute-start.2
  52.5 0.3 copy.28
  52.8 4.0 %collective-permute-start.3 = (f32[4,1,512,1]{2,0,3,1:T(4,128)S(1)}, f32[4,1,512,1]{2,0,3,1:T(4,128)S(1)}, u32[]{:S(2)}, u32[]{:S(2)}) collective-permute-start(f32[4,1,512,1]{2,0,3,1:T(4,128)S(1)} %copy.28), channel_id=1, source_target_pairs={{0,1},{1,2},{2,3},{3,4},{4,5},{5,6},{6,7},{7,8},{8,9},{9,10},{10,1... | collective-permute-start | bytes 24584 | tf_op jit(solution)/shard_map/ppermute | solution.py:18
  56.8 13.6 %all-to-all-start.1 = ((f32[8,64,128]{2,0,1:T(8,128)}), f32[8,64,128]{2,0,1:T(8,128)}, u32[]{:S(2)}, u32[]{:S(2)}) async-start(f32[8,64,128]{2,0,1:T(8,128)} %get-tuple-element.38), calls=%async_computation.2 | async-start | bytes 524288 | tf_op jit(solution)/shard_map/all_to_all | solution.py:40
  70.5 0.4 copy.27
  70.9 1.4 copy.29
  72.3 2.1 %fusion.8 = f32[4,1,512,128]{3,2,1,0:T(8,128)S(1)} fusion(f32[4,1,512,128]{3,2,1,0:T(8,128)S(1)} %fusion.12, f32[4,1,512,1]{3,2,1,0:T(8,128)} %copy.29, f32[4,1,512,1]{3,2,1,0:T(8,128)S(1)} %copy.27), kind=kLoop, calls=%fused_computation.19 | loop fusion | flops 1835008 | bytes 2113536 | tf_op jit(solution)/shard_map/sub | solution.py:31
  74.5 0.8 copy-done.10
  75.4 0.1 copy-done.12
  75.4 0.1 copy-done.14
  75.5 0.1 copy-done.16
  75.6 0.2 fusion.13
  75.8 5.3 %all-to-all-done.1 = f32[8,64,128]{2,0,1:T(8,128)} async-done(((f32[8,64,128]{2,0,1:T(8,128)}), f32[8,64,128]{2,0,1:T(8,128)}, u32[]{:S(2)}, u32[]{:S(2)}) %all-to-all-start.1) | async-done | bytes 262176 | tf_op jit(solution)/shard_map/all_to_all | solution.py:40
  81.0 2.6 %fusion.18 = (f32[1,1,512,128]{3,2,1,0:T(8,128)S(1)}, f32[1,1,512,128]{3,2,1,0:T(8,128)S(1)}, f32[1,1,512,128]{3,2,1,0:T(8,128)S(1)}, f32[1,1,512,128]{3,2,1,0:T(8,128)S(1)}, f32[512,128]{1,0:T(8,128)}) fusion(f32[4,1,512,128]{3,2,1,0:T(8,128)S(1)} %fusion.13, f32[8,64,128]{2,0,1:T(8,128)} %all-to-all-done.1, f32[]{:T(128)} %bitcast), kind=kLoop, calls=%fused_computation.58 | loop fusion | flops 1048576 | bytes 2621444 | tf_op jit(solution)/shard_map/sub | solution.py:55
  83.7 1.3 fusion.31
  85.0 1.5 copy.30
  86.6 1.3 collective-permute-start.4
  87.9 0.3 copy.32
  88.2 4.0 %collective-permute-start.5 = (f32[4,1,512,1]{2,0,3,1:T(4,128)S(1)}, f32[4,1,512,1]{2,0,3,1:T(4,128)S(1)}, u32[]{:S(2)}, u32[]{:S(2)}) collective-permute-start(f32[4,1,512,1]{2,0,3,1:T(4,128)S(1)} %copy.32), channel_id=1, source_target_pairs={{0,1},{1,2},{2,3},{3,4},{4,5},{5,6},{6,7},{7,8},{8,9},{9,10},{10,1... | collective-permute-start | bytes 24584 | tf_op jit(solution)/shard_map/ppermute | solution.py:18
  92.2 1.0 divide_bitcast_fusion
  93.2 0.4 copy.31
  93.6 1.4 copy.33
  95.0 2.1 %fusion.5 = f32[4,1,512,128]{3,2,1,0:T(8,128)S(1)} fusion(f32[4,1,512,1]{3,2,1,0:T(8,128)} %copy.33, f32[1,1,512,128]{3,2,1,0:T(8,128)S(1)} %get-tuple-element.6, f32[1,1,512,128]{3,2,1,0:T(8,128)S(1)} %get-tuple-element.8, f32[1,1,512,128]{3,2,1,0:T(8,128)S(1)} %get-tuple-element.7, f32[1,1,512,128]{3,2,1,0:T(8,128)S(1)} %get-tuple-element.5, ...), kind=kLoop, calls=%fused_computation.8 | loop fusion | flops 3407872 | bytes 3162112 | tf_op jit(solution)/shard_map/sub | solution.py:31
  97.2 0.7 copy-done.1
  97.8 0.1 copy-done.3
  98.0 0.1 copy-done.7
  98.1 0.1 fusion.14
  98.2 1.3 fusion.30
  99.6 1.5 copy.34
  101.1 1.3 collective-permute-start.6
  102.4 0.3 copy.36
  102.7 4.0 %collective-permute-start.7 = (f32[4,1,512,1]{2,0,3,1:T(4,128)S(1)}, f32[4,1,512,1]{2,0,3,1:T(4,128)S(1)}, u32[]{:S(2)}, u32[]{:S(2)}) collective-permute-start(f32[4,1,512,1]{2,0,3,1:T(4,128)S(1)} %copy.36), channel_id=1, source_target_pairs={{0,1},{1,2},{2,3},{3,4},{4,5},{5,6},{6,7},{7,8},{8,9},{9,10},{10,1... | collective-permute-start | bytes 24584 | tf_op jit(solution)/shard_map/ppermute | solution.py:18
  106.8 0.4 copy.35
  107.2 0.3 collective-permute-done.7
  107.5 1.4 copy.37
  108.9 2.1 %fusion.2 = f32[4,1,512,128]{3,2,1,0:T(8,128)S(1)} fusion(f32[4,1,512,128]{3,2,1,0:T(8,128)S(1)} %fusion.14, f32[4,1,512,1]{3,2,1,0:T(8,128)} %copy.37, f32[4,1,512,1]{3,2,1,0:T(8,128)S(1)} %copy.35), kind=kLoop, calls=%fused_computation.3 | loop fusion | flops 1835008 | bytes 2113536 | tf_op jit(solution)/shard_map/sub | solution.py:31
  111.1 0.8 copy-done.2
  111.9 0.1 copy-done.4
  112.0 0.1 copy-done.6
  112.1 0.1 copy-done.8
  112.2 0.2 fusion.15
  112.3 0.7 fusion.17
  113.1 34.5 %reduce-scatter.3.cloned.1.call-done = f32[128,128]{1,0:T(8,128)} async-done(((f32[512,128]{1,0:T(8,128)}), f32[128,128]{1,0:T(8,128)}) %reduce-scatter.3.cloned.1.call-update) | async-done | bytes 65552 | tf_op jit(solution)/shard_map/reduce_scatter | solution.py:67
  147.6 34.5 %reduce-scatter.5.cloned.1.call-done = f32[128,128]{1,0:T(8,128)} async-done(((f32[512,128]{1,0:T(8,128)}), f32[128,128]{1,0:T(8,128)}) %reduce-scatter.5.cloned.1.call-update) | async-done | bytes 65552 | tf_op jit(solution)/shard_map/reduce_scatter | solution.py:67
  182.1 1.5 pad_maximum_fusion.22
  (41 shorter events, 0.8 us)
Async XLA Ops:
  6.5 26.3 %copy-start.17 = (f32[2,1,512,128]{3,2,1,0:T(8,128)S(1)}, f32[2,1,512,128]{3,2,1,0:T(8,128)}, u32[]{:S(2)}) copy-start(f32[2,1,512,128]{3,2,1,0:T(8,128)} %param.4) | copy-start | bytes 1572868
  6.5 26.3 %copy-start.18 = (f32[2,1,512,128]{3,2,1,0:T(8,128)S(1)}, f32[2,1,512,128]{3,2,1,0:T(8,128)}, u32[]{:S(2)}) copy-start(f32[2,1,512,128]{3,2,1,0:T(8,128)} %param.5) | copy-start | bytes 1572868
  8.5 24.4 %all-to-all-start = ((f32[8,64,128]{2,0,1:T(8,128)}), f32[8,64,128]{2,0,1:T(8,128)S(1)}, u32[]{:S(2)}, u32[]{:S(2)}) async-start(f32[8,64,128]{2,0,1:T(8,128)} %get-tuple-element.39), calls=%async_computation | async-start | bytes 524288 | tf_op jit(solution)/shard_map/all_to_all | solution.py:40
  36.9 6.4 %collective-permute-start = (f32[4,1,512,1]{2,0,3,1:T(4,128)S(1)}, f32[4,1,512,1]{2,0,3,1:T(4,128)S(1)}, u32[]{:S(2)}, u32[]{:S(2)}) collective-permute-start(f32[4,1,512,1]{2,0,3,1:T(4,128)S(1)} %copy.22), channel_id=1, source_target_pairs={{1,0},{2,1},{3,2},{4,3},{5,4},{6,5},{7,6},{8,7},{9,8},{10,9},{11,1... | collective-permute-start | bytes 24584 | tf_op jit(solution)/shard_map/ppermute | solution.py:21
  38.5 5.1 %collective-permute-start.1 = (f32[4,1,512,1]{2,0,3,1:T(4,128)S(1)}, f32[4,1,512,1]{2,0,3,1:T(4,128)S(1)}, u32[]{:S(2)}, u32[]{:S(2)}) collective-permute-start(f32[4,1,512,1]{2,0,3,1:T(4,128)S(1)} %copy.24), channel_id=1, source_target_pairs={{0,1},{1,2},{2,3},{3,4},{4,5},{5,6},{6,7},{7,8},{8,9},{9,10},{10,1... | collective-permute-start | bytes 24584 | tf_op jit(solution)/shard_map/ppermute | solution.py:18
  47.1 1.1 copy-start
  47.2 0.7 copy-start.9
  47.2 0.8 copy-start.11
  47.3 0.9 copy-start.13
  47.3 1.0 copy-start.15
  51.2 19.3 %collective-permute-start.2 = (f32[4,1,512,1]{2,0,3,1:T(4,128)S(1)}, f32[4,1,512,1]{2,0,3,1:T(4,128)S(1)}, u32[]{:S(2)}, u32[]{:S(2)}) collective-permute-start(f32[4,1,512,1]{2,0,3,1:T(4,128)S(1)} %copy.26), channel_id=1, source_target_pairs={{1,0},{2,1},{3,2},{4,3},{5,4},{6,5},{7,6},{8,7},{9,8},{10,9},{11,1... | collective-permute-start | bytes 24584 | tf_op jit(solution)/shard_map/ppermute | solution.py:21
  52.8 18.1 %collective-permute-start.3 = (f32[4,1,512,1]{2,0,3,1:T(4,128)S(1)}, f32[4,1,512,1]{2,0,3,1:T(4,128)S(1)}, u32[]{:S(2)}, u32[]{:S(2)}) collective-permute-start(f32[4,1,512,1]{2,0,3,1:T(4,128)S(1)} %copy.28), channel_id=1, source_target_pairs={{0,1},{1,2},{2,3},{3,4},{4,5},{5,6},{6,7},{7,8},{8,9},{9,10},{10,1... | collective-permute-start | bytes 24584 | tf_op jit(solution)/shard_map/ppermute | solution.py:18
  56.8 24.2 %all-to-all-start.1 = ((f32[8,64,128]{2,0,1:T(8,128)}), f32[8,64,128]{2,0,1:T(8,128)}, u32[]{:S(2)}, u32[]{:S(2)}) async-start(f32[8,64,128]{2,0,1:T(8,128)} %get-tuple-element.38), calls=%async_computation.2 | async-start | bytes 524288 | tf_op jit(solution)/shard_map/all_to_all | solution.py:40
  70.5 77.1 %reduce-scatter.3.cloned.1.call-start = ((), (), s32[]{:S(2)}) async-start(), calls=%async_computation.4 | async-start | bytes 327680 | tf_op jit(solution)/shard_map/reduce_scatter | solution.py:67
  74.4 1.0 copy-start.10
  74.4 1.0 copy-start.12
  74.4 1.1 copy-start.14
  74.4 1.2 copy-start.16
  86.6 6.6 %collective-permute-start.4 = (f32[4,1,512,1]{2,0,3,1:T(4,128)S(1)}, f32[4,1,512,1]{2,0,3,1:T(4,128)S(1)}, u32[]{:S(2)}, u32[]{:S(2)}) collective-permute-start(f32[4,1,512,1]{2,0,3,1:T(4,128)S(1)} %copy.30), channel_id=1, source_target_pairs={{1,0},{2,1},{3,2},{4,3},{5,4},{6,5},{7,6},{8,7},{9,8},{10,9},{11,1... | collective-permute-start | bytes 24584 | tf_op jit(solution)/shard_map/ppermute | solution.py:21
  88.2 5.4 %collective-permute-start.5 = (f32[4,1,512,1]{2,0,3,1:T(4,128)S(1)}, f32[4,1,512,1]{2,0,3,1:T(4,128)S(1)}, u32[]{:S(2)}, u32[]{:S(2)}) collective-permute-start(f32[4,1,512,1]{2,0,3,1:T(4,128)S(1)} %copy.32), channel_id=1, source_target_pairs={{0,1},{1,2},{2,3},{3,4},{4,5},{5,6},{6,7},{7,8},{8,9},{9,10},{10,1... | collective-permute-start | bytes 24584 | tf_op jit(solution)/shard_map/ppermute | solution.py:18
  97.1 0.7 copy-start.1
  97.2 0.8 copy-start.3
  97.2 0.9 copy-start.5
  97.2 0.9 copy-start.7
  101.1 5.7 %collective-permute-start.6 = (f32[4,1,512,1]{2,0,3,1:T(4,128)S(1)}, f32[4,1,512,1]{2,0,3,1:T(4,128)S(1)}, u32[]{:S(2)}, u32[]{:S(2)}) collective-permute-start(f32[4,1,512,1]{2,0,3,1:T(4,128)S(1)} %copy.34), channel_id=1, source_target_pairs={{1,0},{2,1},{3,2},{4,3},{5,4},{6,5},{7,6},{8,7},{9,8},{10,9},{11,1... | collective-permute-start | bytes 24584 | tf_op jit(solution)/shard_map/ppermute | solution.py:21
  102.7 4.8 %collective-permute-start.7 = (f32[4,1,512,1]{2,0,3,1:T(4,128)S(1)}, f32[4,1,512,1]{2,0,3,1:T(4,128)S(1)}, u32[]{:S(2)}, u32[]{:S(2)}) collective-permute-start(f32[4,1,512,1]{2,0,3,1:T(4,128)S(1)} %copy.36), channel_id=1, source_target_pairs={{0,1},{1,2},{2,3},{3,4},{4,5},{5,6},{6,7},{7,8},{8,9},{9,10},{10,1... | collective-permute-start | bytes 24584 | tf_op jit(solution)/shard_map/ppermute | solution.py:18
  106.8 75.4 %reduce-scatter.5.cloned.1.call-start = ((), (), s32[]{:S(2)}) async-start(), calls=%async_computation.5 | async-start | bytes 327680 | tf_op jit(solution)/shard_map/reduce_scatter | solution.py:67
  111.0 1.0 copy-start.2
  111.0 1.0 copy-start.4
  111.0 1.1 copy-start.6
  111.0 1.2 copy-start.8
Sparse Core Ops, SparseCore 0:
  106.9 40.6 reduce-scatter.2
  150.5 31.5 reduce-scatter.4
where the time goes:
time: 191 us; the launch traced here: 190 us
  waiting for transfers between devices  84.8 us (44%)
  starting transfers between devices  48.4 us (25%)
  local copies, waits for them, and re-layouts  25.8 us (14%)
  other arithmetic  17.1 us (9%)
  between operations  14.5 us (8%)
    reduce_scatter x2, waiting for transfers between devices, shards(): lax.psum_scatter(product, 'freq', scatter_dimension=0, tiled=True)  69 us
    all_to_all x2, starting transfers between devices, slice_speed(): lax.all_to_all(layer, 'strip', split_axis=1, concat_axis=0, tiled=True)  27.2 us
    ppermute x4, starting transfers between devices, with_halo(): lax.ppermute(lax.slice_in_dim(block, block.shape[dim] - width, None, axis...  15.9 us
    all_to_all x2, waiting for transfers between devices, slice_speed(): lax.all_to_all(layer, 'strip', split_axis=1, concat_axis=0, tiled=True)  15.4 us
    slice x8, local copies, waits for them, and re-layouts, with_halo(): lax.slice_in_dim(block, 0, width, axis=dim)  11.5 us
    sub x4, other arithmetic, laplace_rimmed(): return across + along - 4.0 * center  8.4 us
    ppermute x4, local copies, waits for them, and re-layouts, with_halo(): lax.ppermute(lax.slice_in_dim(block, block.shape[dim] - width, None, axis...  5.49 us
    ppermute x4, starting transfers between devices, with_halo(): lax.ppermute(lax.slice_in_dim(block, 0, width, axis=dim), axis, backward)  5.17 us
  transfers between devices with their start and end apart: 12, of which 5 were waited for; matrix products, arithmetic and copies ran while one was open for 7% of the time, Pallas kernels for 0%

commit v1 on v0

v1 whole, which is shorter than its diff:
```python
import functools

import jax
import jax.numpy as jnp
from jax import lax
from jax.experimental import pallas as pl
from jax.experimental.pallas import tpu as pltpu
from jax.sharding import PartitionSpec as P

FREQS = 4
LANES = 128
TILE = 8
WIN = 32
HALO = 4
CORE_ROWS = 128
ROWS = CORE_ROWS + 2 * TILE
GUARD = TILE
CHUNK = 48

phase_depth = 2.0
fd_coef = 0.03

F32 = jnp.float32


def lanes_of(rows):
    return lax.broadcasted_iota(jnp.int32, (rows, LANES), 1)


def lane_roll(x, shift):
    return pltpu.roll(x, shift % LANES, 1)


def pack_speed(vel_ref, out_ref):
    strips = vel_ref.shape[2] // LANES
    lane = lanes_of(TILE)
    sublane = lax.broadcasted_iota(jnp.int32, (TILE, LANES), 0)
    for strip in range(strips):
        base = 17 * strip
        after = min(strip + 1, strips - 1)
        before = max(strip - 1, 0)
        beside = jnp.zeros((TILE, LANES), F32)
        for depth in range(2):
            here = vel_ref[depth, :, strip * LANES : (strip + 1) * LANES]
            out_ref[base + depth * TILE : base + (depth + 1) * TILE, :] = here
            right = vel_ref[depth, :, after * LANES : (after + 1) * LANES]
            left = vel_ref[depth, :, before * LANES : (before + 1) * LANES]
            start = depth * 2 * HALO
            right = lane_roll(right, start) if depth else right
            left = lane_roll(left, start + 2 * HALO)
            beside = jnp.where((lane >= start) & (lane < start + HALO), right, beside)
            beside = jnp.where(
                (lane >= start + HALO) & (lane < start + 2 * HALO), left, beside
            )
        for shift in (16, 32, 64):
            beside = beside + lane_roll(beside, shift)
        beside = jnp.where(lane // 16 == 7 - sublane, beside, 0.0)
        out_ref[base + 16 : base + 17, :] = jnp.sum(beside, axis=0, keepdims=True)


def prepare(src_ref, rec_ref, *outs):
    messages, own_ref, to_left_ref, to_right_ref = outs[:FREQS], outs[4], outs[5], outs[6]
    fields = (src_ref.at[0, 0], src_ref.at[1, 0], rec_ref.at[0, 0], rec_ref.at[1, 0])
    freq = lax.axis_index("freq")
    rows = src_ref.shape[2]
    for k in range(FREQS):
        block = freq ^ k
        mid = pl.multiple_of(block * CORE_ROWS, CORE_ROWS)
        above = pl.multiple_of(jnp.maximum(mid - TILE, 0), TILE)
        below = pl.multiple_of(jnp.minimum(mid + CORE_ROWS, rows - TILE), TILE)
        for part, field in enumerate(fields):
            out = messages[k].at[part]
            out[TILE : TILE + CORE_ROWS, :] = field[pl.ds(mid, CORE_ROWS), :]
            out[0:TILE, :] = jnp.where(block > 0, field[pl.ds(above, TILE), :], 0.0)
            out[TILE + CORE_ROWS : ROWS, :] = jnp.where(
                block < FREQS - 1, field[pl.ds(below, TILE), :], 0.0
            )
    groups = rows // 64
    lane = lanes_of(64)
    place = lane % WIN
    to_left = jnp.zeros((64, LANES), F32)
    to_right = jnp.zeros((64, LANES), F32)
    for q in range(groups):
        edge = jnp.zeros((64, LANES), F32)
        for part, field in enumerate(fields):
            value = field[q * 64 : (q + 1) * 64, :]
            mine = lane // WIN == part
            edge = jnp.where(
                mine & (place >= 4) & (place < 16), lane_roll(value, part * WIN + 4), edge
            )
            edge = jnp.where(
                mine & (place >= 16) & (place < 28), lane_roll(value, part * WIN + 28), edge
            )
        own_ref[q * 64 : (q + 1) * 64, :] = edge
        slot = place // HALO == q
        to_left = jnp.where(slot, lane_roll(edge, HALO * q - 4), to_left)
        to_right = jnp.where(slot, lane_roll(edge, HALO * q - 24), to_right)
    to_left_ref[...] = to_left
    to_right_ref[...] = to_right


def join_edges(own_ref, left_ref, right_ref, omega_ref, *outs):
    messages, full = outs[:FREQS], outs[FREQS]
    freq = lax.axis_index("freq")
    rows = own_ref.shape[0]
    lane = lanes_of(64)
    place = lane % WIN
    full[0:TILE, :] = jnp.zeros((TILE, LANES), F32)
    full[TILE + rows :, :] = jnp.zeros((TILE, LANES), F32)
    left = left_ref[...]
    right = right_ref[...]
    for q in range(rows // 64):
        edge = own_ref[q * 64 : (q + 1) * 64, :]
        edge = jnp.where(place < 4, lane_roll(left, -HALO * q), edge)
        edge = jnp.where(place >= 28, lane_roll(right, 28 - HALO * q), edge)
        full[TILE + q * 64 : TILE + (q + 1) * 64, :] = edge
    for k in range(FREQS):
        start = pl.multiple_of((freq ^ k) * CORE_ROWS, CORE_ROWS)
        messages[k][0:ROWS, :] = full[pl.ds(start, ROWS), :]
        messages[k][ROWS : ROWS + TILE, :] = jnp.full((TILE, LANES), omega_ref[0], F32)


def sin_cos(x):
    turns = jnp.round(x * 0.6366197723675814)
    r = x - turns * 1.5703125
    r = r - turns * 4.837512969970703125e-4
    r = r - turns * 7.54978995489188216e-8
    square = r * r
    sine = r + r * square * (
        -1.6666654611e-1 + square * (8.3321608736e-3 + square * -1.9515295891e-4)
    )
    cosine = (
        1.0
        - 0.5 * square
        + square
        * square
        * (
            4.166664568298827e-2
            + square * (-1.388731625493765e-3 + square * 2.443315711809948e-5)
        )
    )
    quarter = turns.astype(jnp.int32)
    odd = (quarter & 1) == 1
    out_sin = jnp.where(odd, cosine, sine)
    out_cos = jnp.where(odd, sine, cosine)
    out_sin = jnp.where((quarter & 2) == 2, -out_sin, out_sin)
    out_cos = jnp.where(((quarter + 1) & 2) == 2, -out_cos, out_cos)
    return out_sin, out_cos


def march(*refs):
    speed_ref = refs[0]
    mains = refs[1:5]
    edges = refs[5:9]
    image_ref = refs[9]
    waves, speed, coef, omega, first, second = refs[10:]
    freq = lax.axis_index("freq")
    strip = lax.axis_index("strip")
    strips = lax.axis_size("strip")
    lane = lanes_of(TILE)
    place = lane % WIN

    block_rows = 17 * (CORE_ROWS // TILE)
    mid = pl.multiple_of(freq * block_rows, TILE)
    above = pl.multiple_of(jnp.maximum(mid - 24, 0), TILE)
    below = pl.multiple_of(jnp.minimum(mid + block_rows, speed_ref.shape[0] - 24), TILE)
    stage = omega.at[pl.ds(TILE * 5, 320), :]
    stage[0:24, :] = speed_ref[pl.ds(above, 24), :]
    stage[24 : 24 + block_rows, :] = speed_ref[pl.ds(mid, block_rows), :]
    stage[24 + block_rows : 48 + block_rows, :] = speed_ref[pl.ds(below, 24), :]
    blocks = CORE_ROWS // TILE + 2
    off_left = (place < 4) & (strip == 0)
    off_right = (place >= 28) & (strip == strips - 1)
    inside = jnp.logical_not(off_left | off_right)
    for i in range(blocks):
        base = 7 + 17 * i
        beside = jnp.broadcast_to(stage[base + 16 : base + 17, :], (TILE, LANES))
        beside = pltpu.roll(beside, 0, 1, stride=16, stride_axis=0)
        live = True
        if i == 0:
            live = freq > 0
        elif i == blocks - 1:
            live = freq < FREQS - 1
        for depth in range(2):
            here = stage[base + depth * TILE : base + (depth + 1) * TILE, :]
            halo = lane_roll(beside, 28 - 112 - 2 * HALO * depth)
            window = jnp.where((lane >= 28) & (lane < 36), halo, 0.0)
            window = jnp.where((lane >= 4) & (lane < 16), lane_roll(here, 4), window)
            window = jnp.where((lane >= 16) & (lane < 28), lane_roll(here, 28), window)
            window = window + lane_roll(window, WIN)
            window = window + lane_roll(window, 2 * WIN)
            rows = slice(i * TILE, (i + 1) * TILE)
            speed[0, depth, rows, :] = phase_depth / here
            speed[1, depth, rows, :] = phase_depth / window
            main_coef = fd_coef * here
            edge_coef = jnp.where(inside, fd_coef * window, 0.0)
            if live is not True:
                main_coef = jnp.where(live, main_coef, 0.0)
                edge_coef = jnp.where(live, edge_coef, 0.0)
            coef[0, depth, rows, :] = main_coef
            coef[1, depth, rows, :] = edge_coef

    lane_omega = jnp.zeros((TILE, LANES), F32)
    for k in range(FREQS):
        row = edges[k][ROWS : ROWS + TILE, :]
        omega[k * TILE : (k + 1) * TILE, :] = row
        lane_omega = jnp.where(lane // WIN == k, row, lane_omega)
        waves[k] = mains[k][...]
    omega[FREQS * TILE : (FREQS + 1) * TILE, :] = lane_omega
    for i in range(ROWS // TILE):
        rows = slice(i * TILE, (i + 1) * TILE)
        for part in range(4):
            value = jnp.zeros((TILE, LANES), F32)
            for k in range(FREQS):
                piece = edges[k][rows, :]
                value = jnp.where(
                    lane // WIN == k, lane_roll(piece, (k - part) * WIN), value
                )
            waves[FREQS, part, rows, :] = value

    guard = jnp.zeros((TILE, LANES), F32)
    for buffer in (first, second):
        for part in range(4):
            buffer[part, 0:GUARD, :] = guard
            buffer[part, GUARD + ROWS :, :] = guard
    image_ref[...] = jnp.zeros_like(image_ref)

    chunks = ROWS // CHUNK

    def turn(values, depth, kind, row, freq_row):
        theta = freq_row * speed[kind, depth, pl.ds(row, CHUNK), :]
        sine, cosine = sin_cos(theta)
        src_re, src_im, rec_re, rec_im = values
        return (
            src_re * cosine - src_im * sine,
            src_re * sine + src_im * cosine,
            rec_re * cosine + rec_im * sine,
            rec_im * cosine - rec_re * sine,
        )

    def substep(buffer, depth, kind, row, freq_inverse):
        step = coef[kind, depth, pl.ds(row, CHUNK), :] * freq_inverse
        centers = []
        laps = []
        for part in range(4):
            center = buffer[part, pl.ds(row + GUARD, CHUNK), :]
            up = buffer[part, pl.ds(row + GUARD - 1, CHUNK), :]
            down = buffer[part, pl.ds(row + GUARD + 1, CHUNK), :]
            across = lane_roll(center, 1) + lane_roll(center, LANES - 1)
            centers.append(center)
            laps.append((across + (up + down)) - 4.0 * center)
        src_re, src_im, rec_re, rec_im = centers
        return (
            src_re - step * laps[1],
            src_im + step * laps[0],
            rec_re + step * laps[3],
            rec_im - step * laps[2],
        )

    def store(buffer, row, values):
        for part in range(4):
            buffer[part, pl.ds(row + GUARD, CHUNK), :] = values[part]

    def product(values):
        return values[0] * values[2] + values[1] * values[3]

    def item(k, kind, add_image):
        freq_row = omega[pl.ds(pl.multiple_of(k * TILE, TILE), 1), :]
        freq_inverse = 1.0 / freq_row

        for j in range(chunks):
            row = j * CHUNK
            values = [waves[k, part, pl.ds(row, CHUNK), :] for part in range(4)]
            store(first, row, turn(values, 0, kind, row, freq_row))
        for j in range(chunks):
            store(second, j * CHUNK, substep(first, 0, kind, j * CHUNK, freq_inverse))
        for j in range(chunks):
            row = j * CHUNK
            values = substep(second, 0, kind, row, freq_inverse)
            add_image(0, row, product(values))
            store(first, row, turn(values, 1, kind, row, freq_row))
        for j in range(chunks):
            store(second, j * CHUNK, substep(first, 1, kind, j * CHUNK, freq_inverse))
        for j in range(chunks):
            values = substep(second, 1, kind, j * CHUNK, freq_inverse)
            add_image(1, j * CHUNK, product(values))

    def cut(row):
        low = max(row, TILE)
        high = min(row + CHUNK, TILE + CORE_ROWS)
        return low, high

    def add_main(depth, row, value):
        low, high = cut(row)
        image_ref[depth, low - TILE : high - TILE, :] += value[low - row : high - row, :]

    def patch(depth, row, value):
        low, high = cut(row)
        value = value[low - row : high - row, :]
        value = value + lane_roll(value, WIN)
        value = value + lane_roll(value, 2 * WIN)
        wide = lanes_of(high - low)
        old = image_ref[depth, low - TILE : high - TILE, :]
        new = jnp.where(wide < HALO, lane_roll(value, -4), old)
        new = jnp.where(wide >= LANES - HALO, lane_roll(value, 4), new)
        image_ref[depth, low - TILE : high - TILE, :] = new

    def one_freq(k, carry):
        item(k, 0, add_main)
        return carry

    lax.fori_loop(0, FREQS, one_freq, 0)
    item(FREQS, 1, patch)


def shape(*dims):
    return jax.ShapeDtypeStruct(dims, F32)


def shards(source, receiver, velocity, omega):
    strips = lax.axis_size("strip")
    rows = source.shape[2]
    vmem = pl.BlockSpec(memory_space=pltpu.VMEM)
    smem = pl.BlockSpec(memory_space=pltpu.SMEM)

    packed = pl.pallas_call(
        pack_speed, out_shape=shape(17 * strips, LANES), in_specs=[vmem], out_specs=vmem
    )(velocity)
    speeds = lax.all_to_all(
        packed.reshape(strips, 1, 17 * LANES), "strip", split_axis=0, concat_axis=0, tiled=True
    ).reshape(17 * strips, LANES)

    prepared = pl.pallas_call(
        prepare,
        out_shape=[shape(4, ROWS, LANES)] * FREQS
        + [shape(rows, LANES), shape(64, LANES), shape(64, LANES)],
        in_specs=[vmem, vmem],
        out_specs=[vmem] * 7,
    )(source, receiver)
    mains, own, to_left, to_right = prepared[:FREQS], prepared[4], prepared[5], prepared[6]

    def across(x, k):
        return lax.ppermute(x, "freq", [(i, i ^ k) for i in range(FREQS)])

    from_left = lax.ppermute(to_right, "strip", [(i, i + 1) for i in range(strips - 1)])
    from_right = lax.ppermute(to_left, "strip", [(i + 1, i) for i in range(strips - 1)])
    mains = [mains[0]] + [across(mains[k], k) for k in range(1, FREQS)]
    edges = pl.pallas_call(
        join_edges,
        out_shape=[shape(ROWS + TILE, LANES)] * FREQS,
        in_specs=[vmem, vmem, vmem, smem],
        out_specs=[vmem] * FREQS,
        scratch_shapes=[pltpu.VMEM((rows + 2 * TILE, LANES), F32)],
    )(own, from_left, from_right, omega)
    edges = [edges[0]] + [across(edges[k], k) for k in range(1, FREQS)]

    return pl.pallas_call(
        march,
        out_shape=shape(2, CORE_ROWS, LANES),
        in_specs=[vmem] * 9,
        out_specs=vmem,
        scratch_shapes=[
            pltpu.VMEM((FREQS + 1, 4, ROWS, LANES), F32),
            pltpu.VMEM((2, 2, ROWS, LANES), F32),
            pltpu.VMEM((2, 2, ROWS, LANES), F32),
            pltpu.VMEM((5 * TILE + 320, LANES), F32),
            pltpu.VMEM((4, ROWS + 2 * GUARD, LANES), F32),
            pltpu.VMEM((4, ROWS + 2 * GUARD, LANES), F32),
        ],
    )(speeds, *mains, *edges)


def solution(mesh):
    return jax.shard_map(
        shards,
        mesh=mesh,
        in_specs=(
            P(None, "freq", None, "strip"),
            P(None, "freq", None, "strip"),
            P(None, "strip", None),
            P("freq"),
        ),
        out_specs=P(None, "freq", "strip"),
        check_vma=False,
    )
```

time: 191 us -> 59 us (0.31)
  the two profiles are of different devices: /device:TPU:1 before, /device:TPU:121 now
where the time goes in v1:
time: 59 us; the launch traced here: 58.6 us
  starting transfers between devices  27 us (46%)
  Pallas kernels  19 us (32%)
  waiting for transfers between devices  10.2 us (17%)
  local copies, waits for them, and re-layouts  1.67 us (3%)
  between operations  0.76 us (1%)
    all_to_all x1, starting transfers between devices, shards(): lax.all_to_all(packed.reshape(strips, 1, 17 * LANES), 'strip', split_axis...  10.9 us
    ppermute x6, starting transfers between devices, across(): return lax.ppermute(x, 'freq', [(i, i ^ k) for i in range(FREQS)])  9.86 us
    pallas_call x1, Pallas kernels, shards(): pl.pallas_call(march, out_shape=shape(2, CORE_ROWS, LANES), in_specs=[vme...  8.05 us
    pallas_call x1, Pallas kernels, shards(): pl.pallas_call(pack_speed, out_shape=shape(17 * strips, LANES), in_specs=...  5.64 us
    ppermute x1, waiting for transfers between devices, shards(): lax.ppermute(to_left, 'strip', [(i + 1, i) for i in range(strips - 1)])  5.59 us
    ppermute x6, waiting for transfers between devices, across(): return lax.ppermute(x, 'freq', [(i, i ^ k) for i in range(FREQS)])  4.61 us
    ppermute x1, starting transfers between devices, shards(): lax.ppermute(to_right, 'strip', [(i, i + 1) for i in range(strips - 1)])  4.29 us
    pallas_call x1, Pallas kernels, shards(): pl.pallas_call(prepare, out_shape=[shape(4, ROWS, LANES)] * FREQS + [shap...  3.49 us
  transfers between devices with their start and end apart: 9, of which 3 were waited for; matrix products, arithmetic and copies ran while one was open for 0% of the time, Pallas kernels for 9%

profile of v1, /device:TPU:121, one launch (start us, length us, event | category | flops | bytes accessed | tf_op | source)
XLA Modules:
  0.0 58.6 jit_solution(12926055345483688529)
XLA Ops:
  0.0 5.6 %shard_map.46 = f32[1088,128]{1,0:T(8,128)} custom-call(f32[2,8,8192]{2,1,0:T(8,128)} %vel_ref.1), custom_call_target="tpu_custom_call" | custom-call | tf_op jit(solution)/shard_map/pallas_call | solution.py:326
  5.6 10.9 %all-to-all-start = ((f32[64,1,2176]{2,1,0:T(1,128)}), f32[64,1,2176]{2,1,0:T(1,128)S(1)}, u32[]{:S(2)}, u32[]{:S(2)}) async-start(f32[64,1,2176]{2,1,0:T(1,128)} %bitcast.3), calls=%async_computation | async-start | bytes 1114112 | tf_op jit(solution)/shard_map/all_to_all | solution.py:329
  16.5 3.5 %shard_map.47 = (f32[4,144,128]{2,1,0:T(8,128)}, f32[4,144,128]{2,1,0:T(8,128)}, f32[4,144,128]{2,1,0:T(8,128)}, f32[4,144,128]{2,1,0:T(8,128)}, f32[512,128]{1,...) custom-call(f32[2,1,512,128]{3,2,1,0:T(8,128)} %src_ref.1, f32[2,1,512,128]{3,2,1,0:T(8,128)} %rec_ref.1), custom_call_target="tpu_custom_call" | custom-call | tf_op jit(solution)/shard_map/pallas_call | solution.py:333
  20.0 1.2 %collective-permute-start = (f32[4,144,128]{2,1,0:T(8,128)}, f32[4,144,128]{2,1,0:T(8,128)S(1)}, u32[]{:S(2)}, u32[]{:S(2)}) collective-permute-start(f32[4,144,128]{2,1,0:T(8,128)} %get-tuple-element.17), channel_id=1, source_target_pairs={{0,64},{64,0},{128,192},{192,128},{1,65},{65,1},{129,193},{193,129... | collective-permute-start | bytes 884744 | tf_op jit(solution)/shard_map/ppermute | solution.py:343
  21.3 2.5 %collective-permute-start.1 = (f32[4,144,128]{2,1,0:T(8,128)}, f32[4,144,128]{2,1,0:T(8,128)S(1)}, u32[]{:S(2)}, u32[]{:S(2)}) collective-permute-start(f32[4,144,128]{2,1,0:T(8,128)} %get-tuple-element.18), channel_id=1, source_target_pairs={{0,128},{64,192},{128,0},{192,64},{1,129},{65,193},{129,1},{193,65... | collective-permute-start | bytes 884744 | tf_op jit(solution)/shard_map/ppermute | solution.py:343
  23.7 0.8 %collective-permute-start.2 = (f32[4,144,128]{2,1,0:T(8,128)}, f32[4,144,128]{2,1,0:T(8,128)S(1)}, u32[]{:S(2)}, u32[]{:S(2)}) collective-permute-start(f32[4,144,128]{2,1,0:T(8,128)} %get-tuple-element.19), channel_id=1, source_target_pairs={{0,192},{64,128},{128,64},{192,0},{1,193},{65,129},{129,65},{193,1... | collective-permute-start | bytes 884744 | tf_op jit(solution)/shard_map/ppermute | solution.py:343
  24.5 4.3 %collective-permute-start.3 = (f32[64,128]{1,0:T(8,128)}, f32[64,128]{1,0:T(8,128)S(1)}, u32[]{:S(2)}, u32[]{:S(2)}) collective-permute-start(f32[64,128]{1,0:T(8,128)} %get-tuple-element.21), channel_id=1, source_target_pairs={{0,1},{1,2},{2,3},{3,4},{4,5},{5,6},{6,7},{7,8},{8,9},{9,10},{10,1... | collective-permute-start | bytes 98312 | tf_op jit(solution)/shard_map/ppermute | solution.py:345
  28.8 1.9 %collective-permute-start.4 = (f32[64,128]{1,0:T(8,128)}, f32[64,128]{1,0:T(8,128)S(1)}, u32[]{:S(2)}, u32[]{:S(2)}) collective-permute-start(f32[64,128]{1,0:T(8,128)} %get-tuple-element.22), channel_id=1, source_target_pairs={{1,0},{2,1},{3,2},{4,3},{5,4},{6,5},{7,6},{8,7},{9,8},{10,9},{11,1... | collective-permute-start | bytes 98312 | tf_op jit(solution)/shard_map/ppermute | solution.py:346
  31.3 0.0 collective-permute-done.3.left_ref
  31.4 0.0 copy-start.7
  31.4 5.6 %collective-permute-done.4.right_ref = f32[64,128]{1,0:T(8,128)S(1)} collective-permute-done((f32[64,128]{1,0:T(8,128)}, f32[64,128]{1,0:T(8,128)S(1)}, u32[]{:S(2)}, u32[]{:S(2)}) %collective-permute-start.4) | collective-permute-done | bytes 32800 | tf_op jit(solution)/shard_map/ppermute | solution.py:346
  37.0 0.0 copy-start.8
  37.0 0.0 copy-done.7
  37.0 0.6 %copy-done.8 = f32[64,128]{1,0:T(8,128)} copy-done((f32[64,128]{1,0:T(8,128)}, f32[64,128]{1,0:T(8,128)S(1)}, u32[]{:S(2)}) %copy-start.8) | copy-done | bytes 32792
  37.6 1.9 %shard_map.48 = (f32[152,128]{1,0:T(8,128)}, f32[152,128]{1,0:T(8,128)}, f32[152,128]{1,0:T(8,128)}, f32[152,128]{1,0:T(8,128)}) custom-call(f32[512,128]{1,0:T(8,128)} %get-tuple-element.20.own_ref, f32[64,128]{1,0:T(8,128)} %copy-done.7, f32[64,128]{1,0:T(8,128)} %copy-done.8, f32[1]{0:T(128)S(6)} %copy.6.omega_ref), custom_call_target="tpu_custom_call" | custom-call | tf_op jit(solution)/shard_map/pallas_call | solution.py:348
  39.4 1.6 %collective-permute-start.5 = (f32[152,128]{1,0:T(8,128)}, f32[152,128]{1,0:T(8,128)S(1)}, u32[]{:S(2)}, u32[]{:S(2)}) collective-permute-start(f32[152,128]{1,0:T(8,128)} %get-tuple-element.24), channel_id=1, source_target_pairs={{0,64},{64,0},{128,192},{192,128},{1,65},{65,1},{129,193},{193,129... | collective-permute-start | bytes 233480 | tf_op jit(solution)/shard_map/ppermute | solution.py:343
  41.0 2.5 %collective-permute-start.6 = (f32[152,128]{1,0:T(8,128)}, f32[152,128]{1,0:T(8,128)S(1)}, u32[]{:S(2)}, u32[]{:S(2)}) collective-permute-start(f32[152,128]{1,0:T(8,128)} %get-tuple-element.25), channel_id=1, source_target_pairs={{0,128},{64,192},{128,0},{192,64},{1,129},{65,193},{129,1},{193,65... | collective-permute-start | bytes 233480 | tf_op jit(solution)/shard_map/ppermute | solution.py:343
  43.5 0.0 collective-permute-done.5.refs_6_
  43.5 0.0 copy-start.4
  43.5 1.4 %collective-permute-start.7 = (f32[152,128]{1,0:T(8,128)}, f32[152,128]{1,0:T(8,128)S(1)}, u32[]{:S(2)}, u32[]{:S(2)}) collective-permute-start(f32[152,128]{1,0:T(8,128)} %get-tuple-element.26), channel_id=1, source_target_pairs={{0,192},{64,128},{128,64},{192,0},{1,193},{65,129},{129,65},{193,1... | collective-permute-start | bytes 233480 | tf_op jit(solution)/shard_map/ppermute | solution.py:343
  44.9 1.9 %collective-permute-done.6.refs_7_ = f32[152,128]{1,0:T(8,128)S(1)} collective-permute-done((f32[152,128]{1,0:T(8,128)}, f32[152,128]{1,0:T(8,128)S(1)}, u32[]{:S(2)}, u32[]{:S(2)}) %collective-permute-start.6) | collective-permute-done | bytes 77856 | tf_op jit(solution)/shard_map/ppermute | solution.py:343
  46.7 0.0 copy-start.5
  46.7 2.7 %collective-permute-done.7.refs_8_ = f32[152,128]{1,0:T(8,128)S(1)} collective-permute-done((f32[152,128]{1,0:T(8,128)}, f32[152,128]{1,0:T(8,128)S(1)}, u32[]{:S(2)}, u32[]{:S(2)}) %collective-permute-start.7) | collective-permute-done | bytes 77856 | tf_op jit(solution)/shard_map/ppermute | solution.py:343
  49.5 0.0 copy-start.6
  49.5 0.0 collective-permute-done.refs_2_
  49.5 0.0 copy-start.1
  49.5 0.0 collective-permute-done.1.refs_3_
  49.5 0.0 copy-start.2
  49.5 0.0 collective-permute-done.2.refs_4_
  49.5 0.0 copy-start.3
  49.5 0.0 all-to-all-done
  49.5 0.0 copy-start
  49.5 0.0 copy-done.4
  49.5 0.0 copy-done.5
  49.5 0.5 copy-done.6
  50.1 0.1 copy-done.1
  50.2 0.1 copy-done.2
  50.3 0.1 copy-done.3
  50.5 0.1 copy-done
  50.6 8.0 %shard_map.49 = f32[2,128,128]{2,1,0:T(8,128)} custom-call(f32[1088,128]{1,0:T(8,128)} %bitcast.2, f32[4,144,128]{2,1,0:T(8,128)} %get-tuple-element.16.refs_1_, f32[4,144,128]{2,1,0:T(8,128)} %copy-done.1, f32[4,144,128]{2,1,0:T(8,128)} %copy-done.2, f32[4,144,128]{2,1,0:T(8,128)} %copy-done.3, f32[152,128]{1,0:T(8,128)} %get-tuple-element.23.refs_5_, ...), custom_call_target="tpu_custom_call" | custom-call | tf_op jit(solution)/shard_map/pallas_call | solution.py:357
Async XLA Ops:
  5.6 43.9 %all-to-all-start = ((f32[64,1,2176]{2,1,0:T(1,128)}), f32[64,1,2176]{2,1,0:T(1,128)S(1)}, u32[]{:S(2)}, u32[]{:S(2)}) async-start(f32[64,1,2176]{2,1,0:T(1,128)} %bitcast.3), calls=%async_computation | async-start | bytes 1114112 | tf_op jit(solution)/shard_map/all_to_all | solution.py:329
  20.0 29.4 %collective-permute-start = (f32[4,144,128]{2,1,0:T(8,128)}, f32[4,144,128]{2,1,0:T(8,128)S(1)}, u32[]{:S(2)}, u32[]{:S(2)}) collective-permute-start(f32[4,144,128]{2,1,0:T(8,128)} %get-tuple-element.17), channel_id=1, source_target_pairs={{0,64},{64,0},{128,192},{192,128},{1,65},{65,1},{129,193},{193,129... | collective-permute-start | bytes 884744 | tf_op jit(solution)/shard_map/ppermute | solution.py:343
  21.3 28.2 %collective-permute-start.1 = (f32[4,144,128]{2,1,0:T(8,128)}, f32[4,144,128]{2,1,0:T(8,128)S(1)}, u32[]{:S(2)}, u32[]{:S(2)}) collective-permute-start(f32[4,144,128]{2,1,0:T(8,128)} %get-tuple-element.18), channel_id=1, source_target_pairs={{0,128},{64,192},{128,0},{192,64},{1,129},{65,193},{129,1},{193,65... | collective-permute-start | bytes 884744 | tf_op jit(solution)/shard_map/ppermute | solution.py:343
  23.7 25.8 %collective-permute-start.2 = (f32[4,144,128]{2,1,0:T(8,128)}, f32[4,144,128]{2,1,0:T(8,128)S(1)}, u32[]{:S(2)}, u32[]{:S(2)}) collective-permute-start(f32[4,144,128]{2,1,0:T(8,128)} %get-tuple-element.19), channel_id=1, source_target_pairs={{0,192},{64,128},{128,64},{192,0},{1,193},{65,129},{129,65},{193,1... | collective-permute-start | bytes 884744 | tf_op jit(solution)/shard_map/ppermute | solution.py:343
  24.5 6.9 %collective-permute-start.3 = (f32[64,128]{1,0:T(8,128)}, f32[64,128]{1,0:T(8,128)S(1)}, u32[]{:S(2)}, u32[]{:S(2)}) collective-permute-start(f32[64,128]{1,0:T(8,128)} %get-tuple-element.21), channel_id=1, source_target_pairs={{0,1},{1,2},{2,3},{3,4},{4,5},{5,6},{6,7},{7,8},{8,9},{9,10},{10,1... | collective-permute-start | bytes 98312 | tf_op jit(solution)/shard_map/ppermute | solution.py:345
  28.8 8.2 %collective-permute-start.4 = (f32[64,128]{1,0:T(8,128)}, f32[64,128]{1,0:T(8,128)S(1)}, u32[]{:S(2)}, u32[]{:S(2)}) collective-permute-start(f32[64,128]{1,0:T(8,128)} %get-tuple-element.22), channel_id=1, source_target_pairs={{1,0},{2,1},{3,2},{4,3},{5,4},{6,5},{7,6},{8,7},{9,8},{10,9},{11,1... | collective-permute-start | bytes 98312 | tf_op jit(solution)/shard_map/ppermute | solution.py:346
  31.4 5.6 %copy-start.7 = (f32[64,128]{1,0:T(8,128)}, f32[64,128]{1,0:T(8,128)S(1)}, u32[]{:S(2)}) copy-start(f32[64,128]{1,0:T(8,128)S(1)} %collective-permute-done.3.left_ref) | copy-start | bytes 98308
  37.0 0.6 %copy-start.8 = (f32[64,128]{1,0:T(8,128)}, f32[64,128]{1,0:T(8,128)S(1)}, u32[]{:S(2)}) copy-start(f32[64,128]{1,0:T(8,128)S(1)} %collective-permute-done.4.right_ref) | copy-start | bytes 98308
  39.4 4.0 %collective-permute-start.5 = (f32[152,128]{1,0:T(8,128)}, f32[152,128]{1,0:T(8,128)S(1)}, u32[]{:S(2)}, u32[]{:S(2)}) collective-permute-start(f32[152,128]{1,0:T(8,128)} %get-tuple-element.24), channel_id=1, source_target_pairs={{0,64},{64,0},{128,192},{192,128},{1,65},{65,1},{129,193},{193,129... | collective-permute-start | bytes 233480 | tf_op jit(solution)/shard_map/ppermute | solution.py:343
  41.0 5.7 %collective-permute-start.6 = (f32[152,128]{1,0:T(8,128)}, f32[152,128]{1,0:T(8,128)S(1)}, u32[]{:S(2)}, u32[]{:S(2)}) collective-permute-start(f32[152,128]{1,0:T(8,128)} %get-tuple-element.25), channel_id=1, source_target_pairs={{0,128},{64,192},{128,0},{192,64},{1,129},{65,193},{129,1},{193,65... | collective-permute-start | bytes 233480 | tf_op jit(solution)/shard_map/ppermute | solution.py:343
  43.5 6.0 %copy-start.4 = (f32[152,128]{1,0:T(8,128)}, f32[152,128]{1,0:T(8,128)S(1)}, u32[]{:S(2)}) copy-start(f32[152,128]{1,0:T(8,128)S(1)} %collective-permute-done.5.refs_6_) | copy-start | bytes 233476
  43.5 6.0 %collective-permute-start.7 = (f32[152,128]{1,0:T(8,128)}, f32[152,128]{1,0:T(8,128)S(1)}, u32[]{:S(2)}, u32[]{:S(2)}) collective-permute-start(f32[152,128]{1,0:T(8,128)} %get-tuple-element.26), channel_id=1, source_target_pairs={{0,192},{64,128},{128,64},{192,0},{1,193},{65,129},{129,65},{193,1... | collective-permute-start | bytes 233480 | tf_op jit(solution)/shard_map/ppermute | solution.py:343
  46.7 2.8 %copy-start.5 = (f32[152,128]{1,0:T(8,128)}, f32[152,128]{1,0:T(8,128)S(1)}, u32[]{:S(2)}) copy-start(f32[152,128]{1,0:T(8,128)S(1)} %collective-permute-done.6.refs_7_) | copy-start | bytes 233476
  49.5 0.6 %copy-start.6 = (f32[152,128]{1,0:T(8,128)}, f32[152,128]{1,0:T(8,128)S(1)}, u32[]{:S(2)}) copy-start(f32[152,128]{1,0:T(8,128)S(1)} %collective-permute-done.7.refs_8_) | copy-start | bytes 233476
  49.5 0.8 %copy-start.1 = (f32[4,144,128]{2,1,0:T(8,128)}, f32[4,144,128]{2,1,0:T(8,128)S(1)}, u32[]{:S(2)}) copy-start(f32[4,144,128]{2,1,0:T(8,128)S(1)} %collective-permute-done.refs_2_) | copy-start | bytes 884740
  49.5 0.9 %copy-start.2 = (f32[4,144,128]{2,1,0:T(8,128)}, f32[4,144,128]{2,1,0:T(8,128)S(1)}, u32[]{:S(2)}) copy-start(f32[4,144,128]{2,1,0:T(8,128)S(1)} %collective-permute-done.1.refs_3_) | copy-start | bytes 884740
  49.5 1.0 %copy-start.3 = (f32[4,144,128]{2,1,0:T(8,128)}, f32[4,144,128]{2,1,0:T(8,128)S(1)}, u32[]{:S(2)}) copy-start(f32[4,144,128]{2,1,0:T(8,128)S(1)} %collective-permute-done.2.refs_4_) | copy-start | bytes 884740
  49.5 1.1 %copy-start = (f32[64,1,2176]{2,1,0:T(1,128)}, f32[64,1,2176]{2,1,0:T(1,128)S(1)}, u32[]{:S(2)}) copy-start(f32[64,1,2176]{2,1,0:T(1,128)S(1)} %all-to-all-done) | copy-start | bytes 1671172

commit v2 on v0

v2 whole, which is shorter than its diff:
```python
import functools

import jax
import jax.numpy as jnp
from jax import lax
from jax.experimental import pallas as pl
from jax.experimental.pallas import tpu as pltpu
from jax.sharding import PartitionSpec as P

BLOCKS = 4
ITEMS = 4
LANES = 128
TILE = 8
WIN = 32
HALO = 4
CORE_ROWS = 128
ROWS = CORE_ROWS + 2 * TILE
GUARD = TILE
CHUNK = 72
SPAN = 9

phase_depth = 2.0
fd_coef = 0.03

F32 = jnp.float32


def lanes_of(rows):
    return lax.broadcasted_iota(jnp.int32, (rows, LANES), 1)


def lane_roll(x, shift):
    return pltpu.roll(x, shift % LANES, 1)


def pack_speed(vel_ref, out_ref, held, sem):
    core = lax.axis_index("freq") & 1
    copy = pltpu.make_async_copy(vel_ref.at[core], held, sem)
    copy.start()
    strips = vel_ref.shape[2] // LANES
    group = 16
    dims = (group, TILE, LANES)
    lane = lax.broadcasted_iota(jnp.int32, dims, 2)
    sublane = lax.broadcasted_iota(jnp.int32, dims, 1)
    copy.wait()

    def one_group(step, carry):
        def strip_of(i):
            strip = jnp.clip(step * group + i, 0, strips - 1)
            return held[:, pl.ds(pl.multiple_of(strip * LANES, LANES), LANES)]

        span = [strip_of(i) for i in range(-1, group + 1)]
        left = pltpu.roll(jnp.stack(span[:group]), 2 * HALO, 2)
        beside = jnp.where(lane < HALO, jnp.stack(span[2:]), left)
        beside = jnp.where(lane < 2 * HALO, beside, 0.0)
        for shift in (16, 32, 64):
            beside = beside + pltpu.roll(beside, shift, 2)
        beside = jnp.where((lane >> 4) == 7 - sublane, beside, 0.0)
        beside = jnp.sum(beside, axis=1, keepdims=True)
        out = out_ref.at[pl.ds(pl.multiple_of(step * group * SPAN, TILE), group * SPAN)]
        for i in range(group):
            out[SPAN * i : SPAN * i + TILE, :] = span[i + 1]
            out[SPAN * i + TILE : SPAN * (i + 1), :] = beside[i]
        return carry

    lax.fori_loop(0, strips // group, one_group, 0)


def first_row(block, rows):
    start = jnp.clip(block * CORE_ROWS - TILE, 0, rows - ROWS)
    return pl.multiple_of(start, TILE)


def cut_waves(src_ref, rec_ref, edges_ref, message_ref):
    other = 1 - (lax.axis_index("freq") & 1)
    fields = (src_ref.at[0, 0], src_ref.at[1, 0], rec_ref.at[0, 0], rec_ref.at[1, 0])
    lane = lanes_of(CORE_ROWS)
    packed = jnp.zeros((CORE_ROWS, LANES), F32)
    for group in range(BLOCKS):
        for part, field in enumerate(fields):
            slot = 4 * group + part
            value = field[group * CORE_ROWS : (group + 1) * CORE_ROWS, :]
            packed = jnp.where((lane >> 3) == slot, lane_roll(value, 8 * slot + 4), packed)
    edges_ref[...] = jnp.where((lane & 7) < 4, lane_roll(packed, -4), lane_roll(packed, 4))
    for b in range(2):
        rows = pl.ds(first_row(2 * b + other, src_ref.shape[2]), ROWS)
        for part, field in enumerate(fields):
            message_ref[4 * b + part] = field[rows, :]


SIN_TERMS = (1.0, -0.166666641831398, 0.008333218283951283, -0.00019823516777250916, 2.643730113049969e-06)
COS_TERMS = (1.0, -0.5, 0.041666656732559204, -0.0013888673856854439, 2.4778757506283e-05, -2.6437069777784927e-07)


def horner(terms, x):
    value = terms[-1]
    for term in terms[-2::-1]:
        value = value * x + term
    return value


def sin_cos(x):
    t = 0.5 * x - 0.7853981633974483
    square = t * t
    sine = t * horner(SIN_TERMS, square)
    cosine = horner(COS_TERMS, square)
    twice = -2.0 * sine
    return 1.0 + twice * sine, twice * cosine


def march(*refs):
    speed_refs, src_ref, rec_ref, message_ref, halo_refs = refs[:2], *refs[2:5], refs[5:7]
    own_ref, send_ref = refs[7:9]
    waves, sides, stage, speed, coef, omega, first, second, images, sems = refs[9:]
    freq = lax.axis_index("freq")
    core = freq & 1
    strip = lax.axis_index("strip")
    strips = lax.axis_size("strip")
    copies = []

    def copy_in(source, target):
        copy = pltpu.make_async_copy(source, target, sems.at[len(copies)])
        copy.start()
        copies.append(copy)

    block_rows = SPAN * (CORE_ROWS // TILE)
    for b in range(2):
        mid = pl.multiple_of((2 * b + core) * block_rows, TILE)
        above = pl.multiple_of(jnp.maximum(mid - 16, 0), TILE)
        below = pl.multiple_of(jnp.minimum(mid + block_rows, strips * SPAN - 16), TILE)
        for which, speed_ref in enumerate(speed_refs):
            target = stage.at[core ^ which, b]
            copy_in(speed_ref.at[pl.ds(above, 16)], target.at[0:16])
            copy_in(speed_ref.at[pl.ds(mid, block_rows)], target.at[16 : 16 + block_rows])
            copy_in(speed_ref.at[pl.ds(below, 16)], target.at[16 + block_rows :])
    speed_count = len(copies)
    for b in range(2):
        block = 2 * b + core
        start = first_row(block, src_ref.shape[2])
        landing = pl.ds(pl.multiple_of(start - block * CORE_ROWS + GUARD + TILE, TILE), ROWS)
        rows = pl.ds(start, ROWS)
        copy_in(src_ref.at[:, 0, rows, :], waves.at[2 * b, 0:2, landing, :])
        copy_in(rec_ref.at[:, 0, rows, :], waves.at[2 * b, 2:4, landing, :])
        copy_in(message_ref.at[4 * b : 4 * b + 4], waves.at[2 * b + 1, :, landing, :])
    for k in range(2):
        copy_in(halo_refs[k], sides.at[k])

    guard = jnp.zeros((TILE, LANES), F32)
    for buffer in (first, second):
        for part in range(4):
            buffer[part, 0:GUARD, :] = guard
            buffer[part, GUARD + ROWS :, :] = guard
    images[...] = jnp.zeros_like(images)

    for copy in copies[:speed_count]:
        copy.wait()
    tiles = ROWS // TILE
    dims = (tiles, TILE, LANES)
    lane = lax.broadcasted_iota(jnp.int32, dims, 2)
    place = lane & (WIN - 1)
    tile = lax.broadcasted_iota(jnp.int32, dims, 0)
    on_grid = jnp.logical_not(
        ((place < 4) & (strip == 0)) | ((place >= 28) & (strip == strips - 1))
    )
    upper = (((lane + 112) >> 6) & 1) == 1
    for depth in range(2):
        windows = []
        for b in range(2):
            block = 2 * b + core
            live = jnp.logical_not(
                ((tile == 0) & (block == 0)) | ((tile == tiles - 1) & (block == BLOCKS - 1))
            )
            here = jnp.stack(
                [stage[depth, b, 7 + SPAN * i : 15 + SPAN * i, :] for i in range(tiles)]
            )
            beside = jnp.stack(
                [
                    jnp.broadcast_to(
                        stage[depth, b, 15 + SPAN * i : 16 + SPAN * i, :], (TILE, LANES)
                    )
                    for i in range(tiles)
                ]
            )
            beside = pltpu.roll(beside, 0, 2, stride=16, stride_axis=1)
            window = jnp.where((lane >= 28) & (lane < 36), pltpu.roll(beside, 44, 2), 0.0)
            window = jnp.where((lane >= 4) & (lane < 16), pltpu.roll(here, 4, 2), window)
            window = jnp.where((lane >= 16) & (lane < 28), pltpu.roll(here, 28, 2), window)
            window = window + pltpu.roll(window, WIN, 2)
            window = window + pltpu.roll(window, 2 * WIN, 2)
            windows.append((window, jnp.where(live, window, 0.0)))
            speed[b, depth] = (phase_depth / here).reshape(ROWS, LANES)
            coef[b, depth] = jnp.where(live, fd_coef * here, 0.0).reshape(ROWS, LANES)
        window = jnp.where(upper, windows[1][0], windows[0][0])
        speed[2, depth] = (phase_depth / window).reshape(ROWS, LANES)
        window = jnp.where(upper, windows[1][1], windows[0][1])
        coef[2, depth] = jnp.where(on_grid, fd_coef * window, 0.0).reshape(ROWS, LANES)

    for copy in copies[speed_count:]:
        copy.wait()

    @pl.when(core == 0)
    def _():
        for m in range(2):
            for part in range(4):
                waves[m, part, GUARD : GUARD + TILE, :] = guard

    @pl.when(core == 1)
    def _():
        for m in range(2, 4):
            for part in range(4):
                waves[m, part, GUARD + ROWS - TILE : GUARD + ROWS, :] = guard

    def turned(k, low, high, shift):
        return pltpu.roll(sides[k, low:high, :], (WIN * (shift - core)) & (LANES - 1), 1)

    def pick(low, high, shift):
        odd = ((lanes_of(high - low) >> 5) & 1) == 1
        return jnp.where(odd, turned(1, low, high, shift + 1), turned(0, low, high, shift))

    tile_lane = lanes_of(TILE)
    above = pick(CORE_ROWS - TILE, CORE_ROWS, 1)
    above = jnp.where((tile_lane < 2 * WIN) & (core == 0), 0.0, above)
    below = pick(0, TILE, LANES // WIN - 1)
    below = jnp.where((tile_lane >= 2 * WIN) & (core == 1), 0.0, below)
    beside = jnp.concatenate([above, pick(0, CORE_ROWS, 0), below])
    lane = lanes_of(ROWS)
    place = lane & (WIN - 1)
    for part in range(4):
        own = waves[0, part, GUARD : GUARD + ROWS, :]
        for m in range(1, ITEMS):
            value = lane_roll(waves[m, part, GUARD : GUARD + ROWS, :], WIN * m)
            own = jnp.where((((lane + 16) >> 5) & 3) == m, value, own)
        window = lane_roll(beside, 28 - 8 * part)
        window = jnp.where((place >= 4) & (place < 16), lane_roll(own, 36), window)
        window = jnp.where((place >= 16) & (place < 28), lane_roll(own, 28), window)
        waves[ITEMS, part, GUARD : GUARD + ROWS, :] = window
    rows = [sides[k, CORE_ROWS : CORE_ROWS + TILE, :] for k in range(2)]
    odd = (((tile_lane + 112) >> 5) & 1) == 1
    for m in range(ITEMS):
        omega[m * TILE : (m + 1) * TILE, :] = rows[m & 1]
    omega[ITEMS * TILE :, :] = jnp.where(odd, rows[1], rows[0])

    chunks = ROWS // CHUNK

    def turn(values, depth, kind, row, freq_row):
        theta = freq_row * speed[kind, depth, pl.ds(row, CHUNK), :]
        sine, cosine = sin_cos(theta)
        src_re, src_im, rec_re, rec_im = values
        return (
            src_re * cosine - src_im * sine,
            src_re * sine + src_im * cosine,
            rec_re * cosine + rec_im * sine,
            rec_im * cosine - rec_re * sine,
        )

    def substep(buffer, depth, kind, row, freq_inverse):
        step = coef[kind, depth, pl.ds(row, CHUNK), :] * freq_inverse
        centers = []
        laps = []
        for part in range(4):
            center = buffer[part, pl.ds(row + GUARD, CHUNK), :]
            up = buffer[part, pl.ds(row + GUARD - 1, CHUNK), :]
            down = buffer[part, pl.ds(row + GUARD + 1, CHUNK), :]
            across = lane_roll(center, 1) + lane_roll(center, LANES - 1)
            centers.append(center)
            laps.append((across + (up + down)) - 4.0 * center)
        src_re, src_im, rec_re, rec_im = centers
        return (
            src_re - step * laps[1],
            src_im + step * laps[0],
            rec_re + step * laps[3],
            rec_im - step * laps[2],
        )

    def store(buffer, row, values):
        for part in range(4):
            buffer[part, pl.ds(row + GUARD, CHUNK), :] = values[part]

    def product(values):
        return values[0] * values[2] + values[1] * values[3]

    def add_image(kind, depth, row, value):
        low, high = max(row, TILE), min(row + CHUNK, TILE + CORE_ROWS)
        if low < high:
            images[kind, depth, low - TILE : high - TILE, :] += value[low - row : high - row, :]

    def item(k, carry):
        kind = k >> 1
        freq_row = omega[pl.ds(pl.multiple_of(k * TILE, TILE), 1), :]
        freq_inverse = 1.0 / freq_row

        for j in range(chunks):
            row = j * CHUNK
            values = [waves[k, part, pl.ds(row + GUARD, CHUNK), :] for part in range(4)]
            store(first, row, turn(values, 0, kind, row, freq_row))
        for j in range(chunks):
            store(second, j * CHUNK, substep(first, 0, kind, j * CHUNK, freq_inverse))
        for j in range(chunks):
            row = j * CHUNK
            values = substep(second, 0, kind, row, freq_inverse)
            add_image(kind, 0, row, product(values))
            store(first, row, turn(values, 1, kind, row, freq_row))
        for j in range(chunks):
            store(second, j * CHUNK, substep(first, 1, kind, j * CHUNK, freq_inverse))
        for j in range(chunks):
            values = substep(second, 1, kind, j * CHUNK, freq_inverse)
            add_image(kind, 1, j * CHUNK, product(values))
        return carry

    lax.fori_loop(0, ITEMS + 1, item, 0)
    lane = lanes_of(CORE_ROWS)
    mine = freq >> 1
    for depth in range(2):
        value = images[2, depth]
        value = value + lane_roll(value, -WIN)
        finished = []
        for b in range(2):
            image = jnp.where(lane < HALO, lane_roll(value, -64 * b - 36), images[b, depth])
            image = jnp.where(lane >= LANES - HALO, lane_roll(value, 100 - 64 * b), image)
            finished.append(image)
        own_ref[depth] = jnp.where(mine == 0, finished[0], finished[1])
        send_ref[depth] = jnp.where(mine == 0, finished[1], finished[0])


def shape(*dims):
    return jax.ShapeDtypeStruct(dims, F32)


def shards(source, receiver, velocity, omega):
    strips = lax.axis_size("strip")
    freqs = lax.axis_size("freq")
    vmem = pl.BlockSpec(memory_space=pltpu.VMEM)
    anywhere = pl.BlockSpec(memory_space=pl.ANY)

    def across(x, k):
        return lax.ppermute(x, "freq", [(i, i ^ k) for i in range(freqs)])

    packed = pl.pallas_call(
        pack_speed,
        out_shape=shape(SPAN * strips, LANES),
        in_specs=[anywhere],
        out_specs=vmem,
        scratch_shapes=[
            pltpu.VMEM((TILE, strips * LANES), F32),
            pltpu.SemaphoreType.DMA,
        ],
    )(velocity)
    speeds = lax.all_to_all(
        packed.reshape(strips, 1, SPAN * LANES), "strip", split_axis=0, concat_axis=0, tiled=True
    ).reshape(SPAN * strips, LANES)
    other_speeds = across(speeds, 1)

    edges, message = pl.pallas_call(
        cut_waves,
        out_shape=[shape(CORE_ROWS, LANES), shape(8, ROWS, LANES)],
        in_specs=[vmem, vmem],
        out_specs=[vmem, vmem],
    )(source, receiver)
    from_left = lax.ppermute(edges, "strip", [(i, i + 1) for i in range(strips - 1)])
    from_right = lax.ppermute(edges, "strip", [(i + 1, i) for i in range(strips - 1)])
    message = across(message, 1)
    first_half = (lanes_of(CORE_ROWS) & 7) < 4
    halos = jnp.concatenate(
        [
            jnp.where(first_half, from_right, from_left),
            jnp.broadcast_to(omega[:, None], (TILE, LANES)),
        ]
    )

    own, send = pl.pallas_call(
        march,
        out_shape=[shape(2, CORE_ROWS, LANES)] * 2,
        in_specs=[anywhere] * 7,
        out_specs=[vmem] * 2,
        scratch_shapes=[
            pltpu.VMEM((ITEMS + 1, 4, ROWS + 2 * GUARD, LANES), F32),
            pltpu.VMEM((2, CORE_ROWS + TILE, LANES), F32),
            pltpu.VMEM((2, 2, 32 + SPAN * CORE_ROWS // TILE, LANES), F32),
            pltpu.VMEM((3, 2, ROWS, LANES), F32),
            pltpu.VMEM((3, 2, ROWS, LANES), F32),
            pltpu.VMEM(((ITEMS + 1) * TILE, LANES), F32),
            pltpu.VMEM((4, ROWS + 2 * GUARD, LANES), F32),
            pltpu.VMEM((4, ROWS + 2 * GUARD, LANES), F32),
            pltpu.VMEM((3, 2, CORE_ROWS, LANES), F32),
            pltpu.SemaphoreType.DMA((20,)),
        ],
        compiler_params=pltpu.CompilerParams(vmem_limit_bytes=16 * 1024 * 1024),
    )(speeds, other_speeds, source, receiver, message, halos, across(halos, 1))
    return own + across(send, 2)


def solution(mesh):
    return jax.shard_map(
        shards,
        mesh=mesh,
        in_specs=(
            P(None, "freq", None, "strip"),
            P(None, "freq", None, "strip"),
            P(None, "strip", None),
            P("freq"),
        ),
        out_specs=P(None, "freq", "strip"),
        check_vma=False,
    )
```

time: 191 us -> 52.5 us (0.27)
  the two profiles are of different devices: /device:TPU:1 before, /device:TPU:2 now
where the time goes in v2:
time: 52.5 us; the launch traced here: 52.3 us
  starting transfers between devices  24.1 us (46%)
  waiting for transfers between devices  14.2 us (27%)
  Pallas kernels  12.5 us (24%)
  between operations  0.75 us (1%)
  other arithmetic  0.69 us (1%)
    all_to_all x1, starting transfers between devices, shards(): lax.all_to_all(packed.reshape(strips, 1, SPAN * LANES), 'strip', split_ax...  13.2 us
    ppermute x1, waiting for transfers between devices, shards(): lax.ppermute(edges, 'strip', [(i, i + 1) for i in range(strips - 1)])  7.18 us
    pallas_call x1, Pallas kernels, shards(): pl.pallas_call(march, out_shape=[shape(2, CORE_ROWS, LANES)] * 2, in_spec...  7.06 us
    ppermute x1, starting transfers between devices, shards(): lax.ppermute(edges, 'strip', [(i + 1, i) for i in range(strips - 1)])  6.67 us
    ppermute x4, waiting for transfers between devices, across(): return lax.ppermute(x, 'freq', [(i, i ^ k) for i in range(freqs)])  6.19 us
    pallas_call x1, Pallas kernels, shards(): pl.pallas_call(pack_speed, out_shape=shape(SPAN * strips, LANES), in_spec...  2.95 us
    pallas_call x1, Pallas kernels, shards(): pl.pallas_call(cut_waves, out_shape=[shape(CORE_ROWS, LANES), shape(8, RO...  2.48 us
    ppermute x4, starting transfers between devices, across(): return lax.ppermute(x, 'freq', [(i, i ^ k) for i in range(freqs)])  2.31 us
  transfers between devices with their start and end apart: 7, of which 4 were waited for; matrix products, arithmetic and copies ran while one was open for 0% of the time, Pallas kernels for 5%

profile of v2, /device:TPU:2, one launch (start us, length us, event | category | flops | bytes accessed | tf_op | source)
XLA Modules:
  0.0 52.3 jit_solution(2719686062498886588)
XLA Ops:
  0.0 3.0 %shard_map.46 = f32[576,128]{1,0:T(8,128)} custom-call(f32[2,8,8192]{2,1,0:T(8,128)} %vel_ref.1), custom_call_target="tpu_custom_call" | custom-call | tf_op jit(solution)/shard_map/pallas_call | solution.py:338
  3.0 13.2 %all-to-all-start = ((f32[64,1,1152]{2,1,0:T(1,128)}), f32[64,1,1152]{2,1,0:T(1,128)S(1)}, u32[]{:S(2)}, u32[]{:S(2)}) async-start(f32[64,1,1152]{2,1,0:T(1,128)} %bitcast.6), calls=%async_computation | async-start | bytes 589824 | tf_op jit(solution)/shard_map/all_to_all | solution.py:348
  16.2 0.0 copy-start
  16.2 0.0 copy-start.1
  16.2 2.5 %shard_map.47 = (f32[128,128]{1,0:T(8,128)}, f32[8,144,128]{2,1,0:T(8,128)}) custom-call(f32[2,1,512,128]{3,2,1,0:T(8,128)} %refs_2_.1, f32[2,1,512,128]{3,2,1,0:T(8,128)} %refs_3_.1), custom_call_target="tpu_custom_call" | custom-call | tf_op jit(solution)/shard_map/pallas_call | solution.py:353
  18.7 0.0 collective-permute-start.1
  18.7 6.7 %collective-permute-start.2 = (f32[128,128]{1,0:T(8,128)}, f32[128,128]{1,0:T(8,128)S(1)}, u32[]{:S(2)}, u32[]{:S(2)}) collective-permute-start(f32[128,128]{1,0:T(8,128)} %get-tuple-element.10), channel_id=1, source_target_pairs={{1,0},{2,1},{3,2},{4,3},{5,4},{6,5},{7,6},{8,7},{9,8},{10,9},{11,1... | collective-permute-start | bytes 196616 | tf_op jit(solution)/shard_map/ppermute | solution.py:360
  25.4 1.9 %collective-permute-start.3 = (f32[128,128]{1,0:T(8,128)}, f32[128,128]{1,0:T(8,128)S(1)}, u32[]{:S(2)}, u32[]{:S(2)}) collective-permute-start(f32[128,128]{1,0:T(8,128)} %get-tuple-element.10), channel_id=1, source_target_pairs={{0,1},{1,2},{2,3},{3,4},{4,5},{5,6},{6,7},{7,8},{8,9},{9,10},{10,1... | collective-permute-start | bytes 196616 | tf_op jit(solution)/shard_map/ppermute | solution.py:359
  28.0 0.8 %all-to-all-done = f32[64,1,1152]{2,1,0:T(1,128)S(1)} async-done(((f32[64,1,1152]{2,1,0:T(1,128)}), f32[64,1,1152]{2,1,0:T(1,128)S(1)}, u32[]{:S(2)}, u32[]{:S(2)}) %all-to-all-start) | async-done | bytes 294944 | tf_op jit(solution)/shard_map/all_to_all | solution.py:348
  28.8 0.0 collective-permute-start
  28.8 0.0 collective-permute-done.2
  28.8 7.2 %collective-permute-done.3 = f32[128,128]{1,0:T(8,128)S(1)} collective-permute-done((f32[128,128]{1,0:T(8,128)}, f32[128,128]{1,0:T(8,128)S(1)}, u32[]{:S(2)}, u32[]{:S(2)}) %collective-permute-start.3) | collective-permute-done | bytes 65568 | tf_op jit(solution)/shard_map/ppermute | solution.py:359
  36.0 0.1 collective-permute-start.4
  36.1 1.2 %collective-permute-done.4.refs_6_ = f32[136,128]{1,0:T(8,128)S(1)} collective-permute-done((f32[136,128]{1,0:T(8,128)S(1)}, f32[136,128]{1,0:T(8,128)S(1)}, u32[]{:S(2)}, u32[]{:S(2)}) %collective-permute-start.4) | collective-permute-done | bytes 69664 | tf_op jit(solution)/shard_map/ppermute | solution.py:336
  37.3 0.0 collective-permute-done.1.refs_4_
  37.4 0.0 collective-permute-done.refs_1_
  37.4 0.0 copy-done
  37.4 0.0 copy-done.1
  37.4 7.1 %shard_map.48 = (f32[2,128,128]{2,1,0:T(8,128)S(1)}, f32[2,128,128]{2,1,0:T(8,128)S(1)}) custom-call(f32[576,128]{1,0:T(8,128)S(1)} %bitcast.5, f32[576,128]{1,0:T(8,128)S(1)} %collective-permute-done.refs_1_, f32[2,1,512,128]{3,2,1,0:T(8,128)S(1)} %copy-done, f32[2,1,512,128]{3,2,1,0:T(8,128)S(1)} %copy-done.1, ...), custom_call_target="tpu_custom_call" | custom-call | tf_op jit(solution)/shard_map/pallas_call | solution.py:370
  44.4 2.2 %collective-permute-start.5 = (f32[2,128,128]{2,1,0:T(8,128)S(1)}, f32[2,128,128]{2,1,0:T(8,128)S(1)}, u32[]{:S(2)}, u32[]{:S(2)}) collective-permute-start(f32[2,128,128]{2,1,0:T(8,128)S(1)} %get-tuple-element.12), channel_id=1, source_target_pairs={{0,128},{64,192},{128,0},{192,64},{1,129},{65,193},{129,1},{193,65... | collective-permute-start | bytes 393224 | tf_op jit(solution)/shard_map/ppermute | solution.py:336
  46.7 4.9 %collective-permute-done.5 = f32[2,128,128]{2,1,0:T(8,128)S(1)} collective-permute-done((f32[2,128,128]{2,1,0:T(8,128)S(1)}, f32[2,128,128]{2,1,0:T(8,128)S(1)}, u32[]{:S(2)}, u32[]{:S(2)}) %collective-permute-start.5) | collective-permute-done | bytes 131104 | tf_op jit(solution)/shard_map/ppermute | solution.py:336
  51.6 0.7 %add.5 = f32[2,128,128]{2,1,0:T(8,128)} add(f32[2,128,128]{2,1,0:T(8,128)S(1)} %get-tuple-element.11, f32[2,128,128]{2,1,0:T(8,128)S(1)} %collective-permute-done.5) | non-fusion elementwise | flops 32768 | bytes 393216 | tf_op jit(solution)/shard_map/add | solution.py:389
  (3 shorter events, 0.0 us)
Async XLA Ops:
  3.0 25.8 %all-to-all-start = ((f32[64,1,1152]{2,1,0:T(1,128)}), f32[64,1,1152]{2,1,0:T(1,128)S(1)}, u32[]{:S(2)}, u32[]{:S(2)}) async-start(f32[64,1,1152]{2,1,0:T(1,128)} %bitcast.6), calls=%async_computation | async-start | bytes 589824 | tf_op jit(solution)/shard_map/all_to_all | solution.py:348
  16.2 21.2 %copy-start = (f32[2,1,512,128]{3,2,1,0:T(8,128)S(1)}, f32[2,1,512,128]{3,2,1,0:T(8,128)}, u32[]{:S(2)}) copy-start(f32[2,1,512,128]{3,2,1,0:T(8,128)} %refs_2_.1) | copy-start | bytes 1572868
  16.2 21.2 %copy-start.1 = (f32[2,1,512,128]{3,2,1,0:T(8,128)S(1)}, f32[2,1,512,128]{3,2,1,0:T(8,128)}, u32[]{:S(2)}) copy-start(f32[2,1,512,128]{3,2,1,0:T(8,128)} %refs_3_.1) | copy-start | bytes 1572868
  18.7 18.7 %collective-permute-start.1 = (f32[8,144,128]{2,1,0:T(8,128)}, f32[8,144,128]{2,1,0:T(8,128)S(1)}, u32[]{:S(2)}, u32[]{:S(2)}) collective-permute-start(f32[8,144,128]{2,1,0:T(8,128)} %get-tuple-element.9), channel_id=1, source_target_pairs={{0,64},{64,0},{128,192},{192,128},{1,65},{65,1},{129,193},{193,129... | collective-permute-start | bytes 1769480 | tf_op jit(solution)/shard_map/ppermute | solution.py:336
  18.7 10.1 %collective-permute-start.2 = (f32[128,128]{1,0:T(8,128)}, f32[128,128]{1,0:T(8,128)S(1)}, u32[]{:S(2)}, u32[]{:S(2)}) collective-permute-start(f32[128,128]{1,0:T(8,128)} %get-tuple-element.10), channel_id=1, source_target_pairs={{1,0},{2,1},{3,2},{4,3},{5,4},{6,5},{7,6},{8,7},{9,8},{10,9},{11,1... | collective-permute-start | bytes 196616 | tf_op jit(solution)/shard_map/ppermute | solution.py:360
  25.4 10.6 %collective-permute-start.3 = (f32[128,128]{1,0:T(8,128)}, f32[128,128]{1,0:T(8,128)S(1)}, u32[]{:S(2)}, u32[]{:S(2)}) collective-permute-start(f32[128,128]{1,0:T(8,128)} %get-tuple-element.10), channel_id=1, source_target_pairs={{0,1},{1,2},{2,3},{3,4},{4,5},{5,6},{6,7},{7,8},{8,9},{9,10},{10,1... | collective-permute-start | bytes 196616 | tf_op jit(solution)/shard_map/ppermute | solution.py:359
  28.8 8.6 %collective-permute-start = (f32[576,128]{1,0:T(8,128)S(1)}, f32[576,128]{1,0:T(8,128)S(1)}, u32[]{:S(2)}, u32[]{:S(2)}) collective-permute-start(f32[576,128]{1,0:T(8,128)S(1)} %bitcast.4), channel_id=1, source_target_pairs={{0,64},{64,0},{128,192},{192,128},{1,65},{65,1},{129,193},{193,129... | collective-permute-start | bytes 884744 | tf_op jit(solution)/shard_map/ppermute | solution.py:336
  36.0 1.3 %collective-permute-start.4 = (f32[136,128]{1,0:T(8,128)S(1)}, f32[136,128]{1,0:T(8,128)S(1)}, u32[]{:S(2)}, u32[]{:S(2)}) collective-permute-start(f32[136,128]{1,0:T(8,128)S(1)} %concatenate.3.refs_5_), channel_id=1, source_target_pairs={{0,64},{64,0},{128,192},{192,128},{1,65},{65,1},{129,193},{193,129... | collective-permute-start | bytes 208904 | tf_op jit(solution)/shard_map/ppermute | solution.py:336
  44.4 7.2 %collective-permute-start.5 = (f32[2,128,128]{2,1,0:T(8,128)S(1)}, f32[2,128,128]{2,1,0:T(8,128)S(1)}, u32[]{:S(2)}, u32[]{:S(2)}) collective-permute-start(f32[2,128,128]{2,1,0:T(8,128)S(1)} %get-tuple-element.12), channel_id=1, source_target_pairs={{0,128},{64,192},{128,0},{192,64},{1,129},{65,193},{129,1},{193,65... | collective-permute-start | bytes 393224 | tf_op jit(solution)/shard_map/ppermute | solution.py:336

commit v3 on v2

--- a/solution.py
+++ b/solution.py
@@ -18,6 +18,7 @@
 GUARD = TILE
 CHUNK = 72
 SPAN = 9
+GROUPS = 4
 
 phase_depth = 2.0
 fd_coef = 0.03
@@ -33,23 +34,34 @@
     return pltpu.roll(x, shift % LANES, 1)
 
 
-def pack_speed(vel_ref, out_ref, held, sem):
+def pack_speed(vel_ref, out_ref, held, packed, sems):
     core = lax.axis_index("freq") & 1
-    copy = pltpu.make_async_copy(vel_ref.at[core], held, sem)
-    copy.start()
     strips = vel_ref.shape[2] // LANES
-    group = 16
+    group = strips // GROUPS
+    width = group * LANES
+    reads = []
+    for step in range(GROUPS):
+        columns = slice(step * width, (step + 1) * width)
+        reads.append(
+            pltpu.make_async_copy(
+                vel_ref.at[core, :, columns], held.at[:, columns], sems.at[0, step]
+            )
+        )
+        reads[step].start()
     dims = (group, TILE, LANES)
     lane = lax.broadcasted_iota(jnp.int32, dims, 2)
     sublane = lax.broadcasted_iota(jnp.int32, dims, 1)
-    copy.wait()
-
-    def one_group(step, carry):
-        def strip_of(i):
-            strip = jnp.clip(step * group + i, 0, strips - 1)
-            return held[:, pl.ds(pl.multiple_of(strip * LANES, LANES), LANES)]
-
-        span = [strip_of(i) for i in range(-1, group + 1)]
+
+    def strip_of(strip):
+        strip = min(max(strip, 0), strips - 1)
+        return held[:, strip * LANES : (strip + 1) * LANES]
+
+    writes = []
+    reads[0].wait()
+    for step in range(GROUPS):
+        if step + 1 < GROUPS:
+            reads[step + 1].wait()
+        span = [strip_of(step * group + i) for i in range(-1, group + 1)]
         left = pltpu.roll(jnp.stack(span[:group]), 2 * HALO, 2)
         beside = jnp.where(lane < HALO, jnp.stack(span[2:]), left)
         beside = jnp.where(lane < 2 * HALO, beside, 0.0)
@@ -57,13 +69,17 @@
             beside = beside + pltpu.roll(beside, shift, 2)
         beside = jnp.where((lane >> 4) == 7 - sublane, beside, 0.0)
         beside = jnp.sum(beside, axis=1, keepdims=True)
-        out = out_ref.at[pl.ds(pl.multiple_of(step * group * SPAN, TILE), group * SPAN)]
+        rows = slice(step * group * SPAN, (step + 1) * group * SPAN)
+        out = packed.at[rows]
         for i in range(group):
             out[SPAN * i : SPAN * i + TILE, :] = span[i + 1]
             out[SPAN * i + TILE : SPAN * (i + 1), :] = beside[i]
-        return carry
-
-    lax.fori_loop(0, strips // group, one_group, 0)
+        writes.append(
+            pltpu.make_async_copy(packed.at[rows], out_ref.at[rows], sems.at[1, step])
+        )
+        writes[step].start()
+    for write in writes:
+        write.wait()
 
 
 def first_row(block, rows):
@@ -162,9 +178,9 @@
     on_grid = jnp.logical_not(
         ((place < 4) & (strip == 0)) | ((place >= 28) & (strip == strips - 1))
     )
-    upper = (((lane + 112) >> 6) & 1) == 1
     for depth in range(2):
-        windows = []
+        window = jnp.zeros(dims, F32)
+        window_live = place < 0
         for b in range(2):
             block = 2 * b + core
             live = jnp.logical_not(
@@ -182,18 +198,28 @@
                 ]
             )
             beside = pltpu.roll(beside, 0, 2, stride=16, stride_axis=1)
-            window = jnp.where((lane >= 28) & (lane < 36), pltpu.roll(beside, 44, 2), 0.0)
-            window = jnp.where((lane >= 4) & (lane < 16), pltpu.roll(here, 4, 2), window)
-            window = jnp.where((lane >= 16) & (lane < 28), pltpu.roll(here, 28, 2), window)
-            window = window + pltpu.roll(window, WIN, 2)
-            window = window + pltpu.roll(window, 2 * WIN, 2)
-            windows.append((window, jnp.where(live, window, 0.0)))
+            base = 64 * b
+
+            def lanes_in(low, high):
+                return (lane >= base + low) & (lane < base + high)
+
+            window = jnp.where(
+                lanes_in(16, 28), pltpu.roll(here, (base + 28) % LANES, 2), window
+            )
+            window = jnp.where(
+                lanes_in(28, 36), pltpu.roll(beside, (base + 44) % LANES, 2), window
+            )
+            window = jnp.where(
+                lanes_in(36, 48), pltpu.roll(here, (base + 36) % LANES, 2), window
+            )
+            window_live = window_live | (live & ((((lane + 112) >> 6) & 1) == b))
             speed[b, depth] = (phase_depth / here).reshape(ROWS, LANES)
             coef[b, depth] = jnp.where(live, fd_coef * here, 0.0).reshape(ROWS, LANES)
-        window = jnp.where(upper, windows[1][0], windows[0][0])
+        window = window + pltpu.roll(window, WIN, 2)
         speed[2, depth] = (phase_depth / window).reshape(ROWS, LANES)
-        window = jnp.where(upper, windows[1][1], windows[0][1])
-        coef[2, depth] = jnp.where(on_grid, fd_coef * window, 0.0).reshape(ROWS, LANES)
+        coef[2, depth] = jnp.where(
+            on_grid & window_live, fd_coef * window, 0.0
+        ).reshape(ROWS, LANES)
 
     for copy in copies[speed_count:]:
         copy.wait()
@@ -339,10 +365,11 @@
         pack_speed,
         out_shape=shape(SPAN * strips, LANES),
         in_specs=[anywhere],
-        out_specs=vmem,
+        out_specs=anywhere,
         scratch_shapes=[
             pltpu.VMEM((TILE, strips * LANES), F32),
-            pltpu.SemaphoreType.DMA,
+            pltpu.VMEM((SPAN * strips, LANES), F32),
+            pltpu.SemaphoreType.DMA((2, GROUPS)),
         ],
     )(velocity)
     speeds = lax.all_to_all(
@@ -356,13 +383,17 @@
         in_specs=[vmem, vmem],
         out_specs=[vmem, vmem],
     )(source, receiver)
-    from_left = lax.ppermute(edges, "strip", [(i, i + 1) for i in range(strips - 1)])
-    from_right = lax.ppermute(edges, "strip", [(i + 1, i) for i in range(strips - 1)])
+    def swap(x, pairs):
+        return lax.ppermute(x, "strip", [p for i, j in pairs for p in ((i, j), (j, i))])
+
+    with_far = swap(edges, [(i, i + 1) for i in range(1, strips - 1, 2)])
+    with_near = swap(edges, [(i, i + 1) for i in range(0, strips, 2)])
     message = across(message, 1)
-    first_half = (lanes_of(CORE_ROWS) & 7) < 4
+    parity = lax.axis_index("strip") & 1
+    from_near = (((lanes_of(CORE_ROWS) >> 2) ^ parity) & 1) == 0
     halos = jnp.concatenate(
         [
-            jnp.where(first_half, from_right, from_left),
+            jnp.where(from_near, with_near, with_far),
             jnp.broadcast_to(omega[:, None], (TILE, LANES)),
         ]
     )

time: 52.5 us -> 46.5 us (0.89)
  the two profiles are of different devices: /device:TPU:2 before, /device:TPU:1 now
where the time goes in v3:
time: 46.5 us; the launch traced here: 46 us
  starting transfers between devices  22.7 us (49%)
  Pallas kernels  11.8 us (25%)
  waiting for transfers between devices  10.1 us (22%)
  between operations  0.74 us (2%)
  other arithmetic  0.69 us (1%)
    all_to_all x1, starting transfers between devices, shards(): lax.all_to_all(packed.reshape(strips, 1, SPAN * LANES), 'strip', split_ax...  13.6 us
    ppermute x4, starting transfers between devices, across(): return lax.ppermute(x, 'freq', [(i, i ^ k) for i in range(freqs)])  7.14 us
    pallas_call x1, Pallas kernels, shards(): pl.pallas_call(march, out_shape=[shape(2, CORE_ROWS, LANES)] * 2, in_spec...  6.78 us
    ppermute x4, waiting for transfers between devices, across(): return lax.ppermute(x, 'freq', [(i, i ^ k) for i in range(freqs)])  5.1 us
    all_to_all x1, waiting for transfers between devices, shards(): lax.all_to_all(packed.reshape(strips, 1, SPAN * LANES), 'strip', split_ax...  5.02 us
    pallas_call x1, Pallas kernels, shards(): pl.pallas_call(pack_speed, out_shape=shape(SPAN * strips, LANES), in_spec...  2.49 us
    pallas_call x1, Pallas kernels, shards(): pl.pallas_call(cut_waves, out_shape=[shape(CORE_ROWS, LANES), shape(8, RO...  2.48 us
    ppermute x2, starting transfers between devices, swap(): lax.ppermute(x, 'strip', [p for i, j in pairs for p in ((i, j), (j, i))])  1.94 us
  transfers between devices with their start and end apart: 7, of which 3 were waited for; matrix products, arithmetic and copies ran while one was open for 0% of the time, Pallas kernels for 5%

profile of v3, /device:TPU:1, one launch (start us, length us, event | category | flops | bytes accessed | tf_op | source)
XLA Modules:
  0.0 46.0 jit_solution(10271107728376697762)
XLA Ops:
  0.0 2.5 %shard_map.46 = f32[576,128]{1,0:T(8,128)} custom-call(f32[2,8,8192]{2,1,0:T(8,128)} %vel_ref.1), custom_call_target="tpu_custom_call" | custom-call | tf_op jit(solution)/shard_map/pallas_call | solution.py:364
  2.5 13.6 %all-to-all-start = ((f32[64,1,1152]{2,1,0:T(1,128)}), f32[64,1,1152]{2,1,0:T(1,128)S(1)}, u32[]{:S(2)}, u32[]{:S(2)}) async-start(f32[64,1,1152]{2,1,0:T(1,128)} %bitcast.6), calls=%async_computation | async-start | bytes 589824 | tf_op jit(solution)/shard_map/all_to_all | solution.py:375
  16.1 0.0 copy-start
  16.1 0.0 copy-start.1
  16.1 2.5 %shard_map.47 = (f32[128,128]{1,0:T(8,128)}, f32[8,144,128]{2,1,0:T(8,128)}) custom-call(f32[2,1,512,128]{3,2,1,0:T(8,128)} %refs_2_.1, f32[2,1,512,128]{3,2,1,0:T(8,128)} %refs_3_.1), custom_call_target="tpu_custom_call" | custom-call | tf_op jit(solution)/shard_map/pallas_call | solution.py:380
  18.6 1.0 %collective-permute-start.1 = (f32[8,144,128]{2,1,0:T(8,128)}, f32[8,144,128]{2,1,0:T(8,128)S(1)}, u32[]{:S(2)}, u32[]{:S(2)}) collective-permute-start(f32[8,144,128]{2,1,0:T(8,128)} %get-tuple-element.9), channel_id=1, source_target_pairs={{0,64},{64,0},{128,192},{192,128},{1,65},{65,1},{129,193},{193,129... | collective-permute-start | bytes 1769480 | tf_op jit(solution)/shard_map/ppermute | solution.py:362
  19.6 1.3 %collective-permute-start.2 = (f32[128,128]{1,0:T(8,128)}, f32[128,128]{1,0:T(8,128)S(1)}, u32[]{:S(2)}, u32[]{:S(2)}) collective-permute-start(f32[128,128]{1,0:T(8,128)} %get-tuple-element.10), channel_id=1, source_target_pairs={{0,1},{1,0},{2,3},{3,2},{4,5},{5,4},{6,7},{7,6},{8,9},{9,8},{10,11... | collective-permute-start | bytes 196616 | tf_op jit(solution)/shard_map/ppermute | solution.py:387
  20.9 0.7 %collective-permute-start.3 = (f32[128,128]{1,0:T(8,128)}, f32[128,128]{1,0:T(8,128)S(1)}, u32[]{:S(2)}, u32[]{:S(2)}) collective-permute-start(f32[128,128]{1,0:T(8,128)} %get-tuple-element.10), channel_id=1, source_target_pairs={{1,2},{2,1},{3,4},{4,3},{5,6},{6,5},{7,8},{8,7},{9,10},{10,9},{11,... | collective-permute-start | bytes 196616 | tf_op jit(solution)/shard_map/ppermute | solution.py:387
  22.2 5.0 %all-to-all-done = f32[64,1,1152]{2,1,0:T(1,128)S(1)} async-done(((f32[64,1,1152]{2,1,0:T(1,128)}), f32[64,1,1152]{2,1,0:T(1,128)S(1)}, u32[]{:S(2)}, u32[]{:S(2)}) %all-to-all-start) | async-done | bytes 294944 | tf_op jit(solution)/shard_map/all_to_all | solution.py:375
  27.2 3.6 %collective-permute-start = (f32[576,128]{1,0:T(8,128)S(1)}, f32[576,128]{1,0:T(8,128)S(1)}, u32[]{:S(2)}, u32[]{:S(2)}) collective-permute-start(f32[576,128]{1,0:T(8,128)S(1)} %bitcast.4), channel_id=1, source_target_pairs={{0,64},{64,0},{128,192},{192,128},{1,65},{65,1},{129,193},{193,129... | collective-permute-start | bytes 884744 | tf_op jit(solution)/shard_map/ppermute | solution.py:362
  30.8 0.0 collective-permute-done.2
  30.8 0.0 collective-permute-done.3
  30.8 0.1 collective-permute-start.4
  30.9 1.2 %collective-permute-done.4.refs_6_ = f32[136,128]{1,0:T(8,128)S(1)} collective-permute-done((f32[136,128]{1,0:T(8,128)S(1)}, f32[136,128]{1,0:T(8,128)S(1)}, u32[]{:S(2)}, u32[]{:S(2)}) %collective-permute-start.4) | collective-permute-done | bytes 69664 | tf_op jit(solution)/shard_map/ppermute | solution.py:362
  32.1 0.0 collective-permute-done.1.refs_4_
  32.2 0.0 collective-permute-done.refs_1_
  32.2 0.0 copy-done
  32.2 0.0 copy-done.1
  32.2 6.8 %shard_map.48 = (f32[2,128,128]{2,1,0:T(8,128)S(1)}, f32[2,128,128]{2,1,0:T(8,128)S(1)}) custom-call(f32[576,128]{1,0:T(8,128)S(1)} %bitcast.5, f32[576,128]{1,0:T(8,128)S(1)} %collective-permute-done.refs_1_, f32[2,1,512,128]{3,2,1,0:T(8,128)S(1)} %copy-done, f32[2,1,512,128]{3,2,1,0:T(8,128)S(1)} %copy-done.1, ...), custom_call_target="tpu_custom_call" | custom-call | tf_op jit(solution)/shard_map/pallas_call | solution.py:401
  39.0 2.5 %collective-permute-start.5 = (f32[2,128,128]{2,1,0:T(8,128)S(1)}, f32[2,128,128]{2,1,0:T(8,128)S(1)}, u32[]{:S(2)}, u32[]{:S(2)}) collective-permute-start(f32[2,128,128]{2,1,0:T(8,128)S(1)} %get-tuple-element.12), channel_id=1, source_target_pairs={{0,128},{64,192},{128,0},{192,64},{1,129},{65,193},{129,1},{193,65... | collective-permute-start | bytes 393224 | tf_op jit(solution)/shard_map/ppermute | solution.py:362
  41.5 3.8 %collective-permute-done.5 = f32[2,128,128]{2,1,0:T(8,128)S(1)} collective-permute-done((f32[2,128,128]{2,1,0:T(8,128)S(1)}, f32[2,128,128]{2,1,0:T(8,128)S(1)}, u32[]{:S(2)}, u32[]{:S(2)}) %collective-permute-start.5) | collective-permute-done | bytes 131104 | tf_op jit(solution)/shard_map/ppermute | solution.py:362
  45.3 0.7 %add.5 = f32[2,128,128]{2,1,0:T(8,128)} add(f32[2,128,128]{2,1,0:T(8,128)S(1)} %get-tuple-element.11, f32[2,128,128]{2,1,0:T(8,128)S(1)} %collective-permute-done.5) | non-fusion elementwise | flops 32768 | bytes 393216 | tf_op jit(solution)/shard_map/add | solution.py:420
  (3 shorter events, 0.0 us)
Async XLA Ops:
  2.5 24.7 %all-to-all-start = ((f32[64,1,1152]{2,1,0:T(1,128)}), f32[64,1,1152]{2,1,0:T(1,128)S(1)}, u32[]{:S(2)}, u32[]{:S(2)}) async-start(f32[64,1,1152]{2,1,0:T(1,128)} %bitcast.6), calls=%async_computation | async-start | bytes 589824 | tf_op jit(solution)/shard_map/all_to_all | solution.py:375
  16.1 16.1 %copy-start = (f32[2,1,512,128]{3,2,1,0:T(8,128)S(1)}, f32[2,1,512,128]{3,2,1,0:T(8,128)}, u32[]{:S(2)}) copy-start(f32[2,1,512,128]{3,2,1,0:T(8,128)} %refs_2_.1) | copy-start | bytes 1572868
  16.1 16.0 %copy-start.1 = (f32[2,1,512,128]{3,2,1,0:T(8,128)S(1)}, f32[2,1,512,128]{3,2,1,0:T(8,128)}, u32[]{:S(2)}) copy-start(f32[2,1,512,128]{3,2,1,0:T(8,128)} %refs_3_.1) | copy-start | bytes 1572868
  18.6 13.5 %collective-permute-start.1 = (f32[8,144,128]{2,1,0:T(8,128)}, f32[8,144,128]{2,1,0:T(8,128)S(1)}, u32[]{:S(2)}, u32[]{:S(2)}) collective-permute-start(f32[8,144,128]{2,1,0:T(8,128)} %get-tuple-element.9), channel_id=1, source_target_pairs={{0,64},{64,0},{128,192},{192,128},{1,65},{65,1},{129,193},{193,129... | collective-permute-start | bytes 1769480 | tf_op jit(solution)/shard_map/ppermute | solution.py:362
  19.6 11.2 %collective-permute-start.2 = (f32[128,128]{1,0:T(8,128)}, f32[128,128]{1,0:T(8,128)S(1)}, u32[]{:S(2)}, u32[]{:S(2)}) collective-permute-start(f32[128,128]{1,0:T(8,128)} %get-tuple-element.10), channel_id=1, source_target_pairs={{0,1},{1,0},{2,3},{3,2},{4,5},{5,4},{6,7},{7,6},{8,9},{9,8},{10,11... | collective-permute-start | bytes 196616 | tf_op jit(solution)/shard_map/ppermute | solution.py:387
  20.9 9.9 %collective-permute-start.3 = (f32[128,128]{1,0:T(8,128)}, f32[128,128]{1,0:T(8,128)S(1)}, u32[]{:S(2)}, u32[]{:S(2)}) collective-permute-start(f32[128,128]{1,0:T(8,128)} %get-tuple-element.10), channel_id=1, source_target_pairs={{1,2},{2,1},{3,4},{4,3},{5,6},{6,5},{7,8},{8,7},{9,10},{10,9},{11,... | collective-permute-start | bytes 196616 | tf_op jit(solution)/shard_map/ppermute | solution.py:387
  27.2 4.9 %collective-permute-start = (f32[576,128]{1,0:T(8,128)S(1)}, f32[576,128]{1,0:T(8,128)S(1)}, u32[]{:S(2)}, u32[]{:S(2)}) collective-permute-start(f32[576,128]{1,0:T(8,128)S(1)} %bitcast.4), channel_id=1, source_target_pairs={{0,64},{64,0},{128,192},{192,128},{1,65},{65,1},{129,193},{193,129... | collective-permute-start | bytes 884744 | tf_op jit(solution)/shard_map/ppermute | solution.py:362
  30.8 1.3 %collective-permute-start.4 = (f32[136,128]{1,0:T(8,128)S(1)}, f32[136,128]{1,0:T(8,128)S(1)}, u32[]{:S(2)}, u32[]{:S(2)}) collective-permute-start(f32[136,128]{1,0:T(8,128)S(1)} %concatenate.3.refs_5_), channel_id=1, source_target_pairs={{0,64},{64,0},{128,192},{192,128},{1,65},{65,1},{129,193},{193,129... | collective-permute-start | bytes 208904 | tf_op jit(solution)/shard_map/ppermute | solution.py:362
  39.0 6.4 %collective-permute-start.5 = (f32[2,128,128]{2,1,0:T(8,128)S(1)}, f32[2,128,128]{2,1,0:T(8,128)S(1)}, u32[]{:S(2)}, u32[]{:S(2)}) collective-permute-start(f32[2,128,128]{2,1,0:T(8,128)S(1)} %get-tuple-element.12), channel_id=1, source_target_pairs={{0,128},{64,192},{128,0},{192,64},{1,129},{65,193},{129,1},{193,65... | collective-permute-start | bytes 393224 | tf_op jit(solution)/shard_map/ppermute | solution.py:362

commit v4 on v3

--- a/solution.py
+++ b/solution.py
@@ -18,7 +18,7 @@
 GUARD = TILE
 CHUNK = 72
 SPAN = 9
-GROUPS = 4
+GROUPS = 2
 
 phase_depth = 2.0
 fd_coef = 0.03
@@ -87,8 +87,13 @@
     return pl.multiple_of(start, TILE)
 
 
-def cut_waves(src_ref, rec_ref, edges_ref, message_ref):
+def cut_waves(src_any, rec_any, edges_ref, message_ref, src_ref, rec_ref, sems):
+    copies, copy_in = copier(sems)
+    copy_in(src_any, src_ref)
+    copy_in(rec_any, rec_ref)
     other = 1 - (lax.axis_index("freq") & 1)
+    for copy in copies:
+        copy.wait()
     fields = (src_ref.at[0, 0], src_ref.at[1, 0], rec_ref.at[0, 0], rec_ref.at[1, 0])
     lane = lanes_of(CORE_ROWS)
     packed = jnp.zeros((CORE_ROWS, LANES), F32)
@@ -124,43 +129,8 @@
     return 1.0 + twice * sine, twice * cosine
 
 
-def march(*refs):
-    speed_refs, src_ref, rec_ref, message_ref, halo_refs = refs[:2], *refs[2:5], refs[5:7]
-    own_ref, send_ref = refs[7:9]
-    waves, sides, stage, speed, coef, omega, first, second, images, sems = refs[9:]
-    freq = lax.axis_index("freq")
-    core = freq & 1
-    strip = lax.axis_index("strip")
-    strips = lax.axis_size("strip")
-    copies = []
-
-    def copy_in(source, target):
-        copy = pltpu.make_async_copy(source, target, sems.at[len(copies)])
-        copy.start()
-        copies.append(copy)
-
-    block_rows = SPAN * (CORE_ROWS // TILE)
-    for b in range(2):
-        mid = pl.multiple_of((2 * b + core) * block_rows, TILE)
-        above = pl.multiple_of(jnp.maximum(mid - 16, 0), TILE)
-        below = pl.multiple_of(jnp.minimum(mid + block_rows, strips * SPAN - 16), TILE)
-        for which, speed_ref in enumerate(speed_refs):
-            target = stage.at[core ^ which, b]
-            copy_in(speed_ref.at[pl.ds(above, 16)], target.at[0:16])
-            copy_in(speed_ref.at[pl.ds(mid, block_rows)], target.at[16 : 16 + block_rows])
-            copy_in(speed_ref.at[pl.ds(below, 16)], target.at[16 + block_rows :])
-    speed_count = len(copies)
-    for b in range(2):
-        block = 2 * b + core
-        start = first_row(block, src_ref.shape[2])
-        landing = pl.ds(pl.multiple_of(start - block * CORE_ROWS + GUARD + TILE, TILE), ROWS)
-        rows = pl.ds(start, ROWS)
-        copy_in(src_ref.at[:, 0, rows, :], waves.at[2 * b, 0:2, landing, :])
-        copy_in(rec_ref.at[:, 0, rows, :], waves.at[2 * b, 2:4, landing, :])
-        copy_in(message_ref.at[4 * b : 4 * b + 4], waves.at[2 * b + 1, :, landing, :])
-    for k in range(2):
-        copy_in(halo_refs[k], sides.at[k])
-
+def stepper(waves, speed, coef, omega, first, second, images):
+    chunks = ROWS // CHUNK
     guard = jnp.zeros((TILE, LANES), F32)
     for buffer in (first, second):
         for part in range(4):
@@ -168,6 +138,148 @@
             buffer[part, GUARD + ROWS :, :] = guard
     images[...] = jnp.zeros_like(images)
 
+    def turn(values, depth, kind, row, freq_row):
+        theta = freq_row * speed[kind, depth, pl.ds(row, CHUNK), :]
+        sine, cosine = sin_cos(theta)
+        src_re, src_im, rec_re, rec_im = values
+        return (
+            src_re * cosine - src_im * sine,
+            src_re * sine + src_im * cosine,
+            rec_re * cosine + rec_im * sine,
+            rec_im * cosine - rec_re * sine,
+        )
+
+    def substep(buffer, depth, kind, row, freq_inverse):
+        step = coef[kind, depth, pl.ds(row, CHUNK), :] * freq_inverse
+        centers = []
+        laps = []
+        for part in range(4):
+            center = buffer[part, pl.ds(row + GUARD, CHUNK), :]
+            up = buffer[part, pl.ds(row + GUARD - 1, CHUNK), :]
+            down = buffer[part, pl.ds(row + GUARD + 1, CHUNK), :]
+            across = lane_roll(center, 1) + lane_roll(center, LANES - 1)
+            centers.append(center)
+            laps.append((across + (up + down)) - 4.0 * center)
+        src_re, src_im, rec_re, rec_im = centers
+        return (
+            src_re - step * laps[1],
+            src_im + step * laps[0],
+            rec_re + step * laps[3],
+            rec_im - step * laps[2],
+        )
+
+    def store(buffer, row, values):
+        for part in range(4):
+            buffer[part, pl.ds(row + GUARD, CHUNK), :] = values[part]
+
+    def product(values):
+        return values[0] * values[2] + values[1] * values[3]
+
+    def add_image(kind, depth, row, value):
+        low, high = max(row, TILE), min(row + CHUNK, TILE + CORE_ROWS)
+        if low < high:
+            images[kind, depth, low - TILE : high - TILE, :] += value[low - row : high - row, :]
+
+    def item(k, kind):
+        freq_row = omega[pl.ds(pl.multiple_of(k * TILE, TILE), 1), :]
+        freq_inverse = 1.0 / freq_row
+
+        for j in range(chunks):
+            row = j * CHUNK
+            values = [waves[k, part, pl.ds(row + GUARD, CHUNK), :] for part in range(4)]
+            store(first, row, turn(values, 0, kind, row, freq_row))
+        for j in range(chunks):
+            store(second, j * CHUNK, substep(first, 0, kind, j * CHUNK, freq_inverse))
+        for j in range(chunks):
+            row = j * CHUNK
+            values = substep(second, 0, kind, row, freq_inverse)
+            add_image(kind, 0, row, product(values))
+            store(first, row, turn(values, 1, kind, row, freq_row))
+        for j in range(chunks):
+            store(second, j * CHUNK, substep(first, 1, kind, j * CHUNK, freq_inverse))
+        for j in range(chunks):
+            values = substep(second, 1, kind, j * CHUNK, freq_inverse)
+            add_image(kind, 1, j * CHUNK, product(values))
+
+    return item
+
+
+def clear_above(waves, items):
+    for m in items:
+        for part in range(4):
+            waves[m, part, GUARD : GUARD + TILE, :] = jnp.zeros((TILE, LANES), F32)
+
+
+def clear_below(waves, items):
+    for m in items:
+        for part in range(4):
+            rows = slice(GUARD + ROWS - TILE, GUARD + ROWS)
+            waves[m, part, rows, :] = jnp.zeros((TILE, LANES), F32)
+
+
+def copier(sems):
+    copies = []
+
+    def copy_in(source, target):
+        copy = pltpu.make_async_copy(source, target, sems.at[len(copies)])
+        copy.start()
+        copies.append(copy)
+
+    return copies, copy_in
+
+
+def copy_speeds(copy_in, speed_refs, stage, block, core):
+    block_rows = SPAN * (CORE_ROWS // TILE)
+    mid = pl.multiple_of(block * block_rows, TILE)
+    above = pl.multiple_of(jnp.maximum(mid - 16, 0), TILE)
+    below = pl.multiple_of(jnp.minimum(mid + block_rows, speed_refs[0].shape[0] - 16), TILE)
+    for which, speed_ref in enumerate(speed_refs):
+        target = stage.at[core ^ which]
+        copy_in(speed_ref.at[pl.ds(above, 16)], target.at[0:16])
+        copy_in(speed_ref.at[pl.ds(mid, block_rows)], target.at[16 : 16 + block_rows])
+        copy_in(speed_ref.at[pl.ds(below, 16)], target.at[16 + block_rows :])
+
+
+def copy_waves(copy_in, src_ref, rec_ref, message_ref, waves, block, b, m):
+    start = first_row(block, src_ref.shape[2])
+    landing = pl.ds(pl.multiple_of(start - block * CORE_ROWS + GUARD + TILE, TILE), ROWS)
+    rows = pl.ds(start, ROWS)
+    copy_in(src_ref.at[:, 0, rows, :], waves.at[m, 0:2, landing, :])
+    copy_in(rec_ref.at[:, 0, rows, :], waves.at[m, 2:4, landing, :])
+    copy_in(message_ref.at[pl.ds(4 * b, 4)], waves.at[m + 1, :, landing, :])
+
+
+def tile_speeds(stage, depth):
+    tiles = ROWS // TILE
+    return jnp.stack([stage[depth, 7 + SPAN * i : 15 + SPAN * i, :] for i in range(tiles)])
+
+
+def patch(image, value, b):
+    lane = lanes_of(CORE_ROWS)
+    image = jnp.where(lane < HALO, pltpu.roll(value, (2 * LANES - 64 * b - 36) & 127, 1), image)
+    return jnp.where(
+        lane >= LANES - HALO, pltpu.roll(value, (LANES + 100 - 64 * b) & 127, 1), image
+    )
+
+
+def march_sent(*refs):
+    speed_refs, src_ref, rec_ref, message_ref, halo_refs = refs[:2], *refs[2:5], refs[5:7]
+    send_ref, sums_ref = refs[7:9]
+    waves, sides, stage, speed, coef, omega, first, second, images, sems = refs[9:]
+    freq = lax.axis_index("freq")
+    core = freq & 1
+    strip = lax.axis_index("strip")
+    strips = lax.axis_size("strip")
+    copies, copy_in = copier(sems)
+    for b in range(2):
+        copy_speeds(copy_in, speed_refs, stage.at[b], 2 * b + core, core)
+    speed_count = len(copies)
+    for b in range(2):
+        copy_waves(copy_in, src_ref, rec_ref, message_ref, waves, 2 * b + core, b, 2 * b)
+    for k in range(2):
+        copy_in(halo_refs[k], sides.at[k])
+
+    item = stepper(waves, speed, coef, omega, first, second, images)
     for copy in copies[:speed_count]:
         copy.wait()
     tiles = ROWS // TILE
@@ -186,13 +298,11 @@
             live = jnp.logical_not(
                 ((tile == 0) & (block == 0)) | ((tile == tiles - 1) & (block == BLOCKS - 1))
             )
-            here = jnp.stack(
-                [stage[depth, b, 7 + SPAN * i : 15 + SPAN * i, :] for i in range(tiles)]
-            )
+            here = tile_speeds(stage.at[b], depth)
             beside = jnp.stack(
                 [
                     jnp.broadcast_to(
-                        stage[depth, b, 15 + SPAN * i : 16 + SPAN * i, :], (TILE, LANES)
+                        stage[b, depth, 15 + SPAN * i : 16 + SPAN * i, :], (TILE, LANES)
                     )
                     for i in range(tiles)
                 ]
@@ -226,15 +336,11 @@
 
     @pl.when(core == 0)
     def _():
-        for m in range(2):
-            for part in range(4):
-                waves[m, part, GUARD : GUARD + TILE, :] = guard
+        clear_above(waves, range(2))
 
     @pl.when(core == 1)
     def _():
-        for m in range(2, 4):
-            for part in range(4):
-                waves[m, part, GUARD + ROWS - TILE : GUARD + ROWS, :] = guard
+        clear_below(waves, range(2, 4))
 
     def turned(k, low, high, shift):
         return pltpu.roll(sides[k, low:high, :], (WIN * (shift - core)) & (LANES - 1), 1)
@@ -266,86 +372,66 @@
         omega[m * TILE : (m + 1) * TILE, :] = rows[m & 1]
     omega[ITEMS * TILE :, :] = jnp.where(odd, rows[1], rows[0])
 
-    chunks = ROWS // CHUNK
-
-    def turn(values, depth, kind, row, freq_row):
-        theta = freq_row * speed[kind, depth, pl.ds(row, CHUNK), :]
-        sine, cosine = sin_cos(theta)
-        src_re, src_im, rec_re, rec_im = values
-        return (
-            src_re * cosine - src_im * sine,
-            src_re * sine + src_im * cosine,
-            rec_re * cosine + rec_im * sine,
-            rec_im * cosine - rec_re * sine,
-        )
-
-    def substep(buffer, depth, kind, row, freq_inverse):
-        step = coef[kind, depth, pl.ds(row, CHUNK), :] * freq_inverse
-        centers = []
-        laps = []
-        for part in range(4):
-            center = buffer[part, pl.ds(row + GUARD, CHUNK), :]
-            up = buffer[part, pl.ds(row + GUARD - 1, CHUNK), :]
-            down = buffer[part, pl.ds(row + GUARD + 1, CHUNK), :]
-            across = lane_roll(center, 1) + lane_roll(center, LANES - 1)
-            centers.append(center)
-            laps.append((across + (up + down)) - 4.0 * center)
-        src_re, src_im, rec_re, rec_im = centers
-        return (
-            src_re - step * laps[1],
-            src_im + step * laps[0],
-            rec_re + step * laps[3],
-            rec_im - step * laps[2],
-        )
-
-    def store(buffer, row, values):
-        for part in range(4):
-            buffer[part, pl.ds(row + GUARD, CHUNK), :] = values[part]
-
-    def product(values):
-        return values[0] * values[2] + values[1] * values[3]
-
-    def add_image(kind, depth, row, value):
-        low, high = max(row, TILE), min(row + CHUNK, TILE + CORE_ROWS)
-        if low < high:
-            images[kind, depth, low - TILE : high - TILE, :] += value[low - row : high - row, :]
-
-    def item(k, carry):
-        kind = k >> 1
-        freq_row = omega[pl.ds(pl.multiple_of(k * TILE, TILE), 1), :]
-        freq_inverse = 1.0 / freq_row
-
-        for j in range(chunks):
-            row = j * CHUNK
-            values = [waves[k, part, pl.ds(row + GUARD, CHUNK), :] for part in range(4)]
-            store(first, row, turn(values, 0, kind, row, freq_row))
-        for j in range(chunks):
-            store(second, j * CHUNK, substep(first, 0, kind, j * CHUNK, freq_inverse))
-        for j in range(chunks):
-            row = j * CHUNK
-            values = substep(second, 0, kind, row, freq_inverse)
-            add_image(kind, 0, row, product(values))
-            store(first, row, turn(values, 1, kind, row, freq_row))
-        for j in range(chunks):
-            store(second, j * CHUNK, substep(first, 1, kind, j * CHUNK, freq_inverse))
-        for j in range(chunks):
-            values = substep(second, 1, kind, j * CHUNK, freq_inverse)
-            add_image(kind, 1, j * CHUNK, product(values))
+    sent = 1 - (freq >> 1)
+
+    def step(j, carry):
+        k = jnp.where(j == 2, ITEMS, 2 * sent + j)
+        item(k, k >> 1)
         return carry
 
-    lax.fori_loop(0, ITEMS + 1, item, 0)
-    lane = lanes_of(CORE_ROWS)
-    mine = freq >> 1
+    lax.fori_loop(0, 3, step, 0)
     for depth in range(2):
         value = images[2, depth]
         value = value + lane_roll(value, -WIN)
-        finished = []
-        for b in range(2):
-            image = jnp.where(lane < HALO, lane_roll(value, -64 * b - 36), images[b, depth])
-            image = jnp.where(lane >= LANES - HALO, lane_roll(value, 100 - 64 * b), image)
-            finished.append(image)
-        own_ref[depth] = jnp.where(mine == 0, finished[0], finished[1])
-        send_ref[depth] = jnp.where(mine == 0, finished[1], finished[0])
+        sums_ref[depth] = value
+        send_ref[depth] = patch(images[sent, depth], value, sent)
+
+
+def march_kept(*refs):
+    speed_refs, src_ref, rec_ref, message_ref, halo_refs = refs[:2], *refs[2:5], refs[5:7]
+    sums_ref, image_ref = refs[7:9]
+    waves, stage, speed, coef, omega, first, second, images, sems = refs[9:]
+    freq = lax.axis_index("freq")
+    core = freq & 1
+    b = freq >> 1
+    copies, copy_in = copier(sems)
+    copy_speeds(copy_in, speed_refs, stage, freq, core)
+    copy_waves(copy_in, src_ref, rec_ref, message_ref, waves, freq, b, 0)
+    for k in range(2):
+        copy_in(
+            halo_refs[k].at[CORE_ROWS : CORE_ROWS + TILE], omega.at[k * TILE : (k + 1) * TILE]
+        )
+    item = stepper(waves, speed, coef, omega, first, second, images)
+    for copy in copies:
+        copy.wait()
+    tiles = ROWS // TILE
+    tile = lax.broadcasted_iota(jnp.int32, (tiles, TILE, LANES), 0)
+    live = jnp.logical_not(
+        ((tile == 0) & (freq == 0)) | ((tile == tiles - 1) & (freq == BLOCKS - 1))
+    )
+    for depth in range(2):
+        here = tile_speeds(stage, depth)
+        speed[0, depth] = (phase_depth / here).reshape(ROWS, LANES)
+        coef[0, depth] = jnp.where(live, fd_coef * here, 0.0).reshape(ROWS, LANES)
+
+    @pl.when(freq == 0)
+    def _():
+        clear_above(waves, range(2))
+
+    @pl.when(freq == BLOCKS - 1)
+    def _():
+        clear_below(waves, range(2))
+
+    def step(k, carry):
+        item(k, 0)
+        return carry
+
+    lax.fori_loop(0, 2, step, 0)
+    for depth in range(2):
+        image_ref[depth] = patch(images[0, depth], sums_ref[depth], b)
+
+
+SMALL = pltpu.CompilerParams(vmem_limit_bytes=16 * 1024 * 1024)
 
 
 def shape(*dims):
@@ -380,8 +466,10 @@
     edges, message = pl.pallas_call(
         cut_waves,
         out_shape=[shape(CORE_ROWS, LANES), shape(8, ROWS, LANES)],
-        in_specs=[vmem, vmem],
+        in_specs=[anywhere, anywhere],
         out_specs=[vmem, vmem],
+        scratch_shapes=[pltpu.VMEM(source.shape, F32)] * 2 + [pltpu.SemaphoreType.DMA((2,))],
+        compiler_params=SMALL,
     )(source, receiver)
     def swap(x, pairs):
         return lax.ppermute(x, "strip", [p for i, j in pairs for p in ((i, j), (j, i))])
@@ -398,26 +486,47 @@
         ]
     )
 
-    own, send = pl.pallas_call(
-        march,
+    inputs = (speeds, other_speeds, source, receiver, message, halos, across(halos, 1))
+
+    def scratch(items, kinds):
+        return [
+            pltpu.VMEM((kinds, 2, ROWS, LANES), F32),
+            pltpu.VMEM((kinds, 2, ROWS, LANES), F32),
+            pltpu.VMEM((items * TILE, LANES), F32),
+            pltpu.VMEM((4, ROWS + 2 * GUARD, LANES), F32),
+            pltpu.VMEM((4, ROWS + 2 * GUARD, LANES), F32),
+            pltpu.VMEM((kinds, 2, CORE_ROWS, LANES), F32),
+            pltpu.SemaphoreType.DMA((20,)),
+        ]
+
+    stage_rows = 32 + SPAN * CORE_ROWS // TILE
+    send, sums = pl.pallas_call(
+        march_sent,
         out_shape=[shape(2, CORE_ROWS, LANES)] * 2,
         in_specs=[anywhere] * 7,
         out_specs=[vmem] * 2,
         scratch_shapes=[
             pltpu.VMEM((ITEMS + 1, 4, ROWS + 2 * GUARD, LANES), F32),
             pltpu.VMEM((2, CORE_ROWS + TILE, LANES), F32),
-            pltpu.VMEM((2, 2, 32 + SPAN * CORE_ROWS // TILE, LANES), F32),
-            pltpu.VMEM((3, 2, ROWS, LANES), F32),
-            pltpu.VMEM((3, 2, ROWS, LANES), F32),
-            pltpu.VMEM(((ITEMS + 1) * TILE, LANES), F32),
-            pltpu.VMEM((4, ROWS + 2 * GUARD, LANES), F32),
-            pltpu.VMEM((4, ROWS + 2 * GUARD, LANES), F32),
-            pltpu.VMEM((3, 2, CORE_ROWS, LANES), F32),
-            pltpu.SemaphoreType.DMA((20,)),
-        ],
-        compiler_params=pltpu.CompilerParams(vmem_limit_bytes=16 * 1024 * 1024),
-    )(speeds, other_speeds, source, receiver, message, halos, across(halos, 1))
-    return own + across(send, 2)
+            pltpu.VMEM((2, 2, stage_rows, LANES), F32),
+        ]
+        + scratch(ITEMS + 1, 3),
+        compiler_params=SMALL,
+    )(*inputs)
+    received = across(send, 2)
+    kept = pl.pallas_call(
+        march_kept,
+        out_shape=shape(2, CORE_ROWS, LANES),
+        in_specs=[anywhere] * 7 + [vmem],
+        out_specs=vmem,
+        scratch_shapes=[
+            pltpu.VMEM((2, 4, ROWS + 2 * GUARD, LANES), F32),
+            pltpu.VMEM((2, stage_rows, LANES), F32),
+        ]
+        + scratch(2, 1),
+        compiler_params=SMALL,
+    )(*inputs, sums)
+    return kept + received
 
 
 def solution(mesh):

time: 46.5 us -> 44.2 us (0.951)
  Pallas kernels: 11.8 us -> 10.1 us
    ppermute x4, waiting for transfers between devices: 5.1 us -> 2.84 us  [across(): return lax.ppermute(x, 'freq', [(i, i ^ k) for i in range(freqs)])]
    pallas_call x1, Pallas kernels: 2.48 us -> 0.56 us  [shards(): pl.pallas_call(cut_waves, out_shape=[shape(CORE_ROWS, LANES), shape(8, RO...]
    all_to_all x1, waiting for transfers between devices: 5.02 us -> 6.84 us  [shards(): lax.all_to_all(packed.reshape(strips, 1, SPAN * LANES), 'strip', split_ax...]
    pallas_call x1 -> x2, Pallas kernels: 6.78 us -> 7.35 us  [the longest x1 5.1 us: shards(): pl.pallas_call(march_sent, out_shape=[shape(2, CORE_ROWS, LANES)] * 2, in...]
  transfers between devices with their start and end apart: 7 -> 7, of which waited for: 3 -> 3; matrix products, arithmetic and copies ran while one was open for 0% -> 0% of each run, Pallas kernels for 5% -> 6%
where the time goes in v4:
time: 44.2 us; the launch traced here: 44 us
  starting transfers between devices  22.8 us (52%)
  Pallas kernels  10.1 us (23%)
  waiting for transfers between devices  9.68 us (22%)
  between operations  0.74 us (2%)
  other arithmetic  0.69 us (2%)
    all_to_all x1, starting transfers between devices, shards(): lax.all_to_all(packed.reshape(strips, 1, SPAN * LANES), 'strip', split_ax...  13.6 us
    ppermute x4, starting transfers between devices, across(): return lax.ppermute(x, 'freq', [(i, i ^ k) for i in range(freqs)])  7.23 us
    all_to_all x1, waiting for transfers between devices, shards(): lax.all_to_all(packed.reshape(strips, 1, SPAN * LANES), 'strip', split_ax...  6.84 us
    pallas_call x1, Pallas kernels, shards(): pl.pallas_call(march_sent, out_shape=[shape(2, CORE_ROWS, LANES)] * 2, in...  5.1 us
    ppermute x4, waiting for transfers between devices, across(): return lax.ppermute(x, 'freq', [(i, i ^ k) for i in range(freqs)])  2.84 us
    pallas_call x1, Pallas kernels, shards(): pl.pallas_call(march_kept, out_shape=shape(2, CORE_ROWS, LANES), in_specs...  2.25 us
    pallas_call x1, Pallas kernels, shards(): pl.pallas_call(pack_speed, out_shape=shape(SPAN * strips, LANES), in_spec...  2.21 us
    ppermute x2, starting transfers between devices, swap(): lax.ppermute(x, 'strip', [p for i, j in pairs for p in ((i, j), (j, i))])  1.96 us
  transfers between devices with their start and end apart: 7, of which 3 were waited for; matrix products, arithmetic and copies ran while one was open for 0% of the time, Pallas kernels for 6%

profile of v4, /device:TPU:1, one launch (start us, length us, event | category | flops | bytes accessed | tf_op | source)
XLA Modules:
  0.0 44.0 jit_solution(2530181038725382096)
XLA Ops:
  0.0 0.0 copy-start
  0.0 0.0 copy-start.1
  0.0 2.2 %shard_map.46 = f32[576,128]{1,0:T(8,128)} custom-call(f32[2,8,8192]{2,1,0:T(8,128)} %vel_ref.1), custom_call_target="tpu_custom_call" | custom-call | tf_op jit(solution)/shard_map/pallas_call | solution.py:450
  2.2 13.6 %all-to-all-start = ((f32[64,1,1152]{2,1,0:T(1,128)}), f32[64,1,1152]{2,1,0:T(1,128)S(1)}, u32[]{:S(2)}, u32[]{:S(2)}) async-start(f32[64,1,1152]{2,1,0:T(1,128)} %bitcast.7), calls=%async_computation | async-start | bytes 589824 | tf_op jit(solution)/shard_map/all_to_all | solution.py:461
  15.8 0.0 copy-done
  15.8 0.0 copy-done.1
  15.8 0.6 %shard_map.47 = (f32[128,128]{1,0:T(8,128)S(1)}, f32[8,144,128]{2,1,0:T(8,128)S(1)}) custom-call(f32[2,1,512,128]{3,2,1,0:T(8,128)S(1)} %copy-done, f32[2,1,512,128]{3,2,1,0:T(8,128)S(1)} %copy-done.1), custom_call_target="tpu_custom_call" | custom-call | tf_op jit(solution)/shard_map/pallas_call | solution.py:466
  16.4 1.0 %collective-permute-start.1 = (f32[8,144,128]{2,1,0:T(8,128)S(1)}, f32[8,144,128]{2,1,0:T(8,128)S(1)}, u32[]{:S(2)}, u32[]{:S(2)}) collective-permute-start(f32[8,144,128]{2,1,0:T(8,128)S(1)} %get-tuple-element.9), channel_id=1, source_target_pairs={{0,64},{64,0},{128,192},{192,128},{1,65},{65,1},{129,193},{193,129... | collective-permute-start | bytes 1769480 | tf_op jit(solution)/shard_map/ppermute | solution.py:448
  17.5 1.3 %collective-permute-start.2 = (f32[128,128]{1,0:T(8,128)S(1)}, f32[128,128]{1,0:T(8,128)S(1)}, u32[]{:S(2)}, u32[]{:S(2)}) collective-permute-start(f32[128,128]{1,0:T(8,128)S(1)} %get-tuple-element.10), channel_id=1, source_target_pairs={{0,1},{1,0},{2,3},{3,2},{4,5},{5,4},{6,7},{7,6},{8,9},{9,8},{10,11... | collective-permute-start | bytes 196616 | tf_op jit(solution)/shard_map/ppermute | solution.py:475
  18.8 0.7 %collective-permute-start.3 = (f32[128,128]{1,0:T(8,128)S(1)}, f32[128,128]{1,0:T(8,128)S(1)}, u32[]{:S(2)}, u32[]{:S(2)}) collective-permute-start(f32[128,128]{1,0:T(8,128)S(1)} %get-tuple-element.10), channel_id=1, source_target_pairs={{1,2},{2,1},{3,4},{4,3},{5,6},{6,5},{7,8},{8,7},{9,10},{10,9},{11,... | collective-permute-start | bytes 196616 | tf_op jit(solution)/shard_map/ppermute | solution.py:475
  20.1 6.8 %all-to-all-done = f32[64,1,1152]{2,1,0:T(1,128)S(1)} async-done(((f32[64,1,1152]{2,1,0:T(1,128)}), f32[64,1,1152]{2,1,0:T(1,128)S(1)}, u32[]{:S(2)}, u32[]{:S(2)}) %all-to-all-start) | async-done | bytes 294944 | tf_op jit(solution)/shard_map/all_to_all | solution.py:461
  26.9 3.6 %collective-permute-start = (f32[576,128]{1,0:T(8,128)S(1)}, f32[576,128]{1,0:T(8,128)S(1)}, u32[]{:S(2)}, u32[]{:S(2)}) collective-permute-start(f32[576,128]{1,0:T(8,128)S(1)} %bitcast.4), channel_id=1, source_target_pairs={{0,64},{64,0},{128,192},{192,128},{1,65},{65,1},{129,193},{193,129... | collective-permute-start | bytes 884744 | tf_op jit(solution)/shard_map/ppermute | solution.py:448
  30.5 0.0 collective-permute-done.2
  30.5 0.0 collective-permute-done.3
  30.5 0.1 collective-permute-start.4
  30.6 1.2 %collective-permute-done.4.refs_6_ = f32[136,128]{1,0:T(8,128)S(1)} collective-permute-done((f32[136,128]{1,0:T(8,128)S(1)}, f32[136,128]{1,0:T(8,128)S(1)}, u32[]{:S(2)}, u32[]{:S(2)}) %collective-permute-start.4) | collective-permute-done | bytes 69664 | tf_op jit(solution)/shard_map/ppermute | solution.py:448
  31.9 0.0 collective-permute-done.1.refs_4_
  31.9 0.0 collective-permute-done.refs_1_
  31.9 5.1 %shard_map.48 = (f32[2,128,128]{2,1,0:T(8,128)S(1)}, f32[2,128,128]{2,1,0:T(8,128)S(1)}) custom-call(f32[576,128]{1,0:T(8,128)S(1)} %bitcast.5, f32[576,128]{1,0:T(8,128)S(1)} %collective-permute-done.refs_1_, f32[2,1,512,128]{3,2,1,0:T(8,128)S(1)} %copy-done, f32[2,1,512,128]{3,2,1,0:T(8,128)S(1)} %copy-done.1, ...), custom_call_target="tpu_custom_call" | custom-call | tf_op jit(solution)/shard_map/pallas_call | solution.py:503
  37.0 2.5 %collective-permute-start.5 = (f32[2,128,128]{2,1,0:T(8,128)S(1)}, f32[2,128,128]{2,1,0:T(8,128)S(1)}, u32[]{:S(2)}, u32[]{:S(2)}) collective-permute-start(f32[2,128,128]{2,1,0:T(8,128)S(1)} %get-tuple-element.12), channel_id=1, source_target_pairs={{0,128},{64,192},{128,0},{192,64},{1,129},{65,193},{129,1},{193,65... | collective-permute-start | bytes 393224 | tf_op jit(solution)/shard_map/ppermute | solution.py:448
  39.5 2.3 %shard_map.49 = f32[2,128,128]{2,1,0:T(8,128)S(1)} custom-call(f32[576,128]{1,0:T(8,128)S(1)} %bitcast.6, f32[576,128]{1,0:T(8,128)S(1)} %collective-permute-done.refs_1_, f32[2,1,512,128]{3,2,1,0:T(8,128)S(1)} %copy-done, f32[2,1,512,128]{3,2,1,0:T(8,128)S(1)} %copy-done.1, f32[8,144,128]{2,1,0:T(8,128)S(1)} %collective-permute-done.1.refs_4_, ...), custom_call_target="tpu_custom_call" | custom-call | tf_op jit(solution)/shard_map/pallas_call | solution.py:517
  41.8 1.6 %collective-permute-done.5 = f32[2,128,128]{2,1,0:T(8,128)S(1)} collective-permute-done((f32[2,128,128]{2,1,0:T(8,128)S(1)}, f32[2,128,128]{2,1,0:T(8,128)S(1)}, u32[]{:S(2)}, u32[]{:S(2)}) %collective-permute-start.5) | collective-permute-done | bytes 131104 | tf_op jit(solution)/shard_map/ppermute | solution.py:448
  43.4 0.7 %add.5 = f32[2,128,128]{2,1,0:T(8,128)} add(f32[2,128,128]{2,1,0:T(8,128)S(1)} %shard_map.49, f32[2,128,128]{2,1,0:T(8,128)S(1)} %collective-permute-done.5) | non-fusion elementwise | flops 32768 | bytes 393216 | tf_op jit(solution)/shard_map/add | solution.py:529
  (3 shorter events, 0.0 us)
Async XLA Ops:
  0.0 15.8 %copy-start = (f32[2,1,512,128]{3,2,1,0:T(8,128)S(1)}, f32[2,1,512,128]{3,2,1,0:T(8,128)}, u32[]{:S(2)}) copy-start(f32[2,1,512,128]{3,2,1,0:T(8,128)} %refs_2_.3) | copy-start | bytes 1572868
  0.0 15.8 %copy-start.1 = (f32[2,1,512,128]{3,2,1,0:T(8,128)S(1)}, f32[2,1,512,128]{3,2,1,0:T(8,128)}, u32[]{:S(2)}) copy-start(f32[2,1,512,128]{3,2,1,0:T(8,128)} %refs_3_.3) | copy-start | bytes 1572868
  2.2 24.7 %all-to-all-start = ((f32[64,1,1152]{2,1,0:T(1,128)}), f32[64,1,1152]{2,1,0:T(1,128)S(1)}, u32[]{:S(2)}, u32[]{:S(2)}) async-start(f32[64,1,1152]{2,1,0:T(1,128)} %bitcast.7), calls=%async_computation | async-start | bytes 589824 | tf_op jit(solution)/shard_map/all_to_all | solution.py:461
  16.4 15.5 %collective-permute-start.1 = (f32[8,144,128]{2,1,0:T(8,128)S(1)}, f32[8,144,128]{2,1,0:T(8,128)S(1)}, u32[]{:S(2)}, u32[]{:S(2)}) collective-permute-start(f32[8,144,128]{2,1,0:T(8,128)S(1)} %get-tuple-element.9), channel_id=1, source_target_pairs={{0,64},{64,0},{128,192},{192,128},{1,65},{65,1},{129,193},{193,129... | collective-permute-start | bytes 1769480 | tf_op jit(solution)/shard_map/ppermute | solution.py:448
  17.5 13.0 %collective-permute-start.2 = (f32[128,128]{1,0:T(8,128)S(1)}, f32[128,128]{1,0:T(8,128)S(1)}, u32[]{:S(2)}, u32[]{:S(2)}) collective-permute-start(f32[128,128]{1,0:T(8,128)S(1)} %get-tuple-element.10), channel_id=1, source_target_pairs={{0,1},{1,0},{2,3},{3,2},{4,5},{5,4},{6,7},{7,6},{8,9},{9,8},{10,11... | collective-permute-start | bytes 196616 | tf_op jit(solution)/shard_map/ppermute | solution.py:475
  18.8 11.7 %collective-permute-start.3 = (f32[128,128]{1,0:T(8,128)S(1)}, f32[128,128]{1,0:T(8,128)S(1)}, u32[]{:S(2)}, u32[]{:S(2)}) collective-permute-start(f32[128,128]{1,0:T(8,128)S(1)} %get-tuple-element.10), channel_id=1, source_target_pairs={{1,2},{2,1},{3,4},{4,3},{5,6},{6,5},{7,8},{8,7},{9,10},{10,9},{11,... | collective-permute-start | bytes 196616 | tf_op jit(solution)/shard_map/ppermute | solution.py:475
  26.9 4.9 %collective-permute-start = (f32[576,128]{1,0:T(8,128)S(1)}, f32[576,128]{1,0:T(8,128)S(1)}, u32[]{:S(2)}, u32[]{:S(2)}) collective-permute-start(f32[576,128]{1,0:T(8,128)S(1)} %bitcast.4), channel_id=1, source_target_pairs={{0,64},{64,0},{128,192},{192,128},{1,65},{65,1},{129,193},{193,129... | collective-permute-start | bytes 884744 | tf_op jit(solution)/shard_map/ppermute | solution.py:448
  30.5 1.3 %collective-permute-start.4 = (f32[136,128]{1,0:T(8,128)S(1)}, f32[136,128]{1,0:T(8,128)S(1)}, u32[]{:S(2)}, u32[]{:S(2)}) collective-permute-start(f32[136,128]{1,0:T(8,128)S(1)} %concatenate.3.refs_5_), channel_id=1, source_target_pairs={{0,64},{64,0},{128,192},{192,128},{1,65},{65,1},{129,193},{193,129... | collective-permute-start | bytes 208904 | tf_op jit(solution)/shard_map/ppermute | solution.py:448
  37.0 6.4 %collective-permute-start.5 = (f32[2,128,128]{2,1,0:T(8,128)S(1)}, f32[2,128,128]{2,1,0:T(8,128)S(1)}, u32[]{:S(2)}, u32[]{:S(2)}) collective-permute-start(f32[2,128,128]{2,1,0:T(8,128)S(1)} %get-tuple-element.12), channel_id=1, source_target_pairs={{0,128},{64,192},{128,0},{192,64},{1,129},{65,193},{129,1},{193,65... | collective-permute-start | bytes 393224 | tf_op jit(solution)/shard_map/ppermute | solution.py:448

commit v5 on v4

--- a/solution.py
+++ b/solution.py
@@ -262,10 +262,38 @@
     )
 
 
+def cut_windows(src_ref, rec_ref, message_ref, windows_ref, waves, sems):
+    core = lax.axis_index("freq") & 1
+    copies, copy_in = copier(sems)
+    for b in range(2):
+        copy_waves(copy_in, src_ref, rec_ref, message_ref, waves, 2 * b + core, b, 2 * b)
+    for copy in copies:
+        copy.wait()
+    clear_ends(waves, core)
+    lane = lanes_of(ROWS)
+    place = lane & (WIN - 1)
+    for part in range(4):
+        own = waves[0, part, GUARD : GUARD + ROWS, :]
+        for m in range(1, ITEMS):
+            value = lane_roll(waves[m, part, GUARD : GUARD + ROWS, :], WIN * m)
+            own = jnp.where((((lane + 16) >> 5) & 3) == m, value, own)
+        windows_ref[part] = jnp.where(place < 16, lane_roll(own, 36), lane_roll(own, 28))
+
+
+def clear_ends(waves, core):
+    @pl.when(core == 0)
+    def _():
+        clear_above(waves, range(2))
+
+    @pl.when(core == 1)
+    def _():
+        clear_below(waves, range(2, 4))
+
+
 def march_sent(*refs):
     speed_refs, src_ref, rec_ref, message_ref, halo_refs = refs[:2], *refs[2:5], refs[5:7]
-    send_ref, sums_ref = refs[7:9]
-    waves, sides, stage, speed, coef, omega, first, second, images, sems = refs[9:]
+    windows_ref, send_ref, sums_ref = refs[7:10]
+    waves, sides, stage, speed, coef, omega, first, second, images, sems = refs[10:]
     freq = lax.axis_index("freq")
     core = freq & 1
     strip = lax.axis_index("strip")
@@ -278,6 +306,7 @@
         copy_waves(copy_in, src_ref, rec_ref, message_ref, waves, 2 * b + core, b, 2 * b)
     for k in range(2):
         copy_in(halo_refs[k], sides.at[k])
+    copy_in(windows_ref, waves.at[ITEMS, :, GUARD : GUARD + ROWS, :])
 
     item = stepper(waves, speed, coef, omega, first, second, images)
     for copy in copies[:speed_count]:
@@ -334,13 +363,7 @@
     for copy in copies[speed_count:]:
         copy.wait()
 
-    @pl.when(core == 0)
-    def _():
-        clear_above(waves, range(2))
-
-    @pl.when(core == 1)
-    def _():
-        clear_below(waves, range(2, 4))
+    clear_ends(waves, core)
 
     def turned(k, low, high, shift):
         return pltpu.roll(sides[k, low:high, :], (WIN * (shift - core)) & (LANES - 1), 1)
@@ -355,17 +378,13 @@
     below = pick(0, TILE, LANES // WIN - 1)
     below = jnp.where((tile_lane >= 2 * WIN) & (core == 1), 0.0, below)
     beside = jnp.concatenate([above, pick(0, CORE_ROWS, 0), below])
-    lane = lanes_of(ROWS)
-    place = lane & (WIN - 1)
+    place = lanes_of(ROWS) & (WIN - 1)
+    halo = (place < 4) | (place >= 28)
     for part in range(4):
-        own = waves[0, part, GUARD : GUARD + ROWS, :]
-        for m in range(1, ITEMS):
-            value = lane_roll(waves[m, part, GUARD : GUARD + ROWS, :], WIN * m)
-            own = jnp.where((((lane + 16) >> 5) & 3) == m, value, own)
-        window = lane_roll(beside, 28 - 8 * part)
-        window = jnp.where((place >= 4) & (place < 16), lane_roll(own, 36), window)
-        window = jnp.where((place >= 16) & (place < 28), lane_roll(own, 28), window)
-        waves[ITEMS, part, GUARD : GUARD + ROWS, :] = window
+        window = waves[ITEMS, part, GUARD : GUARD + ROWS, :]
+        waves[ITEMS, part, GUARD : GUARD + ROWS, :] = jnp.where(
+            halo, lane_roll(beside, 28 - 8 * part), window
+        )
     rows = [sides[k, CORE_ROWS : CORE_ROWS + TILE, :] for k in range(2)]
     odd = (((tile_lane + 112) >> 5) & 1) == 1
     for m in range(ITEMS):
@@ -486,6 +505,17 @@
         ]
     )
 
+    windows = pl.pallas_call(
+        cut_windows,
+        out_shape=shape(4, ROWS, LANES),
+        in_specs=[anywhere] * 3,
+        out_specs=vmem,
+        scratch_shapes=[
+            pltpu.VMEM((ITEMS, 4, ROWS + 2 * GUARD, LANES), F32),
+            pltpu.SemaphoreType.DMA((6,)),
+        ],
+        compiler_params=SMALL,
+    )(source, receiver, message)
     inputs = (speeds, other_speeds, source, receiver, message, halos, across(halos, 1))
 
     def scratch(items, kinds):
@@ -496,14 +526,14 @@
             pltpu.VMEM((4, ROWS + 2 * GUARD, LANES), F32),
             pltpu.VMEM((4, ROWS + 2 * GUARD, LANES), F32),
             pltpu.VMEM((kinds, 2, CORE_ROWS, LANES), F32),
-            pltpu.SemaphoreType.DMA((20,)),
+            pltpu.SemaphoreType.DMA((21,)),
         ]
 
     stage_rows = 32 + SPAN * CORE_ROWS // TILE
     send, sums = pl.pallas_call(
         march_sent,
         out_shape=[shape(2, CORE_ROWS, LANES)] * 2,
-        in_specs=[anywhere] * 7,
+        in_specs=[anywhere] * 8,
         out_specs=[vmem] * 2,
         scratch_shapes=[
             pltpu.VMEM((ITEMS + 1, 4, ROWS + 2 * GUARD, LANES), F32),
@@ -512,7 +542,7 @@
         ]
         + scratch(ITEMS + 1, 3),
         compiler_params=SMALL,
-    )(*inputs)
+    )(*inputs, windows)
     received = across(send, 2)
     kept = pl.pallas_call(
         march_kept,

time: 44.2 us -> 43.6 us (0.986)
  waiting for transfers between devices: 9.68 us -> 8.31 us
  Pallas kernels: 10.1 us -> 10.9 us
    ppermute x4, waiting for transfers between devices: 2.84 us -> 1.47 us  [across(): return lax.ppermute(x, 'freq', [(i, i ^ k) for i in range(freqs)])]
    pallas_call x0 -> x1, Pallas kernels: none -> 1.17 us  [shards(): pl.pallas_call(cut_windows, out_shape=shape(4, ROWS, LANES), in_specs=[an...]
  transfers between devices with their start and end apart: 7 -> 7, of which waited for: 3 -> 3; matrix products, arithmetic and copies ran while one was open for 0% -> 0% of each run, Pallas kernels for 6% -> 9%
where the time goes in v5:
time: 43.6 us; the launch traced here: 43.4 us
  starting transfers between devices  22.8 us (52%)
  Pallas kernels  10.9 us (25%)
  waiting for transfers between devices  8.31 us (19%)
  between operations  0.76 us (2%)
  other arithmetic  0.69 us (2%)
    all_to_all x1, starting transfers between devices, shards(): lax.all_to_all(packed.reshape(strips, 1, SPAN * LANES), 'strip', split_ax...  13.6 us
    ppermute x4, starting transfers between devices, across(): return lax.ppermute(x, 'freq', [(i, i ^ k) for i in range(freqs)])  7.23 us
    all_to_all x1, waiting for transfers between devices, shards(): lax.all_to_all(packed.reshape(strips, 1, SPAN * LANES), 'strip', split_ax...  6.84 us
    pallas_call x1, Pallas kernels, shards(): pl.pallas_call(march_sent, out_shape=[shape(2, CORE_ROWS, LANES)] * 2, in...  4.66 us
    pallas_call x1, Pallas kernels, shards(): pl.pallas_call(march_kept, out_shape=shape(2, CORE_ROWS, LANES), in_specs...  2.26 us
    pallas_call x1, Pallas kernels, shards(): pl.pallas_call(pack_speed, out_shape=shape(SPAN * strips, LANES), in_spec...  2.21 us
    ppermute x2, starting transfers between devices, swap(): lax.ppermute(x, 'strip', [p for i, j in pairs for p in ((i, j), (j, i))])  1.96 us
    ppermute x4, waiting for transfers between devices, across(): return lax.ppermute(x, 'freq', [(i, i ^ k) for i in range(freqs)])  1.47 us
  transfers between devices with their start and end apart: 7, of which 3 were waited for; matrix products, arithmetic and copies ran while one was open for 0% of the time, Pallas kernels for 9%

profile of v5, /device:TPU:1, one launch (start us, length us, event | category | flops | bytes accessed | tf_op | source)
XLA Modules:
  0.0 43.4 jit_solution(1907608376359227886)
XLA Ops:
  0.0 0.0 copy-start
  0.0 0.0 copy-start.1
  0.0 2.2 %shard_map.46 = f32[576,128]{1,0:T(8,128)} custom-call(f32[2,8,8192]{2,1,0:T(8,128)} %vel_ref.1), custom_call_target="tpu_custom_call" | custom-call | tf_op jit(solution)/shard_map/pallas_call | solution.py:469
  2.2 13.6 %all-to-all-start = ((f32[64,1,1152]{2,1,0:T(1,128)}), f32[64,1,1152]{2,1,0:T(1,128)S(1)}, u32[]{:S(2)}, u32[]{:S(2)}) async-start(f32[64,1,1152]{2,1,0:T(1,128)} %bitcast.7), calls=%async_computation | async-start | bytes 589824 | tf_op jit(solution)/shard_map/all_to_all | solution.py:480
  15.8 0.0 copy-done
  15.8 0.0 copy-done.1
  15.8 0.6 %shard_map.47 = (f32[128,128]{1,0:T(8,128)S(1)}, f32[8,144,128]{2,1,0:T(8,128)S(1)}) custom-call(f32[2,1,512,128]{3,2,1,0:T(8,128)S(1)} %copy-done, f32[2,1,512,128]{3,2,1,0:T(8,128)S(1)} %copy-done.1), custom_call_target="tpu_custom_call" | custom-call | tf_op jit(solution)/shard_map/pallas_call | solution.py:485
  16.4 1.0 %collective-permute-start.1 = (f32[8,144,128]{2,1,0:T(8,128)S(1)}, f32[8,144,128]{2,1,0:T(8,128)S(1)}, u32[]{:S(2)}, u32[]{:S(2)}) collective-permute-start(f32[8,144,128]{2,1,0:T(8,128)S(1)} %get-tuple-element.9), channel_id=1, source_target_pairs={{0,64},{64,0},{128,192},{192,128},{1,65},{65,1},{129,193},{193,129... | collective-permute-start | bytes 1769480 | tf_op jit(solution)/shard_map/ppermute | solution.py:467
  17.5 1.3 %collective-permute-start.2 = (f32[128,128]{1,0:T(8,128)S(1)}, f32[128,128]{1,0:T(8,128)S(1)}, u32[]{:S(2)}, u32[]{:S(2)}) collective-permute-start(f32[128,128]{1,0:T(8,128)S(1)} %get-tuple-element.10), channel_id=1, source_target_pairs={{0,1},{1,0},{2,3},{3,2},{4,5},{5,4},{6,7},{7,6},{8,9},{9,8},{10,11... | collective-permute-start | bytes 196616 | tf_op jit(solution)/shard_map/ppermute | solution.py:494
  18.8 0.7 %collective-permute-start.3 = (f32[128,128]{1,0:T(8,128)S(1)}, f32[128,128]{1,0:T(8,128)S(1)}, u32[]{:S(2)}, u32[]{:S(2)}) collective-permute-start(f32[128,128]{1,0:T(8,128)S(1)} %get-tuple-element.10), channel_id=1, source_target_pairs={{1,2},{2,1},{3,4},{4,3},{5,6},{6,5},{7,8},{8,7},{9,10},{10,9},{11,... | collective-permute-start | bytes 196616 | tf_op jit(solution)/shard_map/ppermute | solution.py:494
  20.1 6.8 %all-to-all-done = f32[64,1,1152]{2,1,0:T(1,128)S(1)} async-done(((f32[64,1,1152]{2,1,0:T(1,128)}), f32[64,1,1152]{2,1,0:T(1,128)S(1)}, u32[]{:S(2)}, u32[]{:S(2)}) %all-to-all-start) | async-done | bytes 294944 | tf_op jit(solution)/shard_map/all_to_all | solution.py:480
  26.9 3.6 %collective-permute-start = (f32[576,128]{1,0:T(8,128)S(1)}, f32[576,128]{1,0:T(8,128)S(1)}, u32[]{:S(2)}, u32[]{:S(2)}) collective-permute-start(f32[576,128]{1,0:T(8,128)S(1)} %bitcast.4), channel_id=1, source_target_pairs={{0,64},{64,0},{128,192},{192,128},{1,65},{65,1},{129,193},{193,129... | collective-permute-start | bytes 884744 | tf_op jit(solution)/shard_map/ppermute | solution.py:467
  30.5 0.0 collective-permute-done.2
  30.5 0.0 collective-permute-done.3
  30.5 0.1 collective-permute-start.4
  30.6 0.0 collective-permute-done.1.message_ref.refs_4_
  30.6 1.2 %shard_map.48.refs_7_ = f32[4,144,128]{2,1,0:T(8,128)S(1)} custom-call(f32[2,1,512,128]{3,2,1,0:T(8,128)S(1)} %copy-done, f32[2,1,512,128]{3,2,1,0:T(8,128)S(1)} %copy-done.1, f32[8,144,128]{2,1,0:T(8,128)S(1)} %collective-permute-done.1.message_ref.refs_4_), custom_call_target="tpu_custom_call" | custom-call | tf_op jit(solution)/shard_map/pallas_call | solution.py:508
  31.8 0.1 collective-permute-done.4.refs_6_
  31.9 0.0 collective-permute-done.refs_1_
  31.9 4.7 %shard_map.49 = (f32[2,128,128]{2,1,0:T(8,128)S(1)}, f32[2,128,128]{2,1,0:T(8,128)S(1)}) custom-call(f32[576,128]{1,0:T(8,128)S(1)} %bitcast.5, f32[576,128]{1,0:T(8,128)S(1)} %collective-permute-done.refs_1_, f32[2,1,512,128]{3,2,1,0:T(8,128)S(1)} %copy-done, f32[2,1,512,128]{3,2,1,0:T(8,128)S(1)} %copy-done.1, ...), custom_call_target="tpu_custom_call" | custom-call | tf_op jit(solution)/shard_map/pallas_call | solution.py:533
  36.5 2.5 %collective-permute-start.5 = (f32[2,128,128]{2,1,0:T(8,128)S(1)}, f32[2,128,128]{2,1,0:T(8,128)S(1)}, u32[]{:S(2)}, u32[]{:S(2)}) collective-permute-start(f32[2,128,128]{2,1,0:T(8,128)S(1)} %get-tuple-element.12), channel_id=1, source_target_pairs={{0,128},{64,192},{128,0},{192,64},{1,129},{65,193},{129,1},{193,65... | collective-permute-start | bytes 393224 | tf_op jit(solution)/shard_map/ppermute | solution.py:467
  39.1 2.3 %shard_map.50 = f32[2,128,128]{2,1,0:T(8,128)S(1)} custom-call(f32[576,128]{1,0:T(8,128)S(1)} %bitcast.6, f32[576,128]{1,0:T(8,128)S(1)} %collective-permute-done.refs_1_, f32[2,1,512,128]{3,2,1,0:T(8,128)S(1)} %copy-done, f32[2,1,512,128]{3,2,1,0:T(8,128)S(1)} %copy-done.1, f32[8,144,128]{2,1,0:T(8,128)S(1)} %collective-permute-done.1.message_ref.refs_4_, ...), custom_call_target="tpu_custom_call" | custom-call | tf_op jit(solution)/shard_map/pallas_call | solution.py:547
  41.3 1.4 %collective-permute-done.5 = f32[2,128,128]{2,1,0:T(8,128)S(1)} collective-permute-done((f32[2,128,128]{2,1,0:T(8,128)S(1)}, f32[2,128,128]{2,1,0:T(8,128)S(1)}, u32[]{:S(2)}, u32[]{:S(2)}) %collective-permute-start.5) | collective-permute-done | bytes 131104 | tf_op jit(solution)/shard_map/ppermute | solution.py:467
  42.7 0.7 %add.5 = f32[2,128,128]{2,1,0:T(8,128)} add(f32[2,128,128]{2,1,0:T(8,128)S(1)} %shard_map.50, f32[2,128,128]{2,1,0:T(8,128)S(1)} %collective-permute-done.5) | non-fusion elementwise | flops 32768 | bytes 393216 | tf_op jit(solution)/shard_map/add | solution.py:559
  (3 shorter events, 0.0 us)
Async XLA Ops:
  0.0 15.8 %copy-start = (f32[2,1,512,128]{3,2,1,0:T(8,128)S(1)}, f32[2,1,512,128]{3,2,1,0:T(8,128)}, u32[]{:S(2)}) copy-start(f32[2,1,512,128]{3,2,1,0:T(8,128)} %refs_2_.3) | copy-start | bytes 1572868
  0.0 15.8 %copy-start.1 = (f32[2,1,512,128]{3,2,1,0:T(8,128)S(1)}, f32[2,1,512,128]{3,2,1,0:T(8,128)}, u32[]{:S(2)}) copy-start(f32[2,1,512,128]{3,2,1,0:T(8,128)} %refs_3_.3) | copy-start | bytes 1572868
  2.2 24.7 %all-to-all-start = ((f32[64,1,1152]{2,1,0:T(1,128)}), f32[64,1,1152]{2,1,0:T(1,128)S(1)}, u32[]{:S(2)}, u32[]{:S(2)}) async-start(f32[64,1,1152]{2,1,0:T(1,128)} %bitcast.7), calls=%async_computation | async-start | bytes 589824 | tf_op jit(solution)/shard_map/all_to_all | solution.py:480
  16.4 14.2 %collective-permute-start.1 = (f32[8,144,128]{2,1,0:T(8,128)S(1)}, f32[8,144,128]{2,1,0:T(8,128)S(1)}, u32[]{:S(2)}, u32[]{:S(2)}) collective-permute-start(f32[8,144,128]{2,1,0:T(8,128)S(1)} %get-tuple-element.9), channel_id=1, source_target_pairs={{0,64},{64,0},{128,192},{192,128},{1,65},{65,1},{129,193},{193,129... | collective-permute-start | bytes 1769480 | tf_op jit(solution)/shard_map/ppermute | solution.py:467
  17.5 13.0 %collective-permute-start.2 = (f32[128,128]{1,0:T(8,128)S(1)}, f32[128,128]{1,0:T(8,128)S(1)}, u32[]{:S(2)}, u32[]{:S(2)}) collective-permute-start(f32[128,128]{1,0:T(8,128)S(1)} %get-tuple-element.10), channel_id=1, source_target_pairs={{0,1},{1,0},{2,3},{3,2},{4,5},{5,4},{6,7},{7,6},{8,9},{9,8},{10,11... | collective-permute-start | bytes 196616 | tf_op jit(solution)/shard_map/ppermute | solution.py:494
  18.8 11.7 %collective-permute-start.3 = (f32[128,128]{1,0:T(8,128)S(1)}, f32[128,128]{1,0:T(8,128)S(1)}, u32[]{:S(2)}, u32[]{:S(2)}) collective-permute-start(f32[128,128]{1,0:T(8,128)S(1)} %get-tuple-element.10), channel_id=1, source_target_pairs={{1,2},{2,1},{3,4},{4,3},{5,6},{6,5},{7,8},{8,7},{9,10},{10,9},{11,... | collective-permute-start | bytes 196616 | tf_op jit(solution)/shard_map/ppermute | solution.py:494
  26.9 4.9 %collective-permute-start = (f32[576,128]{1,0:T(8,128)S(1)}, f32[576,128]{1,0:T(8,128)S(1)}, u32[]{:S(2)}, u32[]{:S(2)}) collective-permute-start(f32[576,128]{1,0:T(8,128)S(1)} %bitcast.4), channel_id=1, source_target_pairs={{0,64},{64,0},{128,192},{192,128},{1,65},{65,1},{129,193},{193,129... | collective-permute-start | bytes 884744 | tf_op jit(solution)/shard_map/ppermute | solution.py:467
  30.5 1.3 %collective-permute-start.4 = (f32[136,128]{1,0:T(8,128)S(1)}, f32[136,128]{1,0:T(8,128)S(1)}, u32[]{:S(2)}, u32[]{:S(2)}) collective-permute-start(f32[136,128]{1,0:T(8,128)S(1)} %concatenate.3.refs_5_), channel_id=1, source_target_pairs={{0,64},{64,0},{128,192},{192,128},{1,65},{65,1},{129,193},{193,129... | collective-permute-start | bytes 208904 | tf_op jit(solution)/shard_map/ppermute | solution.py:467
  36.5 6.2 %collective-permute-start.5 = (f32[2,128,128]{2,1,0:T(8,128)S(1)}, f32[2,128,128]{2,1,0:T(8,128)S(1)}, u32[]{:S(2)}, u32[]{:S(2)}) collective-permute-start(f32[2,128,128]{2,1,0:T(8,128)S(1)} %get-tuple-element.12), channel_id=1, source_target_pairs={{0,128},{64,192},{128,0},{192,64},{1,129},{65,193},{129,1},{193,65... | collective-permute-start | bytes 393224 | tf_op jit(solution)/shard_map/ppermute | solution.py:467

commit v6 on v5

--- a/solution.py
+++ b/solution.py
@@ -302,11 +302,12 @@
     for b in range(2):
         copy_speeds(copy_in, speed_refs, stage.at[b], 2 * b + core, core)
     speed_count = len(copies)
-    for b in range(2):
-        copy_waves(copy_in, src_ref, rec_ref, message_ref, waves, 2 * b + core, b, 2 * b)
+    sent = 1 - (freq >> 1)
+    sent_block = 2 * sent + core
+    copy_waves(copy_in, src_ref, rec_ref, message_ref, waves, sent_block, sent, 0)
     for k in range(2):
         copy_in(halo_refs[k], sides.at[k])
-    copy_in(windows_ref, waves.at[ITEMS, :, GUARD : GUARD + ROWS, :])
+    copy_in(windows_ref, waves.at[2, :, GUARD : GUARD + ROWS, :])
 
     item = stepper(waves, speed, coef, omega, first, second, images)
     for copy in copies[:speed_count]:
@@ -318,6 +319,9 @@
     tile = lax.broadcasted_iota(jnp.int32, dims, 0)
     on_grid = jnp.logical_not(
         ((place < 4) & (strip == 0)) | ((place >= 28) & (strip == strips - 1))
+    )
+    sent_live = jnp.logical_not(
+        ((tile == 0) & (sent_block == 0)) | ((tile == tiles - 1) & (sent_block == BLOCKS - 1))
     )
     for depth in range(2):
         window = jnp.zeros(dims, F32)
@@ -352,18 +356,25 @@
                 lanes_in(36, 48), pltpu.roll(here, (base + 36) % LANES, 2), window
             )
             window_live = window_live | (live & ((((lane + 112) >> 6) & 1) == b))
-            speed[b, depth] = (phase_depth / here).reshape(ROWS, LANES)
-            coef[b, depth] = jnp.where(live, fd_coef * here, 0.0).reshape(ROWS, LANES)
         window = window + pltpu.roll(window, WIN, 2)
-        speed[2, depth] = (phase_depth / window).reshape(ROWS, LANES)
-        coef[2, depth] = jnp.where(
+        here = tile_speeds(stage.at[sent], depth)
+        speed[0, depth] = (phase_depth / here).reshape(ROWS, LANES)
+        coef[0, depth] = jnp.where(sent_live, fd_coef * here, 0.0).reshape(ROWS, LANES)
+        speed[1, depth] = (phase_depth / window).reshape(ROWS, LANES)
+        coef[1, depth] = jnp.where(
             on_grid & window_live, fd_coef * window, 0.0
         ).reshape(ROWS, LANES)
 
     for copy in copies[speed_count:]:
         copy.wait()
 
-    clear_ends(waves, core)
+    @pl.when(sent_block == 0)
+    def _():
+        clear_above(waves, range(2))
+
+    @pl.when(sent_block == BLOCKS - 1)
+    def _():
+        clear_below(waves, range(2))
 
     def turned(k, low, high, shift):
         return pltpu.roll(sides[k, low:high, :], (WIN * (shift - core)) & (LANES - 1), 1)
@@ -381,29 +392,26 @@
     place = lanes_of(ROWS) & (WIN - 1)
     halo = (place < 4) | (place >= 28)
     for part in range(4):
-        window = waves[ITEMS, part, GUARD : GUARD + ROWS, :]
-        waves[ITEMS, part, GUARD : GUARD + ROWS, :] = jnp.where(
+        window = waves[2, part, GUARD : GUARD + ROWS, :]
+        waves[2, part, GUARD : GUARD + ROWS, :] = jnp.where(
             halo, lane_roll(beside, 28 - 8 * part), window
         )
     rows = [sides[k, CORE_ROWS : CORE_ROWS + TILE, :] for k in range(2)]
     odd = (((tile_lane + 112) >> 5) & 1) == 1
-    for m in range(ITEMS):
-        omega[m * TILE : (m + 1) * TILE, :] = rows[m & 1]
-    omega[ITEMS * TILE :, :] = jnp.where(odd, rows[1], rows[0])
-
-    sent = 1 - (freq >> 1)
-
-    def step(j, carry):
-        k = jnp.where(j == 2, ITEMS, 2 * sent + j)
+    for k in range(2):
+        omega[k * TILE : (k + 1) * TILE, :] = rows[k]
+    omega[2 * TILE :, :] = jnp.where(odd, rows[1], rows[0])
+
+    def step(k, carry):
         item(k, k >> 1)
         return carry
 
     lax.fori_loop(0, 3, step, 0)
     for depth in range(2):
-        value = images[2, depth]
+        value = images[1, depth]
         value = value + lane_roll(value, -WIN)
         sums_ref[depth] = value
-        send_ref[depth] = patch(images[sent, depth], value, sent)
+        send_ref[depth] = patch(images[0, depth], value, sent)
 
 
 def march_kept(*refs):
@@ -536,11 +544,11 @@
         in_specs=[anywhere] * 8,
         out_specs=[vmem] * 2,
         scratch_shapes=[
-            pltpu.VMEM((ITEMS + 1, 4, ROWS + 2 * GUARD, LANES), F32),
+            pltpu.VMEM((3, 4, ROWS + 2 * GUARD, LANES), F32),
             pltpu.VMEM((2, CORE_ROWS + TILE, LANES), F32),
             pltpu.VMEM((2, 2, stage_rows, LANES), F32),
         ]
-        + scratch(ITEMS + 1, 3),
+        + scratch(3, 2),
         compiler_params=SMALL,
     )(*inputs, windows)
     received = across(send, 2)

time: 43.6 us -> 43.4 us (level)
  no operation moved by 1% of the time
where the time goes in v6:
time: 43.4 us; the launch traced here: 43.2 us
  starting transfers between devices  22.8 us (53%)
  Pallas kernels  10.6 us (24%)
  waiting for transfers between devices  8.32 us (19%)
  between operations  0.76 us (2%)
  other arithmetic  0.69 us (2%)
    all_to_all x1, starting transfers between devices, shards(): lax.all_to_all(packed.reshape(strips, 1, SPAN * LANES), 'strip', split_ax...  13.6 us
    ppermute x4, starting transfers between devices, across(): return lax.ppermute(x, 'freq', [(i, i ^ k) for i in range(freqs)])  7.23 us
    all_to_all x1, waiting for transfers between devices, shards(): lax.all_to_all(packed.reshape(strips, 1, SPAN * LANES), 'strip', split_ax...  6.84 us
    pallas_call x1, Pallas kernels, shards(): pl.pallas_call(march_sent, out_shape=[shape(2, CORE_ROWS, LANES)] * 2, in...  4.44 us
    pallas_call x1, Pallas kernels, shards(): pl.pallas_call(march_kept, out_shape=shape(2, CORE_ROWS, LANES), in_specs...  2.26 us
    pallas_call x1, Pallas kernels, shards(): pl.pallas_call(pack_speed, out_shape=shape(SPAN * strips, LANES), in_spec...  2.21 us
    ppermute x2, starting transfers between devices, swap(): lax.ppermute(x, 'strip', [p for i, j in pairs for p in ((i, j), (j, i))])  1.96 us
    ppermute x4, waiting for transfers between devices, across(): return lax.ppermute(x, 'freq', [(i, i ^ k) for i in range(freqs)])  1.47 us
  transfers between devices with their start and end apart: 7, of which 3 were waited for; matrix products, arithmetic and copies ran while one was open for 0% of the time, Pallas kernels for 9%

profile of v6, /device:TPU:1, one launch (start us, length us, event | category | flops | bytes accessed | tf_op | source)
XLA Modules:
  0.0 43.2 jit_solution(3318534471321169698)
XLA Ops:
  0.0 0.0 copy-start
  0.0 0.0 copy-start.1
  0.0 2.2 %shard_map.46 = f32[576,128]{1,0:T(8,128)} custom-call(f32[2,8,8192]{2,1,0:T(8,128)} %vel_ref.1), custom_call_target="tpu_custom_call" | custom-call | tf_op jit(solution)/shard_map/pallas_call | solution.py:477
  2.2 13.6 %all-to-all-start = ((f32[64,1,1152]{2,1,0:T(1,128)}), f32[64,1,1152]{2,1,0:T(1,128)S(1)}, u32[]{:S(2)}, u32[]{:S(2)}) async-start(f32[64,1,1152]{2,1,0:T(1,128)} %bitcast.7), calls=%async_computation | async-start | bytes 589824 | tf_op jit(solution)/shard_map/all_to_all | solution.py:488
  15.8 0.0 copy-done
  15.8 0.0 copy-done.1
  15.8 0.6 %shard_map.47 = (f32[128,128]{1,0:T(8,128)S(1)}, f32[8,144,128]{2,1,0:T(8,128)S(1)}) custom-call(f32[2,1,512,128]{3,2,1,0:T(8,128)S(1)} %copy-done, f32[2,1,512,128]{3,2,1,0:T(8,128)S(1)} %copy-done.1), custom_call_target="tpu_custom_call" | custom-call | tf_op jit(solution)/shard_map/pallas_call | solution.py:493
  16.4 1.0 %collective-permute-start.1 = (f32[8,144,128]{2,1,0:T(8,128)S(1)}, f32[8,144,128]{2,1,0:T(8,128)S(1)}, u32[]{:S(2)}, u32[]{:S(2)}) collective-permute-start(f32[8,144,128]{2,1,0:T(8,128)S(1)} %get-tuple-element.9), channel_id=1, source_target_pairs={{0,64},{64,0},{128,192},{192,128},{1,65},{65,1},{129,193},{193,129... | collective-permute-start | bytes 1769480 | tf_op jit(solution)/shard_map/ppermute | solution.py:475
  17.5 1.3 %collective-permute-start.2 = (f32[128,128]{1,0:T(8,128)S(1)}, f32[128,128]{1,0:T(8,128)S(1)}, u32[]{:S(2)}, u32[]{:S(2)}) collective-permute-start(f32[128,128]{1,0:T(8,128)S(1)} %get-tuple-element.10), channel_id=1, source_target_pairs={{0,1},{1,0},{2,3},{3,2},{4,5},{5,4},{6,7},{7,6},{8,9},{9,8},{10,11... | collective-permute-start | bytes 196616 | tf_op jit(solution)/shard_map/ppermute | solution.py:502
  18.8 0.7 %collective-permute-start.3 = (f32[128,128]{1,0:T(8,128)S(1)}, f32[128,128]{1,0:T(8,128)S(1)}, u32[]{:S(2)}, u32[]{:S(2)}) collective-permute-start(f32[128,128]{1,0:T(8,128)S(1)} %get-tuple-element.10), channel_id=1, source_target_pairs={{1,2},{2,1},{3,4},{4,3},{5,6},{6,5},{7,8},{8,7},{9,10},{10,9},{11,... | collective-permute-start | bytes 196616 | tf_op jit(solution)/shard_map/ppermute | solution.py:502
  20.1 6.8 %all-to-all-done = f32[64,1,1152]{2,1,0:T(1,128)S(1)} async-done(((f32[64,1,1152]{2,1,0:T(1,128)}), f32[64,1,1152]{2,1,0:T(1,128)S(1)}, u32[]{:S(2)}, u32[]{:S(2)}) %all-to-all-start) | async-done | bytes 294944 | tf_op jit(solution)/shard_map/all_to_all | solution.py:488
  26.9 3.6 %collective-permute-start = (f32[576,128]{1,0:T(8,128)S(1)}, f32[576,128]{1,0:T(8,128)S(1)}, u32[]{:S(2)}, u32[]{:S(2)}) collective-permute-start(f32[576,128]{1,0:T(8,128)S(1)} %bitcast.4), channel_id=1, source_target_pairs={{0,64},{64,0},{128,192},{192,128},{1,65},{65,1},{129,193},{193,129... | collective-permute-start | bytes 884744 | tf_op jit(solution)/shard_map/ppermute | solution.py:475
  30.5 0.0 collective-permute-done.2
  30.5 0.0 collective-permute-done.3
  30.5 0.1 collective-permute-start.4
  30.6 0.0 collective-permute-done.1.message_ref.refs_4_
  30.6 1.2 %shard_map.48.refs_7_ = f32[4,144,128]{2,1,0:T(8,128)S(1)} custom-call(f32[2,1,512,128]{3,2,1,0:T(8,128)S(1)} %copy-done, f32[2,1,512,128]{3,2,1,0:T(8,128)S(1)} %copy-done.1, f32[8,144,128]{2,1,0:T(8,128)S(1)} %collective-permute-done.1.message_ref.refs_4_), custom_call_target="tpu_custom_call" | custom-call | tf_op jit(solution)/shard_map/pallas_call | solution.py:516
  31.8 0.1 collective-permute-done.4.refs_6_
  31.9 0.0 collective-permute-done.refs_1_
  31.9 4.4 %shard_map.49 = (f32[2,128,128]{2,1,0:T(8,128)S(1)}, f32[2,128,128]{2,1,0:T(8,128)S(1)}) custom-call(f32[576,128]{1,0:T(8,128)S(1)} %bitcast.5, f32[576,128]{1,0:T(8,128)S(1)} %collective-permute-done.refs_1_, f32[2,1,512,128]{3,2,1,0:T(8,128)S(1)} %copy-done, f32[2,1,512,128]{3,2,1,0:T(8,128)S(1)} %copy-done.1, ...), custom_call_target="tpu_custom_call" | custom-call | tf_op jit(solution)/shard_map/pallas_call | solution.py:541
  36.3 2.5 %collective-permute-start.5 = (f32[2,128,128]{2,1,0:T(8,128)S(1)}, f32[2,128,128]{2,1,0:T(8,128)S(1)}, u32[]{:S(2)}, u32[]{:S(2)}) collective-permute-start(f32[2,128,128]{2,1,0:T(8,128)S(1)} %get-tuple-element.12), channel_id=1, source_target_pairs={{0,128},{64,192},{128,0},{192,64},{1,129},{65,193},{129,1},{193,65... | collective-permute-start | bytes 393224 | tf_op jit(solution)/shard_map/ppermute | solution.py:475
  38.9 2.3 %shard_map.50 = f32[2,128,128]{2,1,0:T(8,128)S(1)} custom-call(f32[576,128]{1,0:T(8,128)S(1)} %bitcast.6, f32[576,128]{1,0:T(8,128)S(1)} %collective-permute-done.refs_1_, f32[2,1,512,128]{3,2,1,0:T(8,128)S(1)} %copy-done, f32[2,1,512,128]{3,2,1,0:T(8,128)S(1)} %copy-done.1, f32[8,144,128]{2,1,0:T(8,128)S(1)} %collective-permute-done.1.message_ref.refs_4_, ...), custom_call_target="tpu_custom_call" | custom-call | tf_op jit(solution)/shard_map/pallas_call | solution.py:555
  41.1 1.4 %collective-permute-done.5 = f32[2,128,128]{2,1,0:T(8,128)S(1)} collective-permute-done((f32[2,128,128]{2,1,0:T(8,128)S(1)}, f32[2,128,128]{2,1,0:T(8,128)S(1)}, u32[]{:S(2)}, u32[]{:S(2)}) %collective-permute-start.5) | collective-permute-done | bytes 131104 | tf_op jit(solution)/shard_map/ppermute | solution.py:475
  42.5 0.7 %add.5 = f32[2,128,128]{2,1,0:T(8,128)} add(f32[2,128,128]{2,1,0:T(8,128)S(1)} %shard_map.50, f32[2,128,128]{2,1,0:T(8,128)S(1)} %collective-permute-done.5) | non-fusion elementwise | flops 32768 | bytes 393216 | tf_op jit(solution)/shard_map/add | solution.py:567
  (3 shorter events, 0.0 us)
Async XLA Ops:
  0.0 15.8 %copy-start = (f32[2,1,512,128]{3,2,1,0:T(8,128)S(1)}, f32[2,1,512,128]{3,2,1,0:T(8,128)}, u32[]{:S(2)}) copy-start(f32[2,1,512,128]{3,2,1,0:T(8,128)} %refs_2_.3) | copy-start | bytes 1572868
  0.0 15.8 %copy-start.1 = (f32[2,1,512,128]{3,2,1,0:T(8,128)S(1)}, f32[2,1,512,128]{3,2,1,0:T(8,128)}, u32[]{:S(2)}) copy-start(f32[2,1,512,128]{3,2,1,0:T(8,128)} %refs_3_.3) | copy-start | bytes 1572868
  2.2 24.7 %all-to-all-start = ((f32[64,1,1152]{2,1,0:T(1,128)}), f32[64,1,1152]{2,1,0:T(1,128)S(1)}, u32[]{:S(2)}, u32[]{:S(2)}) async-start(f32[64,1,1152]{2,1,0:T(1,128)} %bitcast.7), calls=%async_computation | async-start | bytes 589824 | tf_op jit(solution)/shard_map/all_to_all | solution.py:488
  16.4 14.2 %collective-permute-start.1 = (f32[8,144,128]{2,1,0:T(8,128)S(1)}, f32[8,144,128]{2,1,0:T(8,128)S(1)}, u32[]{:S(2)}, u32[]{:S(2)}) collective-permute-start(f32[8,144,128]{2,1,0:T(8,128)S(1)} %get-tuple-element.9), channel_id=1, source_target_pairs={{0,64},{64,0},{128,192},{192,128},{1,65},{65,1},{129,193},{193,129... | collective-permute-start | bytes 1769480 | tf_op jit(solution)/shard_map/ppermute | solution.py:475
  17.5 13.0 %collective-permute-start.2 = (f32[128,128]{1,0:T(8,128)S(1)}, f32[128,128]{1,0:T(8,128)S(1)}, u32[]{:S(2)}, u32[]{:S(2)}) collective-permute-start(f32[128,128]{1,0:T(8,128)S(1)} %get-tuple-element.10), channel_id=1, source_target_pairs={{0,1},{1,0},{2,3},{3,2},{4,5},{5,4},{6,7},{7,6},{8,9},{9,8},{10,11... | collective-permute-start | bytes 196616 | tf_op jit(solution)/shard_map/ppermute | solution.py:502
  18.8 11.7 %collective-permute-start.3 = (f32[128,128]{1,0:T(8,128)S(1)}, f32[128,128]{1,0:T(8,128)S(1)}, u32[]{:S(2)}, u32[]{:S(2)}) collective-permute-start(f32[128,128]{1,0:T(8,128)S(1)} %get-tuple-element.10), channel_id=1, source_target_pairs={{1,2},{2,1},{3,4},{4,3},{5,6},{6,5},{7,8},{8,7},{9,10},{10,9},{11,... | collective-permute-start | bytes 196616 | tf_op jit(solution)/shard_map/ppermute | solution.py:502
  26.9 4.9 %collective-permute-start = (f32[576,128]{1,0:T(8,128)S(1)}, f32[576,128]{1,0:T(8,128)S(1)}, u32[]{:S(2)}, u32[]{:S(2)}) collective-permute-start(f32[576,128]{1,0:T(8,128)S(1)} %bitcast.4), channel_id=1, source_target_pairs={{0,64},{64,0},{128,192},{192,128},{1,65},{65,1},{129,193},{193,129... | collective-permute-start | bytes 884744 | tf_op jit(solution)/shard_map/ppermute | solution.py:475
  30.5 1.3 %collective-permute-start.4 = (f32[136,128]{1,0:T(8,128)S(1)}, f32[136,128]{1,0:T(8,128)S(1)}, u32[]{:S(2)}, u32[]{:S(2)}) collective-permute-start(f32[136,128]{1,0:T(8,128)S(1)} %concatenate.3.refs_5_), channel_id=1, source_target_pairs={{0,64},{64,0},{128,192},{192,128},{1,65},{65,1},{129,193},{193,129... | collective-permute-start | bytes 208904 | tf_op jit(solution)/shard_map/ppermute | solution.py:475
  36.3 6.2 %collective-permute-start.5 = (f32[2,128,128]{2,1,0:T(8,128)S(1)}, f32[2,128,128]{2,1,0:T(8,128)S(1)}, u32[]{:S(2)}, u32[]{:S(2)}) collective-permute-start(f32[2,128,128]{2,1,0:T(8,128)S(1)} %get-tuple-element.12), channel_id=1, source_target_pairs={{0,128},{64,192},{128,0},{192,64},{1,129},{65,193},{129,1},{193,65... | collective-permute-start | bytes 393224 | tf_op jit(solution)/shard_map/ppermute | solution.py:475

commit v7 on v6

--- a/solution.py
+++ b/solution.py
@@ -16,11 +16,11 @@
 CORE_ROWS = 128
 ROWS = CORE_ROWS + 2 * TILE
 GUARD = TILE
-CHUNK = 72
+CHUNK = 48
 SPAN = 9
 GROUPS = 2
 
-phase_depth = 2.0
+half_depth = 1.0
 fd_coef = 0.03
 
 F32 = jnp.float32
@@ -121,7 +121,7 @@
 
 
 def sin_cos(x):
-    t = 0.5 * x - 0.7853981633974483
+    t = x - 0.7853981633974483
     square = t * t
     sine = t * horner(SIN_TERMS, square)
     cosine = horner(COS_TERMS, square)
@@ -358,9 +358,9 @@
             window_live = window_live | (live & ((((lane + 112) >> 6) & 1) == b))
         window = window + pltpu.roll(window, WIN, 2)
         here = tile_speeds(stage.at[sent], depth)
-        speed[0, depth] = (phase_depth / here).reshape(ROWS, LANES)
+        speed[0, depth] = (half_depth / here).reshape(ROWS, LANES)
         coef[0, depth] = jnp.where(sent_live, fd_coef * here, 0.0).reshape(ROWS, LANES)
-        speed[1, depth] = (phase_depth / window).reshape(ROWS, LANES)
+        speed[1, depth] = (half_depth / window).reshape(ROWS, LANES)
         coef[1, depth] = jnp.where(
             on_grid & window_live, fd_coef * window, 0.0
         ).reshape(ROWS, LANES)
@@ -438,7 +438,7 @@
     )
     for depth in range(2):
         here = tile_speeds(stage, depth)
-        speed[0, depth] = (phase_depth / here).reshape(ROWS, LANES)
+        speed[0, depth] = (half_depth / here).reshape(ROWS, LANES)
         coef[0, depth] = jnp.where(live, fd_coef * here, 0.0).reshape(ROWS, LANES)
 
     @pl.when(freq == 0)

time: 43.4 us -> 43.3 us (level)
  no operation moved by 1% of the time
where the time goes in v7:
time: 43.3 us; the launch traced here: 43.1 us
  starting transfers between devices  22.8 us (53%)
  Pallas kernels  10.6 us (24%)
  waiting for transfers between devices  8.34 us (19%)
  between operations  0.76 us (2%)
  other arithmetic  0.69 us (2%)
    all_to_all x1, starting transfers between devices, shards(): lax.all_to_all(packed.reshape(strips, 1, SPAN * LANES), 'strip', split_ax...  13.6 us
    ppermute x4, starting transfers between devices, across(): return lax.ppermute(x, 'freq', [(i, i ^ k) for i in range(freqs)])  7.23 us
    all_to_all x1, waiting for transfers between devices, shards(): lax.all_to_all(packed.reshape(strips, 1, SPAN * LANES), 'strip', split_ax...  6.84 us
    pallas_call x1, Pallas kernels, shards(): pl.pallas_call(march_sent, out_shape=[shape(2, CORE_ROWS, LANES)] * 2, in...  4.38 us
    pallas_call x1, Pallas kernels, shards(): pl.pallas_call(march_kept, out_shape=shape(2, CORE_ROWS, LANES), in_specs...  2.24 us
    pallas_call x1, Pallas kernels, shards(): pl.pallas_call(pack_speed, out_shape=shape(SPAN * strips, LANES), in_spec...  2.21 us
    ppermute x2, starting transfers between devices, swap(): lax.ppermute(x, 'strip', [p for i, j in pairs for p in ((i, j), (j, i))])  1.96 us
    ppermute x4, waiting for transfers between devices, across(): return lax.ppermute(x, 'freq', [(i, i ^ k) for i in range(freqs)])  1.5 us
  transfers between devices with their start and end apart: 7, of which 3 were waited for; matrix products, arithmetic and copies ran while one was open for 0% of the time, Pallas kernels for 9%

profile of v7, /device:TPU:1, one launch (start us, length us, event | category | flops | bytes accessed | tf_op | source)
XLA Modules:
  0.0 43.1 jit_solution(9176722405800494430)
XLA Ops:
  0.0 0.0 copy-start
  0.0 0.0 copy-start.1
  0.0 2.2 %shard_map.46 = f32[576,128]{1,0:T(8,128)} custom-call(f32[2,8,8192]{2,1,0:T(8,128)} %vel_ref.1), custom_call_target="tpu_custom_call" | custom-call | tf_op jit(solution)/shard_map/pallas_call | solution.py:477
  2.2 13.6 %all-to-all-start = ((f32[64,1,1152]{2,1,0:T(1,128)}), f32[64,1,1152]{2,1,0:T(1,128)S(1)}, u32[]{:S(2)}, u32[]{:S(2)}) async-start(f32[64,1,1152]{2,1,0:T(1,128)} %bitcast.7), calls=%async_computation | async-start | bytes 589824 | tf_op jit(solution)/shard_map/all_to_all | solution.py:488
  15.8 0.0 copy-done
  15.8 0.0 copy-done.1
  15.8 0.6 %shard_map.47 = (f32[128,128]{1,0:T(8,128)S(1)}, f32[8,144,128]{2,1,0:T(8,128)S(1)}) custom-call(f32[2,1,512,128]{3,2,1,0:T(8,128)S(1)} %copy-done, f32[2,1,512,128]{3,2,1,0:T(8,128)S(1)} %copy-done.1), custom_call_target="tpu_custom_call" | custom-call | tf_op jit(solution)/shard_map/pallas_call | solution.py:493
  16.4 1.0 %collective-permute-start.1 = (f32[8,144,128]{2,1,0:T(8,128)S(1)}, f32[8,144,128]{2,1,0:T(8,128)S(1)}, u32[]{:S(2)}, u32[]{:S(2)}) collective-permute-start(f32[8,144,128]{2,1,0:T(8,128)S(1)} %get-tuple-element.9), channel_id=1, source_target_pairs={{0,64},{64,0},{128,192},{192,128},{1,65},{65,1},{129,193},{193,129... | collective-permute-start | bytes 1769480 | tf_op jit(solution)/shard_map/ppermute | solution.py:475
  17.5 1.3 %collective-permute-start.2 = (f32[128,128]{1,0:T(8,128)S(1)}, f32[128,128]{1,0:T(8,128)S(1)}, u32[]{:S(2)}, u32[]{:S(2)}) collective-permute-start(f32[128,128]{1,0:T(8,128)S(1)} %get-tuple-element.10), channel_id=1, source_target_pairs={{0,1},{1,0},{2,3},{3,2},{4,5},{5,4},{6,7},{7,6},{8,9},{9,8},{10,11... | collective-permute-start | bytes 196616 | tf_op jit(solution)/shard_map/ppermute | solution.py:502
  18.8 0.7 %collective-permute-start.3 = (f32[128,128]{1,0:T(8,128)S(1)}, f32[128,128]{1,0:T(8,128)S(1)}, u32[]{:S(2)}, u32[]{:S(2)}) collective-permute-start(f32[128,128]{1,0:T(8,128)S(1)} %get-tuple-element.10), channel_id=1, source_target_pairs={{1,2},{2,1},{3,4},{4,3},{5,6},{6,5},{7,8},{8,7},{9,10},{10,9},{11,... | collective-permute-start | bytes 196616 | tf_op jit(solution)/shard_map/ppermute | solution.py:502
  20.1 6.8 %all-to-all-done = f32[64,1,1152]{2,1,0:T(1,128)S(1)} async-done(((f32[64,1,1152]{2,1,0:T(1,128)}), f32[64,1,1152]{2,1,0:T(1,128)S(1)}, u32[]{:S(2)}, u32[]{:S(2)}) %all-to-all-start) | async-done | bytes 294944 | tf_op jit(solution)/shard_map/all_to_all | solution.py:488
  26.9 3.6 %collective-permute-start = (f32[576,128]{1,0:T(8,128)S(1)}, f32[576,128]{1,0:T(8,128)S(1)}, u32[]{:S(2)}, u32[]{:S(2)}) collective-permute-start(f32[576,128]{1,0:T(8,128)S(1)} %bitcast.4), channel_id=1, source_target_pairs={{0,64},{64,0},{128,192},{192,128},{1,65},{65,1},{129,193},{193,129... | collective-permute-start | bytes 884744 | tf_op jit(solution)/shard_map/ppermute | solution.py:475
  30.5 0.0 collective-permute-done.2
  30.5 0.0 collective-permute-done.3
  30.5 0.1 collective-permute-start.4
  30.6 0.0 collective-permute-done.1.message_ref.refs_4_
  30.6 1.2 %shard_map.48.refs_7_ = f32[4,144,128]{2,1,0:T(8,128)S(1)} custom-call(f32[2,1,512,128]{3,2,1,0:T(8,128)S(1)} %copy-done, f32[2,1,512,128]{3,2,1,0:T(8,128)S(1)} %copy-done.1, f32[8,144,128]{2,1,0:T(8,128)S(1)} %collective-permute-done.1.message_ref.refs_4_), custom_call_target="tpu_custom_call" | custom-call | tf_op jit(solution)/shard_map/pallas_call | solution.py:516
  31.8 0.1 collective-permute-done.4.refs_6_
  31.9 0.0 collective-permute-done.refs_1_
  31.9 4.4 %shard_map.49 = (f32[2,128,128]{2,1,0:T(8,128)S(1)}, f32[2,128,128]{2,1,0:T(8,128)S(1)}) custom-call(f32[576,128]{1,0:T(8,128)S(1)} %bitcast.5, f32[576,128]{1,0:T(8,128)S(1)} %collective-permute-done.refs_1_, f32[2,1,512,128]{3,2,1,0:T(8,128)S(1)} %copy-done, f32[2,1,512,128]{3,2,1,0:T(8,128)S(1)} %copy-done.1, ...), custom_call_target="tpu_custom_call" | custom-call | tf_op jit(solution)/shard_map/pallas_call | solution.py:541
  36.3 2.5 %collective-permute-start.5 = (f32[2,128,128]{2,1,0:T(8,128)S(1)}, f32[2,128,128]{2,1,0:T(8,128)S(1)}, u32[]{:S(2)}, u32[]{:S(2)}) collective-permute-start(f32[2,128,128]{2,1,0:T(8,128)S(1)} %get-tuple-element.12), channel_id=1, source_target_pairs={{0,128},{64,192},{128,0},{192,64},{1,129},{65,193},{129,1},{193,65... | collective-permute-start | bytes 393224 | tf_op jit(solution)/shard_map/ppermute | solution.py:475
  38.8 2.2 %shard_map.50 = f32[2,128,128]{2,1,0:T(8,128)S(1)} custom-call(f32[576,128]{1,0:T(8,128)S(1)} %bitcast.6, f32[576,128]{1,0:T(8,128)S(1)} %collective-permute-done.refs_1_, f32[2,1,512,128]{3,2,1,0:T(8,128)S(1)} %copy-done, f32[2,1,512,128]{3,2,1,0:T(8,128)S(1)} %copy-done.1, f32[8,144,128]{2,1,0:T(8,128)S(1)} %collective-permute-done.1.message_ref.refs_4_, ...), custom_call_target="tpu_custom_call" | custom-call | tf_op jit(solution)/shard_map/pallas_call | solution.py:555
  41.0 1.4 %collective-permute-done.5 = f32[2,128,128]{2,1,0:T(8,128)S(1)} collective-permute-done((f32[2,128,128]{2,1,0:T(8,128)S(1)}, f32[2,128,128]{2,1,0:T(8,128)S(1)}, u32[]{:S(2)}, u32[]{:S(2)}) %collective-permute-start.5) | collective-permute-done | bytes 131104 | tf_op jit(solution)/shard_map/ppermute | solution.py:475
  42.5 0.7 %add.5 = f32[2,128,128]{2,1,0:T(8,128)} add(f32[2,128,128]{2,1,0:T(8,128)S(1)} %shard_map.50, f32[2,128,128]{2,1,0:T(8,128)S(1)} %collective-permute-done.5) | non-fusion elementwise | flops 32768 | bytes 393216 | tf_op jit(solution)/shard_map/add | solution.py:567
  (3 shorter events, 0.0 us)
Async XLA Ops:
  0.0 15.8 %copy-start = (f32[2,1,512,128]{3,2,1,0:T(8,128)S(1)}, f32[2,1,512,128]{3,2,1,0:T(8,128)}, u32[]{:S(2)}) copy-start(f32[2,1,512,128]{3,2,1,0:T(8,128)} %refs_2_.3) | copy-start | bytes 1572868
  0.0 15.8 %copy-start.1 = (f32[2,1,512,128]{3,2,1,0:T(8,128)S(1)}, f32[2,1,512,128]{3,2,1,0:T(8,128)}, u32[]{:S(2)}) copy-start(f32[2,1,512,128]{3,2,1,0:T(8,128)} %refs_3_.3) | copy-start | bytes 1572868
  2.2 24.7 %all-to-all-start = ((f32[64,1,1152]{2,1,0:T(1,128)}), f32[64,1,1152]{2,1,0:T(1,128)S(1)}, u32[]{:S(2)}, u32[]{:S(2)}) async-start(f32[64,1,1152]{2,1,0:T(1,128)} %bitcast.7), calls=%async_computation | async-start | bytes 589824 | tf_op jit(solution)/shard_map/all_to_all | solution.py:488
  16.4 14.2 %collective-permute-start.1 = (f32[8,144,128]{2,1,0:T(8,128)S(1)}, f32[8,144,128]{2,1,0:T(8,128)S(1)}, u32[]{:S(2)}, u32[]{:S(2)}) collective-permute-start(f32[8,144,128]{2,1,0:T(8,128)S(1)} %get-tuple-element.9), channel_id=1, source_target_pairs={{0,64},{64,0},{128,192},{192,128},{1,65},{65,1},{129,193},{193,129... | collective-permute-start | bytes 1769480 | tf_op jit(solution)/shard_map/ppermute | solution.py:475
  17.5 13.0 %collective-permute-start.2 = (f32[128,128]{1,0:T(8,128)S(1)}, f32[128,128]{1,0:T(8,128)S(1)}, u32[]{:S(2)}, u32[]{:S(2)}) collective-permute-start(f32[128,128]{1,0:T(8,128)S(1)} %get-tuple-element.10), channel_id=1, source_target_pairs={{0,1},{1,0},{2,3},{3,2},{4,5},{5,4},{6,7},{7,6},{8,9},{9,8},{10,11... | collective-permute-start | bytes 196616 | tf_op jit(solution)/shard_map/ppermute | solution.py:502
  18.8 11.7 %collective-permute-start.3 = (f32[128,128]{1,0:T(8,128)S(1)}, f32[128,128]{1,0:T(8,128)S(1)}, u32[]{:S(2)}, u32[]{:S(2)}) collective-permute-start(f32[128,128]{1,0:T(8,128)S(1)} %get-tuple-element.10), channel_id=1, source_target_pairs={{1,2},{2,1},{3,4},{4,3},{5,6},{6,5},{7,8},{8,7},{9,10},{10,9},{11,... | collective-permute-start | bytes 196616 | tf_op jit(solution)/shard_map/ppermute | solution.py:502
  26.9 4.9 %collective-permute-start = (f32[576,128]{1,0:T(8,128)S(1)}, f32[576,128]{1,0:T(8,128)S(1)}, u32[]{:S(2)}, u32[]{:S(2)}) collective-permute-start(f32[576,128]{1,0:T(8,128)S(1)} %bitcast.4), channel_id=1, source_target_pairs={{0,64},{64,0},{128,192},{192,128},{1,65},{65,1},{129,193},{193,129... | collective-permute-start | bytes 884744 | tf_op jit(solution)/shard_map/ppermute | solution.py:475
  30.5 1.3 %collective-permute-start.4 = (f32[136,128]{1,0:T(8,128)S(1)}, f32[136,128]{1,0:T(8,128)S(1)}, u32[]{:S(2)}, u32[]{:S(2)}) collective-permute-start(f32[136,128]{1,0:T(8,128)S(1)} %concatenate.3.refs_5_), channel_id=1, source_target_pairs={{0,64},{64,0},{128,192},{192,128},{1,65},{65,1},{129,193},{193,129... | collective-permute-start | bytes 208904 | tf_op jit(solution)/shard_map/ppermute | solution.py:475
  36.3 6.2 %collective-permute-start.5 = (f32[2,128,128]{2,1,0:T(8,128)S(1)}, f32[2,128,128]{2,1,0:T(8,128)S(1)}, u32[]{:S(2)}, u32[]{:S(2)}) collective-permute-start(f32[2,128,128]{2,1,0:T(8,128)S(1)} %get-tuple-element.12), channel_id=1, source_target_pairs={{0,128},{64,192},{128,0},{192,64},{1,129},{65,193},{129,1},{193,65... | collective-permute-start | bytes 393224 | tf_op jit(solution)/shard_map/ppermute | solution.py:475

commit v8 on v6

--- a/solution.py
+++ b/solution.py
@@ -18,7 +18,7 @@
 GUARD = TILE
 CHUNK = 72
 SPAN = 9
-GROUPS = 2
+GROUPS = 1
 
 phase_depth = 2.0
 fd_coef = 0.03

time: 43.4 us -> 43.3 us (level)
  no operation moved by 1% of the time
where the time goes in v8:
time: 43.3 us; the launch traced here: 43.1 us
  starting transfers between devices  22.8 us (53%)
  Pallas kernels  10.5 us (24%)
  waiting for transfers between devices  8.32 us (19%)
  between operations  0.76 us (2%)
  other arithmetic  0.69 us (2%)
    all_to_all x1, starting transfers between devices, shards(): lax.all_to_all(packed.reshape(strips, 1, SPAN * LANES), 'strip', split_ax...  13.6 us
    ppermute x4, starting transfers between devices, across(): return lax.ppermute(x, 'freq', [(i, i ^ k) for i in range(freqs)])  7.23 us
    all_to_all x1, waiting for transfers between devices, shards(): lax.all_to_all(packed.reshape(strips, 1, SPAN * LANES), 'strip', split_ax...  6.84 us
    pallas_call x1, Pallas kernels, shards(): pl.pallas_call(march_sent, out_shape=[shape(2, CORE_ROWS, LANES)] * 2, in...  4.44 us
    pallas_call x1, Pallas kernels, shards(): pl.pallas_call(march_kept, out_shape=shape(2, CORE_ROWS, LANES), in_specs...  2.26 us
    pallas_call x1, Pallas kernels, shards(): pl.pallas_call(pack_speed, out_shape=shape(SPAN * strips, LANES), in_spec...  2.11 us
    ppermute x2, starting transfers between devices, swap(): lax.ppermute(x, 'strip', [p for i, j in pairs for p in ((i, j), (j, i))])  1.96 us
    ppermute x4, waiting for transfers between devices, across(): return lax.ppermute(x, 'freq', [(i, i ^ k) for i in range(freqs)])  1.47 us
  transfers between devices with their start and end apart: 7, of which 3 were waited for; matrix products, arithmetic and copies ran while one was open for 0% of the time, Pallas kernels for 9%

profile of v8, /device:TPU:1, one launch (start us, length us, event | category | flops | bytes accessed | tf_op | source)
XLA Modules:
  0.0 43.1 jit_solution(16454708518839900738)
XLA Ops:
  0.0 0.0 copy-start
  0.0 0.0 copy-start.1
  0.0 2.1 %shard_map.46 = f32[576,128]{1,0:T(8,128)} custom-call(f32[2,8,8192]{2,1,0:T(8,128)} %vel_ref.1), custom_call_target="tpu_custom_call" | custom-call | tf_op jit(solution)/shard_map/pallas_call | solution.py:477
  2.1 13.6 %all-to-all-start = ((f32[64,1,1152]{2,1,0:T(1,128)}), f32[64,1,1152]{2,1,0:T(1,128)S(1)}, u32[]{:S(2)}, u32[]{:S(2)}) async-start(f32[64,1,1152]{2,1,0:T(1,128)} %bitcast.7), calls=%async_computation | async-start | bytes 589824 | tf_op jit(solution)/shard_map/all_to_all | solution.py:488
  15.7 0.0 copy-done
  15.7 0.0 copy-done.1
  15.7 0.6 %shard_map.47 = (f32[128,128]{1,0:T(8,128)S(1)}, f32[8,144,128]{2,1,0:T(8,128)S(1)}) custom-call(f32[2,1,512,128]{3,2,1,0:T(8,128)S(1)} %copy-done, f32[2,1,512,128]{3,2,1,0:T(8,128)S(1)} %copy-done.1), custom_call_target="tpu_custom_call" | custom-call | tf_op jit(solution)/shard_map/pallas_call | solution.py:493
  16.3 1.0 %collective-permute-start.1 = (f32[8,144,128]{2,1,0:T(8,128)S(1)}, f32[8,144,128]{2,1,0:T(8,128)S(1)}, u32[]{:S(2)}, u32[]{:S(2)}) collective-permute-start(f32[8,144,128]{2,1,0:T(8,128)S(1)} %get-tuple-element.9), channel_id=1, source_target_pairs={{0,64},{64,0},{128,192},{192,128},{1,65},{65,1},{129,193},{193,129... | collective-permute-start | bytes 1769480 | tf_op jit(solution)/shard_map/ppermute | solution.py:475
  17.4 1.3 %collective-permute-start.2 = (f32[128,128]{1,0:T(8,128)S(1)}, f32[128,128]{1,0:T(8,128)S(1)}, u32[]{:S(2)}, u32[]{:S(2)}) collective-permute-start(f32[128,128]{1,0:T(8,128)S(1)} %get-tuple-element.10), channel_id=1, source_target_pairs={{0,1},{1,0},{2,3},{3,2},{4,5},{5,4},{6,7},{7,6},{8,9},{9,8},{10,11... | collective-permute-start | bytes 196616 | tf_op jit(solution)/shard_map/ppermute | solution.py:502
  18.7 0.7 %collective-permute-start.3 = (f32[128,128]{1,0:T(8,128)S(1)}, f32[128,128]{1,0:T(8,128)S(1)}, u32[]{:S(2)}, u32[]{:S(2)}) collective-permute-start(f32[128,128]{1,0:T(8,128)S(1)} %get-tuple-element.10), channel_id=1, source_target_pairs={{1,2},{2,1},{3,4},{4,3},{5,6},{6,5},{7,8},{8,7},{9,10},{10,9},{11,... | collective-permute-start | bytes 196616 | tf_op jit(solution)/shard_map/ppermute | solution.py:502
  20.0 6.8 %all-to-all-done = f32[64,1,1152]{2,1,0:T(1,128)S(1)} async-done(((f32[64,1,1152]{2,1,0:T(1,128)}), f32[64,1,1152]{2,1,0:T(1,128)S(1)}, u32[]{:S(2)}, u32[]{:S(2)}) %all-to-all-start) | async-done | bytes 294944 | tf_op jit(solution)/shard_map/all_to_all | solution.py:488
  26.8 3.6 %collective-permute-start = (f32[576,128]{1,0:T(8,128)S(1)}, f32[576,128]{1,0:T(8,128)S(1)}, u32[]{:S(2)}, u32[]{:S(2)}) collective-permute-start(f32[576,128]{1,0:T(8,128)S(1)} %bitcast.4), channel_id=1, source_target_pairs={{0,64},{64,0},{128,192},{192,128},{1,65},{65,1},{129,193},{193,129... | collective-permute-start | bytes 884744 | tf_op jit(solution)/shard_map/ppermute | solution.py:475
  30.4 0.0 collective-permute-done.2
  30.4 0.0 collective-permute-done.3
  30.4 0.1 collective-permute-start.4
  30.5 0.0 collective-permute-done.1.message_ref.refs_4_
  30.5 1.2 %shard_map.48.refs_7_ = f32[4,144,128]{2,1,0:T(8,128)S(1)} custom-call(f32[2,1,512,128]{3,2,1,0:T(8,128)S(1)} %copy-done, f32[2,1,512,128]{3,2,1,0:T(8,128)S(1)} %copy-done.1, f32[8,144,128]{2,1,0:T(8,128)S(1)} %collective-permute-done.1.message_ref.refs_4_), custom_call_target="tpu_custom_call" | custom-call | tf_op jit(solution)/shard_map/pallas_call | solution.py:516
  31.7 0.1 collective-permute-done.4.refs_6_
  31.8 0.0 collective-permute-done.refs_1_
  31.8 4.4 %shard_map.49 = (f32[2,128,128]{2,1,0:T(8,128)S(1)}, f32[2,128,128]{2,1,0:T(8,128)S(1)}) custom-call(f32[576,128]{1,0:T(8,128)S(1)} %bitcast.5, f32[576,128]{1,0:T(8,128)S(1)} %collective-permute-done.refs_1_, f32[2,1,512,128]{3,2,1,0:T(8,128)S(1)} %copy-done, f32[2,1,512,128]{3,2,1,0:T(8,128)S(1)} %copy-done.1, ...), custom_call_target="tpu_custom_call" | custom-call | tf_op jit(solution)/shard_map/pallas_call | solution.py:541
  36.2 2.5 %collective-permute-start.5 = (f32[2,128,128]{2,1,0:T(8,128)S(1)}, f32[2,128,128]{2,1,0:T(8,128)S(1)}, u32[]{:S(2)}, u32[]{:S(2)}) collective-permute-start(f32[2,128,128]{2,1,0:T(8,128)S(1)} %get-tuple-element.12), channel_id=1, source_target_pairs={{0,128},{64,192},{128,0},{192,64},{1,129},{65,193},{129,1},{193,65... | collective-permute-start | bytes 393224 | tf_op jit(solution)/shard_map/ppermute | solution.py:475
  38.8 2.3 %shard_map.50 = f32[2,128,128]{2,1,0:T(8,128)S(1)} custom-call(f32[576,128]{1,0:T(8,128)S(1)} %bitcast.6, f32[576,128]{1,0:T(8,128)S(1)} %collective-permute-done.refs_1_, f32[2,1,512,128]{3,2,1,0:T(8,128)S(1)} %copy-done, f32[2,1,512,128]{3,2,1,0:T(8,128)S(1)} %copy-done.1, f32[8,144,128]{2,1,0:T(8,128)S(1)} %collective-permute-done.1.message_ref.refs_4_, ...), custom_call_target="tpu_custom_call" | custom-call | tf_op jit(solution)/shard_map/pallas_call | solution.py:555
  41.0 1.4 %collective-permute-done.5 = f32[2,128,128]{2,1,0:T(8,128)S(1)} collective-permute-done((f32[2,128,128]{2,1,0:T(8,128)S(1)}, f32[2,128,128]{2,1,0:T(8,128)S(1)}, u32[]{:S(2)}, u32[]{:S(2)}) %collective-permute-start.5) | collective-permute-done | bytes 131104 | tf_op jit(solution)/shard_map/ppermute | solution.py:475
  42.4 0.7 %add.5 = f32[2,128,128]{2,1,0:T(8,128)} add(f32[2,128,128]{2,1,0:T(8,128)S(1)} %shard_map.50, f32[2,128,128]{2,1,0:T(8,128)S(1)} %collective-permute-done.5) | non-fusion elementwise | flops 32768 | bytes 393216 | tf_op jit(solution)/shard_map/add | solution.py:567
  (3 shorter events, 0.0 us)
Async XLA Ops:
  0.0 15.7 %copy-start = (f32[2,1,512,128]{3,2,1,0:T(8,128)S(1)}, f32[2,1,512,128]{3,2,1,0:T(8,128)}, u32[]{:S(2)}) copy-start(f32[2,1,512,128]{3,2,1,0:T(8,128)} %refs_2_.3) | copy-start | bytes 1572868
  0.0 15.7 %copy-start.1 = (f32[2,1,512,128]{3,2,1,0:T(8,128)S(1)}, f32[2,1,512,128]{3,2,1,0:T(8,128)}, u32[]{:S(2)}) copy-start(f32[2,1,512,128]{3,2,1,0:T(8,128)} %refs_3_.3) | copy-start | bytes 1572868
  2.1 24.7 %all-to-all-start = ((f32[64,1,1152]{2,1,0:T(1,128)}), f32[64,1,1152]{2,1,0:T(1,128)S(1)}, u32[]{:S(2)}, u32[]{:S(2)}) async-start(f32[64,1,1152]{2,1,0:T(1,128)} %bitcast.7), calls=%async_computation | async-start | bytes 589824 | tf_op jit(solution)/shard_map/all_to_all | solution.py:488
  16.3 14.2 %collective-permute-start.1 = (f32[8,144,128]{2,1,0:T(8,128)S(1)}, f32[8,144,128]{2,1,0:T(8,128)S(1)}, u32[]{:S(2)}, u32[]{:S(2)}) collective-permute-start(f32[8,144,128]{2,1,0:T(8,128)S(1)} %get-tuple-element.9), channel_id=1, source_target_pairs={{0,64},{64,0},{128,192},{192,128},{1,65},{65,1},{129,193},{193,129... | collective-permute-start | bytes 1769480 | tf_op jit(solution)/shard_map/ppermute | solution.py:475
  17.4 13.0 %collective-permute-start.2 = (f32[128,128]{1,0:T(8,128)S(1)}, f32[128,128]{1,0:T(8,128)S(1)}, u32[]{:S(2)}, u32[]{:S(2)}) collective-permute-start(f32[128,128]{1,0:T(8,128)S(1)} %get-tuple-element.10), channel_id=1, source_target_pairs={{0,1},{1,0},{2,3},{3,2},{4,5},{5,4},{6,7},{7,6},{8,9},{9,8},{10,11... | collective-permute-start | bytes 196616 | tf_op jit(solution)/shard_map/ppermute | solution.py:502
  18.7 11.7 %collective-permute-start.3 = (f32[128,128]{1,0:T(8,128)S(1)}, f32[128,128]{1,0:T(8,128)S(1)}, u32[]{:S(2)}, u32[]{:S(2)}) collective-permute-start(f32[128,128]{1,0:T(8,128)S(1)} %get-tuple-element.10), channel_id=1, source_target_pairs={{1,2},{2,1},{3,4},{4,3},{5,6},{6,5},{7,8},{8,7},{9,10},{10,9},{11,... | collective-permute-start | bytes 196616 | tf_op jit(solution)/shard_map/ppermute | solution.py:502
  26.8 4.9 %collective-permute-start = (f32[576,128]{1,0:T(8,128)S(1)}, f32[576,128]{1,0:T(8,128)S(1)}, u32[]{:S(2)}, u32[]{:S(2)}) collective-permute-start(f32[576,128]{1,0:T(8,128)S(1)} %bitcast.4), channel_id=1, source_target_pairs={{0,64},{64,0},{128,192},{192,128},{1,65},{65,1},{129,193},{193,129... | collective-permute-start | bytes 884744 | tf_op jit(solution)/shard_map/ppermute | solution.py:475
  30.4 1.3 %collective-permute-start.4 = (f32[136,128]{1,0:T(8,128)S(1)}, f32[136,128]{1,0:T(8,128)S(1)}, u32[]{:S(2)}, u32[]{:S(2)}) collective-permute-start(f32[136,128]{1,0:T(8,128)S(1)} %concatenate.3.refs_5_), channel_id=1, source_target_pairs={{0,64},{64,0},{128,192},{192,128},{1,65},{65,1},{129,193},{193,129... | collective-permute-start | bytes 208904 | tf_op jit(solution)/shard_map/ppermute | solution.py:475
  36.2 6.2 %collective-permute-start.5 = (f32[2,128,128]{2,1,0:T(8,128)S(1)}, f32[2,128,128]{2,1,0:T(8,128)S(1)}, u32[]{:S(2)}, u32[]{:S(2)}) collective-permute-start(f32[2,128,128]{2,1,0:T(8,128)S(1)} %get-tuple-element.12), channel_id=1, source_target_pairs={{0,128},{64,192},{128,0},{192,64},{1,129},{65,193},{129,1},{193,65... | collective-permute-start | bytes 393224 | tf_op jit(solution)/shard_map/ppermute | solution.py:475
